TPU v7x, 32 devices: a whole 2x2x4 slice. The times are simulated.
32 devices in a mesh: expert: 32 (over z, y, x, core), tensor: 1.
Axes of the slice: x: 2, y: 2, z: 4, core: 2. Of those that a mesh axis runs over, the one named last changes fastest.
Arguments:
- tokens: bfloat16 [8192, 2048], P('expert', 'tensor'), may hold values from -6 to 6
- out_grads: bfloat16 [8192, 2048], P('expert', 'tensor'), may hold values from -6 to 6
- species: int32 [8192, 1], P('expert'), may hold values from 0 to 31; in each aligned block of 256 rows (0 to 255, 256 to 511, ...) at most 16 rows name the same one
- expert_table: int32 [32], replicated, may hold values from 0 to 31, each once
- gate_weight: bfloat16 [32, 2048, 4096], P('expert', None, 'tensor'), may hold values from -0.125 to 0.125
- up_weight: bfloat16 [32, 2048, 4096], P('expert', None, 'tensor'), may hold values from -0.125 to 0.125
- down_weight: bfloat16 [32, 4096, 2048], P('expert', 'tensor'), may hold values from -0.09375 to 0.09375
Outputs:
- token_grads: bfloat16 [8192, 2048], P('expert', 'tensor')
Inputs may be any that keep to these rules, and one draw needn't show every extreme that they name: In each aligned block of 256 rows no species occurs more than 16 times, and in some blocks one species occurs exactly 16 times. `expert_table`: each species has a different expert.
All inputs are finite; a program needn't handle non-finite values.
Results may differ from a plain program's by a relative error of at most 0.0095.
Values may be sent and summed in bfloat16 or wider, within the bound.
No kernel may reach another device: no remote copies, remote signals or barrier semaphores. Data moves between devices by JAX's collectives and lax.ppermute only.
A program may use at most 128 MiB of HBM per device.

v0:
```python
import jax
import jax.numpy as jnp
from jax import lax
from jax.sharding import PartitionSpec as P


def expert_partial(expert_rows, expert_grads, gate_matrix, up_matrix, down_matrix):
    contract = (((1,), (1,)), ((), ()))
    gate_pre = jnp.dot(expert_rows, gate_matrix, preferred_element_type=jnp.float32)
    up_pre = jnp.dot(expert_rows, up_matrix, preferred_element_type=jnp.float32)
    hidden_grad = lax.dot_general(
        expert_grads, down_matrix, contract, preferred_element_type=jnp.float32
    )
    sigmoid_gate = jax.nn.sigmoid(gate_pre)
    up_grad = (hidden_grad * gate_pre * sigmoid_gate).astype(jnp.bfloat16)
    gate_grad = (
        hidden_grad * up_pre * sigmoid_gate * (1.0 + gate_pre * (1.0 - sigmoid_gate))
    ).astype(jnp.bfloat16)
    partial_sum = lax.dot_general(
        gate_grad, gate_matrix, contract, preferred_element_type=jnp.float32
    )
    return partial_sum + lax.dot_general(
        up_grad, up_matrix, contract, preferred_element_type=jnp.float32
    )


def per_device(tokens, out_grads, species, expert_table, gate_weight, up_weight, down_weight):
    tensor_size = lax.axis_size("tensor")
    tensor_index = lax.axis_index("tensor")
    experts = expert_table.shape[0]
    group_tokens_count = tokens.shape[0]
    rows_dev = group_tokens_count // tensor_size
    head_width = tokens.shape[1]
    model_width = head_width * tensor_size
    capacity = 2 * rows_dev // experts
    expert_ids = jnp.arange(experts, dtype=jnp.int32)
    species_hits = species == expert_ids[None, :]
    expert_of = jnp.sum(jnp.where(species_hits, expert_table[None, :], 0), axis=1).reshape(
        tensor_size, rows_dev
    )
    onehot = (expert_of[:, :, None] == expert_ids[None, None, :]).astype(jnp.int32)
    earlier = jnp.cumsum(onehot, axis=1) - onehot
    slot_of = jnp.sum(earlier * onehot, axis=2)
    place_of = expert_of * capacity + slot_of
    slot_ids = jnp.arange(experts * capacity, dtype=jnp.int32)
    select = (slot_ids[None, :, None] == place_of[:, None, :]).astype(jnp.bfloat16)
    group_select = select.reshape(tensor_size, experts, capacity, rows_dev)
    own_select = lax.dynamic_index_in_dim(select, tensor_index, 0, keepdims=False)
    group_tokens, group_grads = (
        lax.all_gather(tokens, "tensor", axis=1, tiled=True),
        lax.all_gather(out_grads, "tensor", axis=1, tiled=True),
    )
    packed_rows = jnp.einsum(
        "tecr,trd->etcd",
        group_select,
        group_tokens.reshape(tensor_size, rows_dev, model_width),
        preferred_element_type=jnp.float32,
    ).astype(jnp.bfloat16)
    packed_grads = jnp.einsum(
        "tecr,trd->etcd",
        group_select,
        group_grads.reshape(tensor_size, rows_dev, model_width),
        preferred_element_type=jnp.float32,
    ).astype(jnp.bfloat16)
    packed_rows = packed_rows.reshape(experts, tensor_size * capacity, model_width)
    packed_grads = packed_grads.reshape(experts, tensor_size * capacity, model_width)
    expert_rows, expert_grads = (
        lax.all_to_all(packed_rows, "expert", split_axis=0, concat_axis=0, tiled=True),
        lax.all_to_all(packed_grads, "expert", split_axis=0, concat_axis=0, tiled=True),
    )
    slot_count = expert_rows.shape[0] * expert_rows.shape[1]
    partial_sum = expert_partial(
        expert_rows.reshape(slot_count, model_width),
        expert_grads.reshape(slot_count, model_width),
        gate_weight[0],
        up_weight[0],
        down_weight[0],
    )
    summed = lax.psum_scatter(
        partial_sum.reshape(experts, tensor_size * capacity, model_width).astype(jnp.bfloat16),
        "tensor",
        scatter_dimension=1,
        tiled=True,
    )
    returned = lax.all_to_all(summed, "expert", split_axis=0, concat_axis=0, tiled=True)
    own_grads = lax.dot_general(
        own_select,
        returned.reshape(experts * capacity, model_width),
        (((0,), (0,)), ((), ())),
        preferred_element_type=jnp.float32,
    ).astype(jnp.bfloat16)
    token_grads = lax.all_to_all(own_grads, "tensor", split_axis=1, concat_axis=0, tiled=True)
    return token_grads


def solution(mesh):
    placed = (
        P("expert", "tensor"),
        P("expert", "tensor"),
        P("expert", None),
        P(),
        P("expert", None, "tensor"),
        P("expert", None, "tensor"),
        P("expert", "tensor", None),
    )
    return jax.shard_map(
        per_device, mesh=mesh, in_specs=placed, out_specs=P("expert", "tensor"), check_vma=False
    )
```

profile of v0, /device:TPU:0, one launch (start us, length us, event | category | flops | bytes accessed | tf_op | source)
XLA Modules:
  0.0 227.9 jit_solution(9945226470370597248)
XLA Ops:
  0.0 0.0 copy-start
  0.0 0.0 copy-start.2
  0.0 0.9 select_reduce_fusion
  1.0 0.6 reduce-window.6
  1.6 0.2 slice_reduce_fusion
  1.9 0.1 copy.13
  1.9 0.1 broadcast.118
  2.0 0.1 fusion.29
  2.1 0.0 copy-done
  2.1 2.1 convolution_convert_fusion.1
  4.3 7.3 %all-to-all-start = ((bf16[32,16,2048]{2,1,0:T(8,128)(2,1)}), bf16[32,16,2048]{2,1,0:T(8,128)(2,1)S(1)}, u32[]{:S(2)}, u32[]{:S(2)}) async-start(bf16[32,16,2048]{2,1,0:T(8,128)(2,1)} %convolution_convert_fusion.1), calls=%async_computation | async-start | bytes 4194304 | tf_op jit(solution)/shard_map/all_to_all | solution.py:69
  11.6 0.0 copy-done.2
  11.6 2.2 convolution_convert_fusion
  13.7 46.7 %all-to-all-done = bf16[32,16,2048]{2,1,0:T(8,128)(2,1)S(1)} async-done(((bf16[32,16,2048]{2,1,0:T(8,128)(2,1)}), bf16[32,16,2048]{2,1,0:T(8,128)(2,1)S(1)}, u32[]{:S(2)}, u32[]{:S(2)}) %all-to-all-start) | async-done | bytes 2097184 | tf_op jit(solution)/shard_map/all_to_all | solution.py:69
  60.5 4.1 %all-to-all-start.1 = ((bf16[32,16,2048]{2,1,0:T(8,128)(2,1)}), bf16[32,16,2048]{2,1,0:T(8,128)(2,1)}, u32[]{:S(2)}, u32[]{:S(2)}) async-start(bf16[32,16,2048]{2,1,0:T(8,128)(2,1)} %convolution_convert_fusion), calls=%async_computation.1 | async-start | bytes 4194304 | tf_op jit(solution)/shard_map/all_to_all | solution.py:68
  64.6 14.5 %fusion.8 = f32[512,4096]{1,0:T(8,128)} fusion(bf16[512,2048]{1,0:T(8,128)(2,1)S(1)} %bitcast.52, bf16[1,4096,2048]{2,1,0:T(8,128)(2,1)} %param.13), kind=kOutput, calls=%fused_computation.8 | convolution fusion | flops 8589934592 | bytes 27262976 | tf_op jit(solution)/shard_map/dot_general | solution.py:11
  79.1 34.4 %all-to-all-done.1 = bf16[32,16,2048]{2,1,0:T(8,128)(2,1)} async-done(((bf16[32,16,2048]{2,1,0:T(8,128)(2,1)}), bf16[32,16,2048]{2,1,0:T(8,128)(2,1)}, u32[]{:S(2)}, u32[]{:S(2)}) %all-to-all-start.1) | async-done | bytes 2097184 | tf_op jit(solution)/shard_map/all_to_all | solution.py:68
  113.5 14.9 %fusion.2 = f32[512,4096]{1,0:T(8,128)} fusion(bf16[512,2048]{1,0:T(8,128)(2,1)} %bitcast.12, bf16[1,2048,4096]{2,1,0:T(8,128)(2,1)} %param.11), kind=kOutput, calls=%fused_computation.2 | convolution fusion | flops 8589934592 | bytes 27262976 | tf_op jit(solution)/shard_map/dot_general | solution.py:9
  128.4 27.1 %fusion = f32[512,2048]{1,0:T(8,128)} fusion(bf16[1,2048,4096]{2,1,0:T(8,128)(2,1)} %param.11, f32[512,4096]{1,0:T(8,128)} %fusion.2, f32[512,4096]{1,0:T(8,128)} %fusion.8, bf16[512,2048]{1,0:T(8,128)(2,1)} %bitcast.12, bf16[1,2048,4096]{2,1,0:T(8,128)(2,1)} %param.12), kind=kOutput, calls=%fused_computation | convolution fusion | flops 17200840704 | bytes 56623104 | tf_op jit(solution)/shard_map/dot_general | solution.py:19
  155.5 0.0 copy-start.1
  155.5 18.1 %add_convert_fusion = bf16[512,2048]{1,0:T(8,128)(2,1)S(1)} fusion(f32[512,2048]{1,0:T(8,128)} %fusion, bf16[1,2048,4096]{2,1,0:T(8,128)(2,1)} %param.12, f32[512,4096]{1,0:T(8,128)} %fusion.8, f32[512,4096]{1,0:T(8,128)} %fusion.2), kind=kOutput, calls=%fused_computation.13 | convolution fusion | flops 8604614656 | bytes 39845888 | tf_op jit(solution)/shard_map/dot_general | solution.py:22
  173.7 52.5 %all_to_all.15 = bf16[32,16,2048]{2,1,0:T(8,128)(2,1)S(1)} all-to-all(bf16[32,16,2048]{2,1,0:T(8,128)(2,1)S(1)} %bitcast.53), channel_id=1, replica_groups=mesh['expert'=32,'tensor'=1] {'expert'}, dimensions={0} | all-to-all | bytes 4194304 | tf_op jit(solution)/shard_map/all_to_all | solution.py:85
  226.2 1.7 convolution_convert_fusion.2
  227.9 0.0 copy-done.1
  (7 shorter events, 0.1 us)
Async XLA Ops:
  0.0 2.1 copy-start
  0.0 11.6 %copy-start.2 = (bf16[256,2048]{1,0:T(8,128)(2,1)S(1)}, bf16[256,2048]{1,0:T(8,128)(2,1)}, u32[]{:S(2)}) copy-start(bf16[256,2048]{1,0:T(8,128)(2,1)} %param.7) | copy-start | bytes 3145732
  4.3 56.2 %all-to-all-start = ((bf16[32,16,2048]{2,1,0:T(8,128)(2,1)}), bf16[32,16,2048]{2,1,0:T(8,128)(2,1)S(1)}, u32[]{:S(2)}, u32[]{:S(2)}) async-start(bf16[32,16,2048]{2,1,0:T(8,128)(2,1)} %convolution_convert_fusion.1), calls=%async_computation | async-start | bytes 4194304 | tf_op jit(solution)/shard_map/all_to_all | solution.py:69
  60.5 53.0 %all-to-all-start.1 = ((bf16[32,16,2048]{2,1,0:T(8,128)(2,1)}), bf16[32,16,2048]{2,1,0:T(8,128)(2,1)}, u32[]{:S(2)}, u32[]{:S(2)}) async-start(bf16[32,16,2048]{2,1,0:T(8,128)(2,1)} %convolution_convert_fusion), calls=%async_computation.1 | async-start | bytes 4194304 | tf_op jit(solution)/shard_map/all_to_all | solution.py:68
  155.5 72.4 %copy-start.1 = (bf16[256,2048]{1,0:T(8,128)(2,1)S(1)}, bf16[256,2048]{1,0:T(8,128)(2,1)}, u32[]{:S(2)}) copy-start(bf16[256,2048]{1,0:T(8,128)(2,1)} %param.8) | copy-start | bytes 3145732
where the time goes:
time: 228 us
  waiting for transfers between devices  81.1 us (36%)
  matrix products  80.7 us (35%)
  blocking collectives  52.5 us (23%)
  starting transfers between devices  11.4 us (5%)
    all_to_all x1, blocking collectives, per_device(): lax.all_to_all(summed, 'expert', split_axis=0, concat_axis=0, tiled=True)  52.5 us
    all_to_all x1, waiting for transfers between devices, per_device(): lax.all_to_all(packed_grads, 'expert', split_axis=0, concat_axis=0, tiled...  46.7 us
    all_to_all x1, waiting for transfers between devices, per_device(): lax.all_to_all(packed_rows, 'expert', split_axis=0, concat_axis=0, tiled=...  34.4 us
    dot_general x1, matrix products, expert_partial(): lax.dot_general(gate_grad, gate_matrix, contract, preferred_element_type=...  27.1 us
    dot_general x1, matrix products, expert_partial(): lax.dot_general(up_grad, up_matrix, contract, preferred_element_type=jnp....  18.1 us
    dot_general x1, matrix products, expert_partial(): jnp.dot(expert_rows, gate_matrix, preferred_element_type=jnp.float32)  14.9 us
    dot_general x1, matrix products, expert_partial(): lax.dot_general(expert_grads, down_matrix, contract, preferred_element_ty...  14.5 us
    all_to_all x1, starting transfers between devices, per_device(): lax.all_to_all(packed_grads, 'expert', split_axis=0, concat_axis=0, tiled...  7.3 us
  transfers between devices with their start and end apart: 2, of which 2 were waited for; matrix products, arithmetic and copies ran while one was open for 7% of the time, Pallas kernels for 0%

commit v1 on v0

v1 whole, which is shorter than its diff:
```python
import jax
import jax.numpy as jnp
from jax import lax
from jax.sharding import PartitionSpec as P

PIECES = 2


def dot(a, b, contract):
    return lax.dot_general(a, b, (contract, ((), ())), preferred_element_type=jnp.float32)


def expert_partial(gate_pre, up_pre, hidden_grad, gate_matrix, up_matrix):
    sigmoid_gate = jax.nn.sigmoid(gate_pre)
    up_grad = (hidden_grad * gate_pre * sigmoid_gate).astype(jnp.bfloat16)
    gate_grad = (
        hidden_grad * up_pre * sigmoid_gate * (1.0 + gate_pre * (1.0 - sigmoid_gate))
    ).astype(jnp.bfloat16)
    return dot(gate_grad, gate_matrix, ((1,), (1,))) + dot(up_grad, up_matrix, ((1,), (1,)))


def places(species, expert_table, tensor_size, capacity):
    experts = expert_table.shape[0]
    rows_dev = species.shape[0] // tensor_size
    expert_ids = jnp.arange(experts, dtype=jnp.int32)
    species_hits = species == expert_ids[None, :]
    expert_of = jnp.sum(jnp.where(species_hits, expert_table[None, :], 0), axis=1).reshape(
        tensor_size, rows_dev
    )
    onehot = (expert_of[:, :, None] == expert_ids[None, None, :]).astype(jnp.int32)
    earlier = jnp.cumsum(onehot, axis=1) - onehot
    slot_of = jnp.sum(earlier * onehot, axis=2)
    return expert_of, slot_of


def per_device(tokens, out_grads, species, expert_table, gate_weight, up_weight, down_weight):
    tensor_size = lax.axis_size("tensor")
    tensor_index = lax.axis_index("tensor")
    experts = expert_table.shape[0]
    rows_dev = tokens.shape[0] // tensor_size
    model_width = tokens.shape[1] * tensor_size
    capacity = 2 * rows_dev // experts
    pieces = PIECES if capacity % (8 * PIECES) == 0 else 1
    depth = capacity // pieces
    expert_of, slot_of = places(species, expert_table, tensor_size, capacity)
    gate, up, down = gate_weight[0], up_weight[0], down_weight[0]
    group_tokens, group_grads = (
        lax.all_gather(tokens, "tensor", axis=1, tiled=True),
        lax.all_gather(out_grads, "tensor", axis=1, tiled=True),
    )
    place_ids = jnp.arange(experts * depth, dtype=jnp.int32)

    def select_of(piece):
        slot = slot_of - piece * depth
        place = jnp.where((slot >= 0) & (slot < depth), expert_of * depth + slot, -1)
        return (place_ids[None, :, None] == place[:, None, :]).astype(jnp.bfloat16)

    def send(select, rows):
        packed = jnp.einsum(
            "tecr,trd->etcd",
            select.reshape(tensor_size, experts, depth, rows_dev),
            rows.reshape(tensor_size, rows_dev, model_width),
            preferred_element_type=jnp.float32,
        ).astype(jnp.bfloat16)
        packed = packed.reshape(experts, tensor_size * depth, model_width)
        return lax.all_to_all(packed, "expert", split_axis=0, concat_axis=0, tiled=True)

    selects = [select_of(k) for k in range(pieces)]
    arrived = [(send(s, group_tokens), send(s, group_grads)) for s in selects]
    own = None
    for select, (rows, grads) in zip(selects, arrived):
        slot_count = rows.shape[0] * rows.shape[1]
        rows = rows.reshape(slot_count, model_width)
        grads = grads.reshape(slot_count, model_width)
        gate_pre = dot(rows, gate, ((1,), (0,)))
        up_pre = dot(rows, up, ((1,), (0,)))
        hidden_grad = dot(grads, down, ((1,), (1,)))
        partial_sum = expert_partial(gate_pre, up_pre, hidden_grad, gate, up)
        summed = lax.psum_scatter(
            partial_sum.reshape(experts, tensor_size * depth, model_width).astype(jnp.bfloat16),
            "tensor",
            scatter_dimension=1,
            tiled=True,
        )
        returned = lax.all_to_all(summed, "expert", split_axis=0, concat_axis=0, tiled=True)
        own_select = lax.dynamic_index_in_dim(select, tensor_index, 0, keepdims=False)
        term = dot(own_select, returned.reshape(experts * depth, model_width), ((0,), (0,)))
        own = term if own is None else own + term
    return lax.all_to_all(
        own.astype(jnp.bfloat16), "tensor", split_axis=1, concat_axis=0, tiled=True
    )


def solution(mesh):
    placed = (
        P("expert", "tensor"),
        P("expert", "tensor"),
        P("expert", None),
        P(),
        P("expert", None, "tensor"),
        P("expert", None, "tensor"),
        P("expert", "tensor", None),
    )
    return jax.shard_map(
        per_device, mesh=mesh, in_specs=placed, out_specs=P("expert", "tensor"), check_vma=False
    )
```

time: 228 us -> 226 us (level)
  blocking collectives: 52.5 us -> 0 us
  matrix products: 80.7 us -> 125 us
  starting transfers between devices: 11.4 us -> 30.4 us
  waiting for transfers between devices: 81.1 us -> 67.4 us
    all_to_all x1 -> x0, blocking collectives: 52.5 us -> none  [per_device(): lax.all_to_all(summed, 'expert', split_axis=0, concat_axis=0, tiled=True)]
    dot_general x7 -> x16, matrix products: 80.7 us -> 125 us  [the longest x12 119 us: dot(): lax.dot_general(a, b, (contract, ((), ())), preferred_element_type=jnp.fl...]
    all_to_all x2 -> x6, starting transfers between devices: 11.4 us -> 30.4 us  [the longest x4 20.7 us: send(): lax.all_to_all(packed, 'expert', split_axis=0, concat_axis=0, tiled=True)]
    all_to_all x2 -> x6, waiting for transfers between devices: 81.1 us -> 67.4 us  [the longest x4 43 us: send(): lax.all_to_all(packed, 'expert', split_axis=0, concat_axis=0, tiled=True)]
  transfers between devices with their start and end apart: 2 -> 6, of which waited for: 2 -> 4; matrix products, arithmetic and copies ran while one was open for 7% -> 54% of each run, Pallas kernels for 0% -> 0%
where the time goes in v1:
time: 226 us; the launch traced here: 225 us
  matrix products  125 us (55%)
  waiting for transfers between devices  67.4 us (30%)
  starting transfers between devices  30.4 us (13%)
    dot_general x12, matrix products, dot(): lax.dot_general(a, b, (contract, ((), ())), preferred_element_type=jnp.fl...  119 us
    all_to_all x4, waiting for transfers between devices, send(): lax.all_to_all(packed, 'expert', split_axis=0, concat_axis=0, tiled=True)  43 us
    all_to_all x2, waiting for transfers between devices, per_device(): lax.all_to_all(summed, 'expert', split_axis=0, concat_axis=0, tiled=True)  24.4 us
    all_to_all x4, starting transfers between devices, send(): lax.all_to_all(packed, 'expert', split_axis=0, concat_axis=0, tiled=True)  20.7 us
    all_to_all x2, starting transfers between devices, per_device(): lax.all_to_all(summed, 'expert', split_axis=0, concat_axis=0, tiled=True)  9.64 us
    dot_general x4, matrix products, send(): jnp.einsum('tecr,trd->etcd', select.reshape(tensor_size, experts, depth,...  5.87 us
  transfers between devices with their start and end apart: 6, of which 4 were waited for; matrix products, arithmetic and copies ran while one was open for 54% of the time, Pallas kernels for 0%

profile of v1, /device:TPU:0, one launch (start us, length us, event | category | flops | bytes accessed | tf_op | source)
XLA Modules:
  0.0 225.2 jit_solution(18113290218745963134)
XLA Ops:
  0.0 0.0 copy-start
  0.0 0.0 copy-start.2
  0.0 0.9 select_reduce_fusion
  1.0 0.6 reduce-window.6
  1.6 0.2 slice_reduce_fusion
  1.9 0.1 copy.13
  1.9 0.1 broadcast.232
  2.0 0.1 fusion.96
  2.1 0.0 copy-done
  2.1 1.4 convolution_convert_fusion.2
  3.6 7.3 %all-to-all-start.1 = ((bf16[32,8,2048]{2,1,0:T(8,128)(2,1)}), bf16[32,8,2048]{2,1,0:T(8,128)(2,1)S(1)}, u32[]{:S(2)}, u32[]{:S(2)}) async-start(bf16[32,8,2048]{2,1,0:T(8,128)(2,1)} %convolution_convert_fusion.2), calls=%async_computation.1 | async-start | bytes 2097152 | tf_op jit(solution)/shard_map/all_to_all | solution.py:66
  10.9 0.0 copy-done.2
  10.9 1.5 convolution_convert_fusion.3
  12.4 24.8 %all-to-all-done.1 = bf16[32,8,2048]{2,1,0:T(8,128)(2,1)S(1)} async-done(((bf16[32,8,2048]{2,1,0:T(8,128)(2,1)}), bf16[32,8,2048]{2,1,0:T(8,128)(2,1)S(1)}, u32[]{:S(2)}, u32[]{:S(2)}) %all-to-all-start.1) | async-done | bytes 1048608 | tf_op jit(solution)/shard_map/all_to_all | solution.py:66
  37.1 3.7 %all-to-all-start = ((bf16[32,8,2048]{2,1,0:T(8,128)(2,1)}), bf16[32,8,2048]{2,1,0:T(8,128)(2,1)}, u32[]{:S(2)}, u32[]{:S(2)}) async-start(bf16[32,8,2048]{2,1,0:T(8,128)(2,1)} %convolution_convert_fusion.3), calls=%async_computation | async-start | bytes 2097152 | tf_op jit(solution)/shard_map/all_to_all | solution.py:66
  40.9 1.5 convolution_convert_fusion
  42.4 1.5 convolution_convert_fusion.1
  43.9 10.1 %fusion.6 = f32[256,4096]{1,0:T(8,128)} fusion(bf16[1,2048,4096]{2,1,0:T(8,128)(2,1)} %param.11, bf16[32,8,2048]{2,1,0:T(8,128)(2,1)S(1)} %all-to-all-done.1), kind=kOutput, calls=%fused_computation.6 | convolution fusion | flops 4294967296 | bytes 22020096 | tf_op jit(solution)/shard_map/dot_general | solution.py:10
  54.0 13.1 %all-to-all-done = bf16[32,8,2048]{2,1,0:T(8,128)(2,1)} async-done(((bf16[32,8,2048]{2,1,0:T(8,128)(2,1)}), bf16[32,8,2048]{2,1,0:T(8,128)(2,1)}, u32[]{:S(2)}, u32[]{:S(2)}) %all-to-all-start) | async-done | bytes 1048608 | tf_op jit(solution)/shard_map/all_to_all | solution.py:66
  67.1 3.8 %all-to-all-start.4 = ((bf16[32,8,2048]{2,1,0:T(8,128)(2,1)}), bf16[32,8,2048]{2,1,0:T(8,128)(2,1)S(1)}, u32[]{:S(2)}, u32[]{:S(2)}) async-start(bf16[32,8,2048]{2,1,0:T(8,128)(2,1)} %convolution_convert_fusion), calls=%async_computation.4 | async-start | bytes 2097152 | tf_op jit(solution)/shard_map/all_to_all | solution.py:66
  70.9 12.6 %fusion.18 = f32[256,4096]{1,0:T(8,128)} fusion(bf16[1,4096,2048]{2,1,0:T(8,128)(2,1)} %param.13, bf16[32,8,2048]{2,1,0:T(8,128)(2,1)} %all-to-all-done), kind=kOutput, calls=%fused_computation.18 | convolution fusion | flops 4294967296 | bytes 22020096 | tf_op jit(solution)/shard_map/dot_general | solution.py:10
  83.5 14.3 %fusion.41 = bf16[256,4096]{1,0:T(8,128)(2,1)} fusion(f32[256,4096]{1,0:T(8,128)} %fusion.18, bf16[1,2048,4096]{2,1,0:T(8,128)(2,1)} %param.12, f32[256,4096]{1,0:T(8,128)} %fusion.6, bf16[32,8,2048]{2,1,0:T(8,128)(2,1)S(1)} %all-to-all-done.1), kind=kOutput, calls=%fused_computation.27 | convolution fusion | flops 4305453056 | bytes 28311552 | tf_op jit(solution)/shard_map/dot_general | solution.py:10
  97.9 12.3 %fusion.4 = f32[256,2048]{1,0:T(8,128)} fusion(bf16[256,4096]{1,0:T(8,128)(2,1)} %fusion.41, bf16[1,2048,4096]{2,1,0:T(8,128)(2,1)} %param.11), kind=kOutput, calls=%fused_computation.4 | convolution fusion | flops 4294967296 | bytes 20971520 | tf_op jit(solution)/shard_map/dot_general | solution.py:10
  110.1 0.0 all-to-all-done.4
  110.1 5.9 %all-to-all-start.3 = ((bf16[32,8,2048]{2,1,0:T(8,128)(2,1)}), bf16[32,8,2048]{2,1,0:T(8,128)(2,1)S(1)}, u32[]{:S(2)}, u32[]{:S(2)}) async-start(bf16[32,8,2048]{2,1,0:T(8,128)(2,1)} %convolution_convert_fusion.1), calls=%async_computation.3 | async-start | bytes 2097152 | tf_op jit(solution)/shard_map/all_to_all | solution.py:66
  116.0 0.0 copy-start.3
  116.0 10.2 %fusion.2 = f32[256,4096]{1,0:T(8,128)} fusion(bf16[1,2048,4096]{2,1,0:T(8,128)(2,1)} %param.11, bf16[32,8,2048]{2,1,0:T(8,128)(2,1)S(1)} %all-to-all-done.4), kind=kOutput, calls=%fused_computation.2 | convolution fusion | flops 4294967296 | bytes 22020096 | tf_op jit(solution)/shard_map/dot_general | solution.py:10
  126.3 0.0 copy-done.3
  126.3 10.7 %fusion.57 = bf16[32,8,2048]{2,1,0:T(8,128)(2,1)} fusion(f32[256,2048]{1,0:T(8,128)} %fusion.4, bf16[1,2048,4096]{2,1,0:T(8,128)(2,1)} %param.12, f32[256,4096]{1,0:T(8,128)} %fusion.18, f32[256,4096]{1,0:T(8,128)S(1)} %copy-done.3), kind=kOutput, calls=%fused_computation.42 | convolution fusion | flops 4302307328 | bytes 28311552 | tf_op jit(solution)/shard_map/dot_general | solution.py:10
  136.9 5.1 %all-to-all-done.3 = bf16[32,8,2048]{2,1,0:T(8,128)(2,1)S(1)} async-done(((bf16[32,8,2048]{2,1,0:T(8,128)(2,1)}), bf16[32,8,2048]{2,1,0:T(8,128)(2,1)S(1)}, u32[]{:S(2)}, u32[]{:S(2)}) %all-to-all-start.3) | async-done | bytes 1048608 | tf_op jit(solution)/shard_map/all_to_all | solution.py:66
  142.0 3.7 %all-to-all-start.2 = ((bf16[32,8,2048]{2,1,0:T(8,128)(2,1)}), bf16[32,8,2048]{2,1,0:T(8,128)(2,1)}, u32[]{:S(2)}, u32[]{:S(2)}) async-start(bf16[32,8,2048]{2,1,0:T(8,128)(2,1)} %fusion.57), calls=%async_computation.2 | async-start | bytes 2097152 | tf_op jit(solution)/shard_map/all_to_all | solution.py:85
  145.8 10.1 %fusion.16 = f32[256,4096]{1,0:T(8,128)} fusion(bf16[1,4096,2048]{2,1,0:T(8,128)(2,1)} %param.13, bf16[32,8,2048]{2,1,0:T(8,128)(2,1)S(1)} %all-to-all-done.3), kind=kOutput, calls=%fused_computation.16 | convolution fusion | flops 4294967296 | bytes 22020096 | tf_op jit(solution)/shard_map/dot_general | solution.py:10
  155.9 14.3 %fusion.38 = bf16[256,4096]{1,0:T(8,128)(2,1)} fusion(f32[256,4096]{1,0:T(8,128)} %fusion.16, bf16[1,2048,4096]{2,1,0:T(8,128)(2,1)} %param.12, f32[256,4096]{1,0:T(8,128)} %fusion.2, bf16[32,8,2048]{2,1,0:T(8,128)(2,1)S(1)} %all-to-all-done.4), kind=kOutput, calls=%fused_computation.26 | convolution fusion | flops 4305453056 | bytes 28311552 | tf_op jit(solution)/shard_map/dot_general | solution.py:10
  170.2 8.7 %fusion = f32[256,2048]{1,0:T(8,128)S(1)} fusion(bf16[256,4096]{1,0:T(8,128)(2,1)} %fusion.38, bf16[1,2048,4096]{2,1,0:T(8,128)(2,1)} %param.11), kind=kOutput, calls=%fused_computation | convolution fusion | flops 4294967296 | bytes 20971520 | tf_op jit(solution)/shard_map/dot_general | solution.py:10
  178.9 11.4 %fusion.60 = bf16[32,8,2048]{2,1,0:T(8,128)(2,1)} fusion(f32[256,2048]{1,0:T(8,128)S(1)} %fusion, bf16[1,2048,4096]{2,1,0:T(8,128)(2,1)} %param.12, f32[256,4096]{1,0:T(8,128)} %fusion.16, f32[256,4096]{1,0:T(8,128)} %fusion.2), kind=kOutput, calls=%fused_computation.43 | convolution fusion | flops 4302307328 | bytes 28311552 | tf_op jit(solution)/shard_map/dot_general | solution.py:10
  190.3 0.0 all-to-all-done.2
  190.3 5.9 %all-to-all-start.5 = ((bf16[32,8,2048]{2,1,0:T(8,128)(2,1)}), bf16[32,8,2048]{2,1,0:T(8,128)(2,1)}, u32[]{:S(2)}, u32[]{:S(2)}) async-start(bf16[32,8,2048]{2,1,0:T(8,128)(2,1)} %fusion.60), calls=%async_computation.5 | async-start | bytes 2097152 | tf_op jit(solution)/shard_map/all_to_all | solution.py:85
  196.2 0.0 copy-start.1
  196.2 1.8 fusion.69
  198.1 24.4 %all-to-all-done.5 = bf16[32,8,2048]{2,1,0:T(8,128)(2,1)} async-done(((bf16[32,8,2048]{2,1,0:T(8,128)(2,1)}), bf16[32,8,2048]{2,1,0:T(8,128)(2,1)}, u32[]{:S(2)}, u32[]{:S(2)}) %all-to-all-start.5) | async-done | bytes 1048608 | tf_op jit(solution)/shard_map/all_to_all | solution.py:85
  222.4 2.7 %fusion.56 = bf16[256,2048]{1,0:T(8,128)(2,1)} fusion(f32[256,2048]{1,0:T(8,128)S(1)} %fusion.69, bf16[32,8,2048]{2,1,0:T(8,128)(2,1)} %all-to-all-done.5, s32[256]{0:T(256)S(1)} %get-tuple-element.5), kind=kOutput, calls=%fused_computation.37 | convolution fusion | flops 269549568 | bytes 4195328 | tf_op jit(solution)/shard_map/dot_general | solution.py:10
  225.2 0.0 copy-done.1
  (7 shorter events, 0.1 us)
Async XLA Ops:
  0.0 2.1 copy-start
  0.0 10.9 %copy-start.2 = (bf16[256,2048]{1,0:T(8,128)(2,1)S(1)}, bf16[256,2048]{1,0:T(8,128)(2,1)}, u32[]{:S(2)}) copy-start(bf16[256,2048]{1,0:T(8,128)(2,1)} %param.8) | copy-start | bytes 3145732
  3.6 33.5 %all-to-all-start.1 = ((bf16[32,8,2048]{2,1,0:T(8,128)(2,1)}), bf16[32,8,2048]{2,1,0:T(8,128)(2,1)S(1)}, u32[]{:S(2)}, u32[]{:S(2)}) async-start(bf16[32,8,2048]{2,1,0:T(8,128)(2,1)} %convolution_convert_fusion.2), calls=%async_computation.1 | async-start | bytes 2097152 | tf_op jit(solution)/shard_map/all_to_all | solution.py:66
  37.1 30.0 %all-to-all-start = ((bf16[32,8,2048]{2,1,0:T(8,128)(2,1)}), bf16[32,8,2048]{2,1,0:T(8,128)(2,1)}, u32[]{:S(2)}, u32[]{:S(2)}) async-start(bf16[32,8,2048]{2,1,0:T(8,128)(2,1)} %convolution_convert_fusion.3), calls=%async_computation | async-start | bytes 2097152 | tf_op jit(solution)/shard_map/all_to_all | solution.py:66
  67.1 43.0 %all-to-all-start.4 = ((bf16[32,8,2048]{2,1,0:T(8,128)(2,1)}), bf16[32,8,2048]{2,1,0:T(8,128)(2,1)S(1)}, u32[]{:S(2)}, u32[]{:S(2)}) async-start(bf16[32,8,2048]{2,1,0:T(8,128)(2,1)} %convolution_convert_fusion), calls=%async_computation.4 | async-start | bytes 2097152 | tf_op jit(solution)/shard_map/all_to_all | solution.py:66
  110.1 31.9 %all-to-all-start.3 = ((bf16[32,8,2048]{2,1,0:T(8,128)(2,1)}), bf16[32,8,2048]{2,1,0:T(8,128)(2,1)S(1)}, u32[]{:S(2)}, u32[]{:S(2)}) async-start(bf16[32,8,2048]{2,1,0:T(8,128)(2,1)} %convolution_convert_fusion.1), calls=%async_computation.3 | async-start | bytes 2097152 | tf_op jit(solution)/shard_map/all_to_all | solution.py:66
  116.0 10.2 %copy-start.3 = (f32[256,4096]{1,0:T(8,128)S(1)}, f32[256,4096]{1,0:T(8,128)}, u32[]{:S(2)}) copy-start(f32[256,4096]{1,0:T(8,128)} %fusion.6) | copy-start | bytes 12582916
  142.0 48.3 %all-to-all-start.2 = ((bf16[32,8,2048]{2,1,0:T(8,128)(2,1)}), bf16[32,8,2048]{2,1,0:T(8,128)(2,1)}, u32[]{:S(2)}, u32[]{:S(2)}) async-start(bf16[32,8,2048]{2,1,0:T(8,128)(2,1)} %fusion.57), calls=%async_computation.2 | async-start | bytes 2097152 | tf_op jit(solution)/shard_map/all_to_all | solution.py:85
  190.3 32.1 %all-to-all-start.5 = ((bf16[32,8,2048]{2,1,0:T(8,128)(2,1)}), bf16[32,8,2048]{2,1,0:T(8,128)(2,1)}, u32[]{:S(2)}, u32[]{:S(2)}) async-start(bf16[32,8,2048]{2,1,0:T(8,128)(2,1)} %fusion.60), calls=%async_computation.5 | async-start | bytes 2097152 | tf_op jit(solution)/shard_map/all_to_all | solution.py:85
  196.2 28.9 %copy-start.1 = (bf16[256,2048]{1,0:T(8,128)(2,1)S(1)}, bf16[256,2048]{1,0:T(8,128)(2,1)}, u32[]{:S(2)}) copy-start(bf16[256,2048]{1,0:T(8,128)(2,1)} %param.7) | copy-start | bytes 3145732

commit v2 on v1

v2 whole, which is shorter than its diff:
```python
import functools

import jax
import jax.numpy as jnp
from jax import lax
from jax.experimental import pallas as pl
from jax.experimental.pallas import tpu as pltpu
from jax.sharding import PartitionSpec as P

PIECES = 2
MIB = 1 << 20


def dot(a, b, contract):
    return lax.dot_general(a, b, (contract, ((), ())), preferred_element_type=jnp.float32)


def hidden_grads(gate_pre, up_pre, hidden_grad):
    sigmoid_gate = jax.nn.sigmoid(gate_pre)
    up_grad = (hidden_grad * gate_pre * sigmoid_gate).astype(jnp.bfloat16)
    gate_grad = (
        hidden_grad * up_pre * sigmoid_gate * (1.0 + gate_pre * (1.0 - sigmoid_gate))
    ).astype(jnp.bfloat16)
    return gate_grad, up_grad


def expert_partial(rows, grads, gate, up, down):
    gate_pre, up_pre = dot(rows, gate, ((1,), (0,))), dot(rows, up, ((1,), (0,)))
    hidden_grad = dot(grads, down, ((1,), (1,)))
    gate_grad, up_grad = hidden_grads(gate_pre, up_pre, hidden_grad)
    partial_sum = dot(gate_grad, gate, ((1,), (1,))) + dot(up_grad, up, ((1,), (1,)))
    return partial_sum.astype(jnp.bfloat16)


def expert_kernel(pair_ref, gate_ref, up_ref, down_ref, out_ref, total):
    width = out_ref.shape[1]
    step = pl.program_id(0)

    @pl.when(step == 0)
    def _():
        total[...] = jnp.zeros_like(total)

    gate, up = gate_ref[0], up_ref[0]
    rows = pair_ref[:, :width]
    gate_pre, up_pre = dot(rows, gate, ((1,), (0,))), dot(rows, up, ((1,), (0,)))
    hidden_grad = dot(pair_ref[:, width:], down_ref[0], ((1,), (1,)))
    gate_grad, up_grad = hidden_grads(gate_pre, up_pre, hidden_grad)
    total[...] += dot(gate_grad, gate, ((1,), (1,))) + dot(up_grad, up, ((1,), (1,)))

    @pl.when(step == pl.num_programs(0) - 1)
    def _():
        out_ref[...] = total[...].astype(out_ref.dtype)


def expert_piece(pair, gate_weight, up_weight, down_weight):
    rows, width = pair.shape[0], pair.shape[1] // 2
    hidden = gate_weight.shape[2]
    tile = min(512, hidden)
    return pl.pallas_call(
        expert_kernel,
        grid=(hidden // tile,),
        in_specs=[
            pl.BlockSpec((rows, 2 * width), lambda i: (0, 0)),
            pl.BlockSpec((1, width, tile), lambda i: (0, 0, i)),
            pl.BlockSpec((1, width, tile), lambda i: (0, 0, i)),
            pl.BlockSpec((1, tile, width), lambda i: (0, i, 0)),
        ],
        out_specs=pl.BlockSpec((rows, width), lambda i: (0, 0)),
        out_shape=jax.ShapeDtypeStruct((rows, width), jnp.bfloat16),
        scratch_shapes=[pltpu.VMEM((rows, width), jnp.float32)],
        compiler_params=pltpu.CompilerParams(vmem_limit_bytes=40 * MIB),
        cost_estimate=pl.CostEstimate(
            flops=10 * rows * width * hidden,
            bytes_accessed=6 * width * hidden + 6 * rows * width,
            transcendentals=rows * hidden,
        ),
    )(pair, gate_weight, up_weight, down_weight)


def pack_kernel(place_ref, rows_ref, grads_ref, out_ref):
    count, width = out_ref.shape[0], rows_ref.shape[1]
    ids = lax.broadcasted_iota(jnp.int32, (count, place_ref.shape[1]), 0)
    select = (ids == place_ref[...]).astype(jnp.bfloat16)
    out_ref[:, :width] = dot(select, rows_ref[...], ((1,), (0,))).astype(out_ref.dtype)
    out_ref[:, width:] = dot(select, grads_ref[...], ((1,), (0,))).astype(out_ref.dtype)


def pack_pair(place, tokens, out_grads, count):
    rows, width = tokens.shape
    return pl.pallas_call(
        pack_kernel,
        out_shape=jax.ShapeDtypeStruct((count, 2 * width), jnp.bfloat16),
        compiler_params=pltpu.CompilerParams(vmem_limit_bytes=24 * MIB),
        cost_estimate=pl.CostEstimate(
            flops=4 * count * rows * width, bytes_accessed=4 * (rows + count) * width, transcendentals=0
        ),
    )(place[None, :], tokens, out_grads)


def places(species, expert_table, tensor_size):
    experts = expert_table.shape[0]
    rows_dev = species.shape[0] // tensor_size
    expert_ids = jnp.arange(experts, dtype=jnp.int32)
    species_hits = species == expert_ids[None, :]
    expert_of = jnp.sum(jnp.where(species_hits, expert_table[None, :], 0), axis=1).reshape(
        tensor_size, rows_dev
    )
    onehot = (expert_of[:, :, None] == expert_ids[None, None, :]).astype(jnp.int32)
    earlier = jnp.cumsum(onehot, axis=1) - onehot
    slot_of = jnp.sum(earlier * onehot, axis=2)
    return expert_of, slot_of


def in_pieces(tokens, out_grads, species, expert_table, gate_weight, up_weight, down_weight):
    rows_dev, width = tokens.shape
    experts = expert_table.shape[0]
    depth = 2 * rows_dev // experts // PIECES
    count = experts * depth
    expert_of, slot_of = places(species, expert_table, 1)
    slot = slot_of[0][None, :] - depth * jnp.arange(PIECES, dtype=jnp.int32)[:, None]
    place_of = jnp.where((slot >= 0) & (slot < depth), expert_of * depth + slot, -1)
    exchange = functools.partial(
        lax.all_to_all, axis_name="expert", split_axis=0, concat_axis=0, tiled=True
    )
    arrived = []
    for piece in range(PIECES):
        packed = pack_pair(place_of[piece], tokens, out_grads, count)
        arrived.append(exchange(packed.reshape(experts, depth, 2 * width)))
    own = None
    for piece in range(PIECES):
        pair = arrived[piece].reshape(count, 2 * width)
        partial_sum = expert_piece(pair, gate_weight, up_weight, down_weight)
        returned = exchange(partial_sum.reshape(experts, depth, width)).reshape(count, width)
        ids = jnp.arange(count, dtype=jnp.int32)
        select = (ids[:, None] == place_of[piece][None, :]).astype(jnp.bfloat16)
        term = dot(select, returned, ((0,), (0,)))
        own = term if own is None else own + term
    return own.astype(jnp.bfloat16)


def in_groups(tokens, out_grads, species, expert_table, gate_weight, up_weight, down_weight):
    tensor_size = lax.axis_size("tensor")
    tensor_index = lax.axis_index("tensor")
    experts = expert_table.shape[0]
    rows_dev = tokens.shape[0] // tensor_size
    model_width = tokens.shape[1] * tensor_size
    capacity = 2 * rows_dev // experts
    expert_of, slot_of = places(species, expert_table, tensor_size)
    group_tokens, group_grads = (
        lax.all_gather(tokens, "tensor", axis=1, tiled=True),
        lax.all_gather(out_grads, "tensor", axis=1, tiled=True),
    )
    place_of = expert_of * capacity + slot_of
    place_ids = jnp.arange(experts * capacity, dtype=jnp.int32)
    select = (place_ids[None, :, None] == place_of[:, None, :]).astype(jnp.bfloat16)

    def send(rows):
        packed = jnp.einsum(
            "tecr,trd->etcd",
            select.reshape(tensor_size, experts, capacity, rows_dev),
            rows.reshape(tensor_size, rows_dev, model_width),
            preferred_element_type=jnp.float32,
        ).astype(jnp.bfloat16)
        packed = packed.reshape(experts, tensor_size * capacity, model_width)
        arrived = lax.all_to_all(packed, "expert", split_axis=0, concat_axis=0, tiled=True)
        return arrived.reshape(-1, model_width)

    partial_sum = expert_partial(
        send(group_tokens), send(group_grads), gate_weight[0], up_weight[0], down_weight[0]
    )
    summed = lax.psum_scatter(
        partial_sum.reshape(experts, tensor_size * capacity, model_width),
        "tensor",
        scatter_dimension=1,
        tiled=True,
    )
    returned = lax.all_to_all(summed, "expert", split_axis=0, concat_axis=0, tiled=True)
    own_select = lax.dynamic_index_in_dim(select, tensor_index, 0, keepdims=False)
    own = dot(own_select, returned.reshape(experts * capacity, model_width), ((0,), (0,)))
    return lax.all_to_all(
        own.astype(jnp.bfloat16), "tensor", split_axis=1, concat_axis=0, tiled=True
    )


def per_device(tokens, out_grads, species, expert_table, *weights):
    whole = lax.axis_size("tensor") == 1
    capacity = 2 * tokens.shape[0] // expert_table.shape[0]
    form = in_pieces if whole and capacity % (8 * PIECES) == 0 else in_groups
    return form(tokens, out_grads, species, expert_table, *weights)


def solution(mesh):
    placed = (
        P("expert", "tensor"),
        P("expert", "tensor"),
        P("expert", None),
        P(),
        P("expert", None, "tensor"),
        P("expert", None, "tensor"),
        P("expert", "tensor", None),
    )
    return jax.shard_map(
        per_device, mesh=mesh, in_specs=placed, out_specs=P("expert", "tensor"), check_vma=False
    )
```

time: 226 us -> 183 us (0.81)
  matrix products: 125 us -> 3.18 us
  Pallas kernels: 0 us -> 62.6 us
  waiting for transfers between devices: 67.4 us -> 90.3 us
  starting transfers between devices: 30.4 us -> 21.3 us
  local copies, waits for them, and re-layouts: 0.42 us -> 2.87 us
    dot_general x12 -> x2, matrix products: 119 us -> 3.18 us  [dot(): lax.dot_general(a, b, (contract, ((), ())), preferred_element_type=jnp.fl...]
    pallas_call x0 -> x4, Pallas kernels: none -> 62.6 us  [the longest x2 58.5 us: expert_piece(): pl.pallas_call(expert_kernel, grid=(hidden // tile,), in_specs=[pl.BlockS...]
    all_to_all x6 -> x4, waiting for transfers between devices: 67.4 us -> 90.3 us  [the longest x2 65.8 us: in_pieces(): arrived.append(exchange(packed.reshape(experts, depth, 2 * width)))]
    all_to_all x6 -> x4, starting transfers between devices: 30.4 us -> 21.3 us  [the longest x2 11.4 us: in_pieces(): arrived.append(exchange(packed.reshape(experts, depth, 2 * width)))]
    dot_general x4 -> x0, matrix products: 5.87 us -> none  [send(): jnp.einsum('tecr,trd->etcd', select.reshape(tensor_size, experts, depth,...]
    unnamed x8 -> x10, local copies, waits for them, and re-layouts: 0.02 us -> 2.46 us
  transfers between devices with their start and end apart: 6 -> 4, of which waited for: 4 -> 3; matrix products, arithmetic and copies ran while one was open for 54% -> 1% of each run, Pallas kernels for 0% -> 33%
where the time goes in v2:
time: 183 us; the launch traced here: 182 us
  waiting for transfers between devices  90.3 us (49%)
  Pallas kernels  62.6 us (34%)
  starting transfers between devices  21.3 us (12%)
  matrix products  3.18 us (2%)
  local copies, waits for them, and re-layouts  2.87 us (2%)
    all_to_all x2, waiting for transfers between devices, in_pieces(): arrived.append(exchange(packed.reshape(experts, depth, 2 * width)))  65.8 us
    pallas_call x2, Pallas kernels, expert_piece(): pl.pallas_call(expert_kernel, grid=(hidden // tile,), in_specs=[pl.BlockS...  58.5 us
    all_to_all x2, waiting for transfers between devices, in_pieces(): exchange(partial_sum.reshape(experts, depth, width)).reshape(count, width)  24.5 us
    all_to_all x2, starting transfers between devices, in_pieces(): arrived.append(exchange(packed.reshape(experts, depth, 2 * width)))  11.4 us
    all_to_all x2, starting transfers between devices, in_pieces(): exchange(partial_sum.reshape(experts, depth, width)).reshape(count, width)  9.84 us
    pallas_call x2, Pallas kernels, pack_pair(): pl.pallas_call(pack_kernel, out_shape=jax.ShapeDtypeStruct((count, 2 * wi...  4.05 us
  transfers between devices with their start and end apart: 4, of which 3 were waited for; matrix products, arithmetic and copies ran while one was open for 1% of the time, Pallas kernels for 33%

profile of v2, /device:TPU:0, one launch (start us, length us, event | category | flops | bytes accessed | tf_op | source)
XLA Modules:
  0.0 182.0 jit_solution(65140285013402896)
XLA Ops:
  0.0 0.8 select_reduce_fusion
  0.8 0.6 reduce-window.6
  1.4 0.2 slice_reduce_fusion
  1.7 0.1 copy.13
  1.8 0.1 broadcast.63
  1.9 0.1 fusion.6
  2.0 0.1 and_select_fusion
  2.1 0.0 copy-start
  2.1 1.2 copy-done
  3.3 0.0 copy-start.2
  3.3 1.2 copy-done.2
  4.5 2.0 %shard_map.73 = bf16[256,4096]{1,0:T(8,128)(2,1)} custom-call(s32[1,256]{1,0:T(1,128)S(1)} %get-tuple-element.6.place_ref, bf16[256,2048]{1,0:T(8,128)(2,1)S(1)} %copy-done, bf16[256,2048]{1,0:T(8,128)(2,1)S(1)} %copy-done.2), custom_call_target="tpu_custom_call" | custom-call | flops 536870912 | bytes 4194304 | tf_op jit(solution)/shard_map/pallas_call | solution.py:90
  6.5 0.0 copy-start.1
  6.5 0.0 copy-start.3
  6.5 7.4 %all-to-all-start = ((bf16[32,8,4096]{2,1,0:T(8,128)(2,1)}), bf16[32,8,4096]{2,1,0:T(8,128)(2,1)}, u32[]{:S(2)}, u32[]{:S(2)}) async-start(bf16[32,8,4096]{2,1,0:T(8,128)(2,1)} %bitcast.8), calls=%async_computation | async-start | bytes 4194304 | tf_op jit(solution)/shard_map/all_to_all | solution.py:128
  14.0 0.0 copy-done.1
  14.0 0.0 copy-done.3
  14.0 2.0 %shard_map.75 = bf16[256,4096]{1,0:T(8,128)(2,1)} custom-call(s32[1,256]{1,0:T(1,128)S(1)} %get-tuple-element.5.place_ref, bf16[256,2048]{1,0:T(8,128)(2,1)S(1)} %copy-done.1, bf16[256,2048]{1,0:T(8,128)(2,1)S(1)} %copy-done.3), custom_call_target="tpu_custom_call" | custom-call | flops 536870912 | bytes 4194304 | tf_op jit(solution)/shard_map/pallas_call | solution.py:90
  16.0 46.8 %all-to-all-done = bf16[32,8,4096]{2,1,0:T(8,128)(2,1)} async-done(((bf16[32,8,4096]{2,1,0:T(8,128)(2,1)}), bf16[32,8,4096]{2,1,0:T(8,128)(2,1)}, u32[]{:S(2)}, u32[]{:S(2)}) %all-to-all-start) | async-done | bytes 2097184 | tf_op jit(solution)/shard_map/all_to_all | solution.py:128
  62.8 4.0 %all-to-all-start.2 = ((bf16[32,8,4096]{2,1,0:T(8,128)(2,1)}), bf16[32,8,4096]{2,1,0:T(8,128)(2,1)S(1)}, u32[]{:S(2)}, u32[]{:S(2)}) async-start(bf16[32,8,4096]{2,1,0:T(8,128)(2,1)} %bitcast.13), calls=%async_computation.2 | async-start | bytes 4194304 | tf_op jit(solution)/shard_map/all_to_all | solution.py:128
  66.8 29.9 %shard_map.74 = bf16[256,2048]{1,0:T(8,128)(2,1)} custom-call(bf16[256,4096]{1,0:T(8,128)(2,1)} %bitcast.9.pair_ref, bf16[1,2048,4096]{2,1,0:T(8,128)(2,1)} %gate_ref.3, bf16[1,2048,4096]{2,1,0:T(8,128)(2,1)} %up_ref.3, bf16[1,4096,2048]{2,1,0:T(8,128)(2,1)} %down_ref.3), custom_call_target="tpu_custom_call" | custom-call | flops 21474836480 | bytes 53477376 | tf_op jit(solution)/shard_map/pallas_call | solution.py:59
  96.7 19.0 %all-to-all-done.2 = bf16[32,8,4096]{2,1,0:T(8,128)(2,1)S(1)} async-done(((bf16[32,8,4096]{2,1,0:T(8,128)(2,1)}), bf16[32,8,4096]{2,1,0:T(8,128)(2,1)S(1)}, u32[]{:S(2)}, u32[]{:S(2)}) %all-to-all-start.2) | async-done | bytes 2097184 | tf_op jit(solution)/shard_map/all_to_all | solution.py:128
  115.7 4.0 %all-to-all-start.1 = ((bf16[32,8,2048]{2,1,0:T(8,128)(2,1)}), bf16[32,8,2048]{2,1,0:T(8,128)(2,1)S(1)}, u32[]{:S(2)}, u32[]{:S(2)}) async-start(bf16[32,8,2048]{2,1,0:T(8,128)(2,1)} %bitcast.10), calls=%async_computation.1 | async-start | bytes 2097152 | tf_op jit(solution)/shard_map/all_to_all | solution.py:133
  119.8 28.6 %shard_map.76 = bf16[256,2048]{1,0:T(8,128)(2,1)} custom-call(bf16[256,4096]{1,0:T(8,128)(2,1)S(1)} %bitcast.29, bf16[1,2048,4096]{2,1,0:T(8,128)(2,1)} %gate_ref.3, bf16[1,2048,4096]{2,1,0:T(8,128)(2,1)} %up_ref.3, bf16[1,4096,2048]{2,1,0:T(8,128)(2,1)} %down_ref.3), custom_call_target="tpu_custom_call" | custom-call | flops 21474836480 | bytes 53477376 | tf_op jit(solution)/shard_map/pallas_call | solution.py:59
  148.4 0.0 all-to-all-done.1
  148.4 0.0 copy-start.4
  148.4 5.8 %all-to-all-start.3 = ((bf16[32,8,2048]{2,1,0:T(8,128)(2,1)}), bf16[32,8,2048]{2,1,0:T(8,128)(2,1)S(1)}, u32[]{:S(2)}, u32[]{:S(2)}) async-start(bf16[32,8,2048]{2,1,0:T(8,128)(2,1)} %bitcast.15), calls=%async_computation.3 | async-start | bytes 2097152 | tf_op jit(solution)/shard_map/all_to_all | solution.py:133
  154.3 0.0 copy-done.4
  154.3 1.7 fusion.2
  156.0 24.5 %all-to-all-done.3 = bf16[32,8,2048]{2,1,0:T(8,128)(2,1)S(1)} async-done(((bf16[32,8,2048]{2,1,0:T(8,128)(2,1)}), bf16[32,8,2048]{2,1,0:T(8,128)(2,1)S(1)}, u32[]{:S(2)}, u32[]{:S(2)}) %all-to-all-start.3) | async-done | bytes 1048608 | tf_op jit(solution)/shard_map/all_to_all | solution.py:133
  180.5 1.5 fusion
  (8 shorter events, 0.1 us)
Async XLA Ops:
  2.1 1.2 copy-start
  3.3 1.2 copy-start.2
  6.5 7.4 %copy-start.1 = (bf16[256,2048]{1,0:T(8,128)(2,1)S(1)}, bf16[256,2048]{1,0:T(8,128)(2,1)}, u32[]{:S(2)}) copy-start(bf16[256,2048]{1,0:T(8,128)(2,1)} %rows_ref.3) | copy-start | bytes 3145732
  6.5 7.4 %copy-start.3 = (bf16[256,2048]{1,0:T(8,128)(2,1)S(1)}, bf16[256,2048]{1,0:T(8,128)(2,1)}, u32[]{:S(2)}) copy-start(bf16[256,2048]{1,0:T(8,128)(2,1)} %grads_ref.3) | copy-start | bytes 3145732
  6.5 56.3 %all-to-all-start = ((bf16[32,8,4096]{2,1,0:T(8,128)(2,1)}), bf16[32,8,4096]{2,1,0:T(8,128)(2,1)}, u32[]{:S(2)}, u32[]{:S(2)}) async-start(bf16[32,8,4096]{2,1,0:T(8,128)(2,1)} %bitcast.8), calls=%async_computation | async-start | bytes 4194304 | tf_op jit(solution)/shard_map/all_to_all | solution.py:128
  62.8 52.9 %all-to-all-start.2 = ((bf16[32,8,4096]{2,1,0:T(8,128)(2,1)}), bf16[32,8,4096]{2,1,0:T(8,128)(2,1)S(1)}, u32[]{:S(2)}, u32[]{:S(2)}) async-start(bf16[32,8,4096]{2,1,0:T(8,128)(2,1)} %bitcast.13), calls=%async_computation.2 | async-start | bytes 4194304 | tf_op jit(solution)/shard_map/all_to_all | solution.py:128
  115.7 32.7 %all-to-all-start.1 = ((bf16[32,8,2048]{2,1,0:T(8,128)(2,1)}), bf16[32,8,2048]{2,1,0:T(8,128)(2,1)S(1)}, u32[]{:S(2)}, u32[]{:S(2)}) async-start(bf16[32,8,2048]{2,1,0:T(8,128)(2,1)} %bitcast.10), calls=%async_computation.1 | async-start | bytes 2097152 | tf_op jit(solution)/shard_map/all_to_all | solution.py:133
  148.4 5.8 %copy-start.4 = (bf16[32,8,2048]{2,1,0:T(8,128)(2,1)}, bf16[32,8,2048]{2,1,0:T(8,128)(2,1)S(1)}, u32[]{:S(2)}) copy-start(bf16[32,8,2048]{2,1,0:T(8,128)(2,1)S(1)} %all-to-all-done.1) | copy-start | bytes 3145732
  148.4 32.1 %all-to-all-start.3 = ((bf16[32,8,2048]{2,1,0:T(8,128)(2,1)}), bf16[32,8,2048]{2,1,0:T(8,128)(2,1)S(1)}, u32[]{:S(2)}, u32[]{:S(2)}) async-start(bf16[32,8,2048]{2,1,0:T(8,128)(2,1)} %bitcast.15), calls=%async_computation.3 | async-start | bytes 2097152 | tf_op jit(solution)/shard_map/all_to_all | solution.py:133

commit v3 on v2

--- a/solution.py
+++ b/solution.py
@@ -1,5 +1,3 @@
-import functools
-
 import jax
 import jax.numpy as jnp
 from jax import lax
@@ -7,7 +5,6 @@
 from jax.experimental.pallas import tpu as pltpu
 from jax.sharding import PartitionSpec as P
 
-PIECES = 2
 MIB = 1 << 20
 
 
@@ -32,69 +29,115 @@
     return partial_sum.astype(jnp.bfloat16)
 
 
-def expert_kernel(pair_ref, gate_ref, up_ref, down_ref, out_ref, total):
-    width = out_ref.shape[1]
+def expert_kernel(*refs):
+    count = (len(refs) - 5) // 2
+    block_refs, (gate_ref, up_ref, down_ref) = refs[:count], refs[count : count + 3]
+    out_refs, (pair, total) = refs[count + 3 : 2 * count + 3], refs[2 * count + 3 :]
+    depth, width = out_refs[0].shape
     step = pl.program_id(0)
 
     @pl.when(step == 0)
     def _():
+        for k, block_ref in enumerate(block_refs):
+            pair[k * depth : (k + 1) * depth, :] = block_ref[...]
         total[...] = jnp.zeros_like(total)
 
     gate, up = gate_ref[0], up_ref[0]
-    rows = pair_ref[:, :width]
+    rows = pair[:, :width]
     gate_pre, up_pre = dot(rows, gate, ((1,), (0,))), dot(rows, up, ((1,), (0,)))
-    hidden_grad = dot(pair_ref[:, width:], down_ref[0], ((1,), (1,)))
+    hidden_grad = dot(pair[:, width:], down_ref[0], ((1,), (1,)))
     gate_grad, up_grad = hidden_grads(gate_pre, up_pre, hidden_grad)
     total[...] += dot(gate_grad, gate, ((1,), (1,))) + dot(up_grad, up, ((1,), (1,)))
 
     @pl.when(step == pl.num_programs(0) - 1)
     def _():
-        out_ref[...] = total[...].astype(out_ref.dtype)
-
-
-def expert_piece(pair, gate_weight, up_weight, down_weight):
-    rows, width = pair.shape[0], pair.shape[1] // 2
+        for k, out_ref in enumerate(out_refs):
+            out_ref[...] = total[k * depth : (k + 1) * depth, :].astype(out_ref.dtype)
+
+
+def expert_piece(blocks, gate_weight, up_weight, down_weight):
+    depth, width = blocks[0].shape[0], blocks[0].shape[1] // 2
+    rows = depth * len(blocks)
     hidden = gate_weight.shape[2]
     tile = min(512, hidden)
     return pl.pallas_call(
         expert_kernel,
         grid=(hidden // tile,),
-        in_specs=[
-            pl.BlockSpec((rows, 2 * width), lambda i: (0, 0)),
+        in_specs=[pl.BlockSpec((depth, 2 * width), lambda i: (0, 0))] * len(blocks)
+        + [
             pl.BlockSpec((1, width, tile), lambda i: (0, 0, i)),
             pl.BlockSpec((1, width, tile), lambda i: (0, 0, i)),
             pl.BlockSpec((1, tile, width), lambda i: (0, i, 0)),
         ],
-        out_specs=pl.BlockSpec((rows, width), lambda i: (0, 0)),
-        out_shape=jax.ShapeDtypeStruct((rows, width), jnp.bfloat16),
-        scratch_shapes=[pltpu.VMEM((rows, width), jnp.float32)],
+        out_specs=[pl.BlockSpec((depth, width), lambda i: (0, 0))] * len(blocks),
+        out_shape=[jax.ShapeDtypeStruct((depth, width), jnp.bfloat16)] * len(blocks),
+        scratch_shapes=[
+            pltpu.VMEM((rows, 2 * width), jnp.bfloat16),
+            pltpu.VMEM((rows, width), jnp.float32),
+        ],
         compiler_params=pltpu.CompilerParams(vmem_limit_bytes=40 * MIB),
         cost_estimate=pl.CostEstimate(
             flops=10 * rows * width * hidden,
             bytes_accessed=6 * width * hidden + 6 * rows * width,
             transcendentals=rows * hidden,
         ),
-    )(pair, gate_weight, up_weight, down_weight)
-
-
-def pack_kernel(place_ref, rows_ref, grads_ref, out_ref):
-    count, width = out_ref.shape[0], rows_ref.shape[1]
+        name="expert_piece",
+    )(*blocks, gate_weight, up_weight, down_weight)
+
+
+def pack_kernel(place_ref, rows_ref, grads_ref, *out_refs):
+    depth, width = out_refs[0].shape[0], rows_ref.shape[1]
+    count = depth * len(out_refs)
     ids = lax.broadcasted_iota(jnp.int32, (count, place_ref.shape[1]), 0)
     select = (ids == place_ref[...]).astype(jnp.bfloat16)
-    out_ref[:, :width] = dot(select, rows_ref[...], ((1,), (0,))).astype(out_ref.dtype)
-    out_ref[:, width:] = dot(select, grads_ref[...], ((1,), (0,))).astype(out_ref.dtype)
-
-
-def pack_pair(place, tokens, out_grads, count):
+    for low, ref in ((0, rows_ref), (width, grads_ref)):
+        packed = dot(select, ref[...], ((1,), (0,))).astype(jnp.bfloat16)
+        for k, out_ref in enumerate(out_refs):
+            out_ref[:, low : low + width] = packed[k * depth : (k + 1) * depth, :]
+
+
+def pack_blocks(place, tokens, out_grads, blocks, depth):
     rows, width = tokens.shape
+    count = blocks * depth
     return pl.pallas_call(
         pack_kernel,
-        out_shape=jax.ShapeDtypeStruct((count, 2 * width), jnp.bfloat16),
+        out_shape=[jax.ShapeDtypeStruct((depth, 2 * width), jnp.bfloat16)] * blocks,
         compiler_params=pltpu.CompilerParams(vmem_limit_bytes=24 * MIB),
         cost_estimate=pl.CostEstimate(
             flops=4 * count * rows * width, bytes_accessed=4 * (rows + count) * width, transcendentals=0
         ),
+        name="pack_blocks",
     )(place[None, :], tokens, out_grads)
+
+
+def unpack_kernel(*refs):
+    (place_ref, before_ref), (out_ref, gathered) = refs[:2], refs[-2:]
+    low = 0
+    for block_ref in refs[2:-2]:
+        high = low + block_ref.shape[0]
+        gathered[low:high, :] = block_ref[...]
+        low = high
+    ids = lax.broadcasted_iota(jnp.int32, (place_ref.shape[0], low), 1)
+    select = (ids == place_ref[...]).astype(jnp.bfloat16)
+    found = dot(select, gathered[...], ((1,), (0,)))
+    out_ref[...] = (found + before_ref[...].astype(jnp.float32)).astype(out_ref.dtype)
+
+
+def unpack_blocks(place, before, blocks):
+    rows, width = before.shape
+    count = sum(block.shape[0] for block in blocks)
+    return pl.pallas_call(
+        unpack_kernel,
+        out_shape=jax.ShapeDtypeStruct((rows, width), jnp.bfloat16),
+        scratch_shapes=[pltpu.VMEM((count, width), jnp.bfloat16)],
+        compiler_params=pltpu.CompilerParams(vmem_limit_bytes=24 * MIB),
+        cost_estimate=pl.CostEstimate(
+            flops=2 * rows * count * width,
+            bytes_accessed=2 * (2 * rows + count) * width,
+            transcendentals=0,
+        ),
+        name="unpack_blocks",
+    )(place[:, None], before, *blocks)
 
 
 def places(species, expert_table, tensor_size):
@@ -111,31 +154,48 @@
     return expert_of, slot_of
 
 
-def in_pieces(tokens, out_grads, species, expert_table, gate_weight, up_weight, down_weight):
+def after(arrays, others):
+    tied = lax.optimization_barrier((tuple(arrays), tuple(others)))
+    return list(tied[0])
+
+
+def in_halves(tokens, out_grads, species, expert_table, gate_weight, up_weight, down_weight):
     rows_dev, width = tokens.shape
     experts = expert_table.shape[0]
-    depth = 2 * rows_dev // experts // PIECES
-    count = experts * depth
-    expert_of, slot_of = places(species, expert_table, 1)
-    slot = slot_of[0][None, :] - depth * jnp.arange(PIECES, dtype=jnp.int32)[:, None]
-    place_of = jnp.where((slot >= 0) & (slot < depth), expert_of * depth + slot, -1)
-    exchange = functools.partial(
-        lax.all_to_all, axis_name="expert", split_axis=0, concat_axis=0, tiled=True
-    )
-    arrived = []
-    for piece in range(PIECES):
-        packed = pack_pair(place_of[piece], tokens, out_grads, count)
-        arrived.append(exchange(packed.reshape(experts, depth, 2 * width)))
-    own = None
-    for piece in range(PIECES):
-        pair = arrived[piece].reshape(count, 2 * width)
-        partial_sum = expert_piece(pair, gate_weight, up_weight, down_weight)
-        returned = exchange(partial_sum.reshape(experts, depth, width)).reshape(count, width)
-        ids = jnp.arange(count, dtype=jnp.int32)
-        select = (ids[:, None] == place_of[piece][None, :]).astype(jnp.bfloat16)
-        term = dot(select, returned, ((0,), (0,)))
-        own = term if own is None else own + term
-    return own.astype(jnp.bfloat16)
+    depth, half = 2 * rows_dev // experts, experts // 2
+    count = half * depth
+    expert_of, slot_of = (found[0] for found in places(species, expert_table, 1))
+    step_of = expert_of ^ lax.axis_index("expert").astype(jnp.int32)
+    far_place = jnp.where(step_of >= half, (step_of - half) * depth + slot_of, -1)
+    near_place = jnp.where(step_of < half, (expert_of % half) * depth + slot_of, -1)
+    weights = gate_weight, up_weight, down_weight
+
+    def hop(array, k):
+        return lax.ppermute(array, "expert", [(i, i ^ (half + k)) for i in range(experts)])
+
+    def exchange(array):
+        return lax.all_to_all(
+            array.reshape(half, depth, -1),
+            "expert",
+            split_axis=0,
+            concat_axis=0,
+            axis_index_groups=[list(range(half)), list(range(half, experts))],
+            tiled=True,
+        ).reshape(count, -1)
+
+    far = pack_blocks(far_place, tokens, out_grads, half, depth)
+    far = [hop(block, k) for k, block in enumerate(far)]
+    near = exchange(pack_blocks(near_place, tokens, out_grads, 1, count)[0])
+    near = exchange(expert_piece([near], *weights)[0])
+    split = half // 2
+    first = expert_piece(far[:split], *weights)
+    first = [hop(block, k) for k, block in enumerate(after(first, far[split:]))]
+    last = expert_piece(far[split:], *weights)
+    last = [hop(block, k + split) for k, block in enumerate(last)]
+    own = unpack_blocks(near_place, jnp.zeros_like(tokens), [near])
+    first_place = jnp.where(far_place < split * depth, far_place, -1)
+    own = unpack_blocks(first_place, own, first)
+    return unpack_blocks(far_place - split * depth, own, last)
 
 
 def in_groups(tokens, out_grads, species, expert_table, gate_weight, up_weight, down_weight):
@@ -184,8 +244,10 @@
 
 def per_device(tokens, out_grads, species, expert_table, *weights):
     whole = lax.axis_size("tensor") == 1
-    capacity = 2 * tokens.shape[0] // expert_table.shape[0]
-    form = in_pieces if whole and capacity % (8 * PIECES) == 0 else in_groups
+    experts = expert_table.shape[0]
+    by_steps = experts % 4 == 0 and experts & (experts - 1) == 0
+    whole = whole and by_steps and (2 * tokens.shape[0] // experts) % 16 == 0
+    form = in_halves if whole else in_groups
     return form(tokens, out_grads, species, expert_table, *weights)
 
 

time: 183 us -> 222 us (1.21)
  starting transfers between devices: 21.3 us -> 78.6 us
  waiting for transfers between devices: 90.3 us -> 46.6 us
  Pallas kernels: 62.6 us -> 87.2 us
  local copies, waits for them, and re-layouts: 2.87 us -> 6.34 us
  matrix products: 3.18 us -> 0 us
    all_to_all x4 -> x2, waiting for transfers between devices: 90.3 us -> 0.01 us  [exchange(): lax.all_to_all(array.reshape(half, depth, -1), 'expert', split_axis=0, co...]
    ppermute x0 -> x32, starting transfers between devices: none -> 68.5 us  [hop(): lax.ppermute(array, 'expert', [(i, i ^ half + k) for i in range(experts)])]
    ppermute x0 -> x32, waiting for transfers between devices: none -> 46.6 us  [hop(): lax.ppermute(array, 'expert', [(i, i ^ half + k) for i in range(experts)])]
    pallas_call x2 -> x3, Pallas kernels: 58.5 us -> 81.2 us  [expert_piece(): pl.pallas_call(expert_kernel, grid=(hidden // tile,), in_specs=[pl.BlockS...]
    all_to_all x4 -> x2, starting transfers between devices: 21.3 us -> 10.1 us  [exchange(): lax.all_to_all(array.reshape(half, depth, -1), 'expert', split_axis=0, co...]
    dot_general x2 -> x0, matrix products: 3.18 us -> none  [dot(): lax.dot_general(a, b, (contract, ((), ())), preferred_element_type=jnp.fl...]
    unnamed x10 -> x18, local copies, waits for them, and re-layouts: 2.46 us -> 5.55 us
    pallas_call x2 -> x5, Pallas kernels: 4.05 us -> 5.95 us  [the longest x2 3.55 us: pack_blocks(): pl.pallas_call(pack_kernel, out_shape=[jax.ShapeDtypeStruct((depth, 2 * w...]
  transfers between devices with their start and end apart: 4 -> 34, of which waited for: 3 -> 12; matrix products, arithmetic and copies ran while one was open for 1% -> 0% of each run, Pallas kernels for 33% -> 38%
where the time goes in v3:
time: 222 us; the launch traced here: 221 us
  Pallas kernels  87.2 us (39%)
  starting transfers between devices  78.6 us (35%)
  waiting for transfers between devices  46.6 us (21%)
  local copies, waits for them, and re-layouts  6.34 us (3%)
    pallas_call x3, Pallas kernels, expert_piece(): pl.pallas_call(expert_kernel, grid=(hidden // tile,), in_specs=[pl.BlockS...  81.2 us
    ppermute x32, starting transfers between devices, hop(): lax.ppermute(array, 'expert', [(i, i ^ half + k) for i in range(experts)])  68.5 us
    ppermute x32, waiting for transfers between devices, hop(): lax.ppermute(array, 'expert', [(i, i ^ half + k) for i in range(experts)])  46.6 us
    all_to_all x2, starting transfers between devices, exchange(): lax.all_to_all(array.reshape(half, depth, -1), 'expert', split_axis=0, co...  10.1 us
    unnamed x18, local copies, waits for them, and re-layouts  5.55 us
  transfers between devices with their start and end apart: 34, of which 12 were waited for; matrix products, arithmetic and copies ran while one was open for 0% of the time, Pallas kernels for 38%

profile of v3, /device:TPU:0, one launch (start us, length us, event | category | flops | bytes accessed | tf_op | source)
XLA Modules:
  0.0 220.6 jit_solution(867618888979146340)
XLA Ops:
  0.0 0.8 select_reduce_fusion
  0.8 0.6 reduce-window.6
  2.0 1.2 copy-done
  3.2 1.2 copy-done.2
  4.4 2.1 pack_blocks.2
  6.5 6.3 %all-to-all-start = ((bf16[16,16,4096]{2,1,0:T(8,128)(2,1)}), bf16[16,16,4096]{2,1,0:T(8,128)(2,1)S(1)}, u32[]{:S(2)}, u32[]{:S(2)}) async-start(bf16[16,16,4096]{2,1,0:T(8,128)(2,1)} %bitcast.11), calls=%async_computation | async-start | bytes 4194304 | tf_op jit(solution)/shard_map/all_to_all | solution.py:177
  12.8 1.2 copy-done.1
  14.0 1.2 copy-done.3
  15.2 1.5 pack_blocks.3
  16.7 0.7 copy-done.8
  17.4 4.9 %collective-permute-start.10 = (bf16[16,4096]{1,0:T(8,128)(2,1)S(1)}, bf16[16,4096]{1,0:T(8,128)(2,1)S(1)}, u32[]{:S(2)}, u32[]{:S(2)}) collective-permute-start(bf16[16,4096]{1,0:T(8,128)(2,1)S(1)} %get-tuple-element.63), channel_id=1, source_target_pairs={{0,26},{1,27},{2,24},{3,25},{4,30},{5,31},{6,28},{7,29},{8,18},{9,... | collective-permute-start | bytes 393224 | tf_op jit(solution)/shard_map/ppermute | solution.py:174
  22.3 4.2 %collective-permute-start.12 = (bf16[16,4096]{1,0:T(8,128)(2,1)S(1)}, bf16[16,4096]{1,0:T(8,128)(2,1)S(1)}, u32[]{:S(2)}, u32[]{:S(2)}) collective-permute-start(bf16[16,4096]{1,0:T(8,128)(2,1)S(1)} %get-tuple-element.65), channel_id=1, source_target_pairs={{0,28},{1,29},{2,30},{3,31},{4,24},{5,25},{6,26},{7,27},{8,20},{9,... | collective-permute-start | bytes 393224 | tf_op jit(solution)/shard_map/ppermute | solution.py:174
  26.8 5.3 %collective-permute-start.14 = (bf16[16,4096]{1,0:T(8,128)(2,1)S(1)}, bf16[16,4096]{1,0:T(8,128)(2,1)S(1)}, u32[]{:S(2)}, u32[]{:S(2)}) collective-permute-start(bf16[16,4096]{1,0:T(8,128)(2,1)S(1)} %get-tuple-element.67), channel_id=1, source_target_pairs={{0,30},{1,31},{2,28},{3,29},{4,26},{5,27},{6,24},{7,25},{8,22},{9,... | collective-permute-start | bytes 393224 | tf_op jit(solution)/shard_map/ppermute | solution.py:174
  32.1 19.4 %collective-permute-done.10.refs_2_ = bf16[16,4096]{1,0:T(8,128)(2,1)S(1)} collective-permute-done((bf16[16,4096]{1,0:T(8,128)(2,1)S(1)}, bf16[16,4096]{1,0:T(8,128)(2,1)S(1)}, u32[]{:S(2)}, u32[]{:S(2)}) %collective-permute-start.10) | collective-permute-done | bytes 131104 | tf_op jit(solution)/shard_map/ppermute | solution.py:174
  52.1 1.3 collective-permute-done.11.refs_3_
  53.4 3.9 %collective-permute-start.8 = (bf16[16,4096]{1,0:T(8,128)(2,1)}, bf16[16,4096]{1,0:T(8,128)(2,1)S(1)}, u32[]{:S(2)}, u32[]{:S(2)}) collective-permute-start(bf16[16,4096]{1,0:T(8,128)(2,1)} %get-tuple-element.61), channel_id=1, source_target_pairs={{0,24},{1,25},{2,26},{3,27},{4,28},{5,29},{6,30},{7,31},{8,16},{9,... | collective-permute-start | bytes 393224 | tf_op jit(solution)/shard_map/ppermute | solution.py:174
  57.3 2.2 collective-permute-done.12.refs_4_
  59.5 2.1 collective-permute-done.13.refs_5_
  61.6 3.5 %collective-permute-done.14.refs_6_ = bf16[16,4096]{1,0:T(8,128)(2,1)S(1)} collective-permute-done((bf16[16,4096]{1,0:T(8,128)(2,1)S(1)}, bf16[16,4096]{1,0:T(8,128)(2,1)S(1)}, u32[]{:S(2)}, u32[]{:S(2)}) %collective-permute-start.14) | collective-permute-done | bytes 131104 | tf_op jit(solution)/shard_map/ppermute | solution.py:174
  65.1 1.9 collective-permute-done.15.refs_7_
  67.0 13.6 %collective-permute-start.2 = (bf16[16,4096]{1,0:T(8,128)(2,1)}, bf16[16,4096]{1,0:T(8,128)(2,1)S(1)}, u32[]{:S(2)}, u32[]{:S(2)}) collective-permute-start(bf16[16,4096]{1,0:T(8,128)(2,1)} %get-tuple-element.47), channel_id=1, source_target_pairs={{0,18},{1,19},{2,16},{3,17},{4,22},{5,23},{6,20},{7,21},{8,26},{9,... | collective-permute-start | bytes 393224 | tf_op jit(solution)/shard_map/ppermute | solution.py:174
  80.5 28.7 %expert_piece.3 = bf16[256,2048]{1,0:T(8,128)(2,1)} custom-call(bf16[256,4096]{1,0:T(8,128)(2,1)S(1)} %bitcast.24, bf16[1,2048,4096]{2,1,0:T(8,128)(2,1)} %refs_8_.3, bf16[1,2048,4096]{2,1,0:T(8,128)(2,1)} %refs_9_.3, bf16[1,4096,2048]{2,1,0:T(8,128)(2,1)} %refs_10_.3), custom_call_target="tpu_custom_call" | custom-call | flops 21474836480 | bytes 53477376 | tf_op jit(solution)/shard_map/expert_piece/pallas_call | solution.py:63
  109.3 3.8 %all-to-all-start.1 = ((bf16[16,16,2048]{2,1,0:T(8,128)(2,1)}), bf16[16,16,2048]{2,1,0:T(8,128)(2,1)S(1)}, u32[]{:S(2)}, u32[]{:S(2)}) async-start(bf16[16,16,2048]{2,1,0:T(8,128)(2,1)} %bitcast.13), calls=%async_computation.1 | async-start | bytes 2097152 | tf_op jit(solution)/shard_map/all_to_all | solution.py:177
  113.1 1.3 collective-permute-start.3
  114.5 3.4 %collective-permute-start.4 = (bf16[16,4096]{1,0:T(8,128)(2,1)}, bf16[16,4096]{1,0:T(8,128)(2,1)S(1)}, u32[]{:S(2)}, u32[]{:S(2)}) collective-permute-start(bf16[16,4096]{1,0:T(8,128)(2,1)} %copy-done.7), channel_id=1, source_target_pairs={{0,20},{1,21},{2,22},{3,23},{4,16},{5,17},{6,18},{7,19},{8,28},{9,... | collective-permute-start | bytes 393224 | tf_op jit(solution)/shard_map/ppermute | solution.py:174
  118.0 3.4 %collective-permute-start.6 = (bf16[16,4096]{1,0:T(8,128)(2,1)}, bf16[16,4096]{1,0:T(8,128)(2,1)S(1)}, u32[]{:S(2)}, u32[]{:S(2)}) collective-permute-start(bf16[16,4096]{1,0:T(8,128)(2,1)} %copy-done.5), channel_id=1, source_target_pairs={{0,22},{1,23},{2,20},{3,21},{4,18},{5,19},{6,16},{7,17},{8,30},{9,... | collective-permute-start | bytes 393224 | tf_op jit(solution)/shard_map/ppermute | solution.py:174
  121.4 1.1 collective-permute-start.7
  122.5 26.6 %expert_piece.5 = (bf16[16,2048]{1,0:T(8,128)(2,1)S(1)}, bf16[16,2048]{1,0:T(8,128)(2,1)S(1)}, bf16[16,2048]{1,0:T(8,128)(2,1)S(1)}, bf16[16,2048]{1,0:T(8,128)(...) custom-call(bf16[16,4096]{1,0:T(8,128)(2,1)S(1)} %collective-permute, ...), custom_call_target="tpu_custom_call" | custom-call | flops 10737418240 | bytes 51904512 | tf_op jit(solution)/shard_map/expert_piece/pallas_call | solution.py:63
  149.1 3.5 %collective-permute-start.24 = (bf16[16,2048]{1,0:T(8,128)(2,1)S(1)}, bf16[16,2048]{1,0:T(8,128)(2,1)S(1)}, u32[]{:S(2)}, u32[]{:S(2)}) collective-permute-start(bf16[16,2048]{1,0:T(8,128)(2,1)S(1)} %get-tuple-element.77), channel_id=1, source_target_pairs={{0,24},{1,25},{2,26},{3,27},{4,28},{5,29},{6,30},{7,31},{8,16},{9,... | collective-permute-start | bytes 196616 | tf_op jit(solution)/shard_map/ppermute | solution.py:174
  152.7 3.4 %collective-permute-start.26 = (bf16[16,2048]{1,0:T(8,128)(2,1)S(1)}, bf16[16,2048]{1,0:T(8,128)(2,1)S(1)}, u32[]{:S(2)}, u32[]{:S(2)}) collective-permute-start(bf16[16,2048]{1,0:T(8,128)(2,1)S(1)} %get-tuple-element.79), channel_id=1, source_target_pairs={{0,26},{1,27},{2,24},{3,25},{4,30},{5,31},{6,28},{7,29},{8,18},{9,... | collective-permute-start | bytes 196616 | tf_op jit(solution)/shard_map/ppermute | solution.py:174
  156.1 25.8 %expert_piece.4 = (bf16[16,2048]{1,0:T(8,128)(2,1)S(1)}, bf16[16,2048]{1,0:T(8,128)(2,1)S(1)}, bf16[16,2048]{1,0:T(8,128)(2,1)S(1)}, bf16[16,2048]{1,0:T(8,128)(...) custom-call(bf16[16,4096]{1,0:T(8,128)(2,1)S(1)} %collective-permute, ...), custom_call_target="tpu_custom_call" | custom-call | flops 10737418240 | bytes 51904512 | tf_op jit(solution)/shard_map/expert_piece/pallas_call | solution.py:63
  182.0 2.4 %collective-permute-start.17 = (bf16[16,2048]{1,0:T(8,128)(2,1)S(1)}, bf16[16,2048]{1,0:T(8,128)(2,1)S(1)}, u32[]{:S(2)}, u32[]{:S(2)}) collective-permute-start(bf16[16,2048]{1,0:T(8,128)(2,1)S(1)} %get-tuple-element.70), channel_id=1, source_target_pairs={{0,17},{1,16},{2,19},{3,18},{4,21},{5,20},{6,23},{7,22},{8,25},{9,... | collective-permute-start | bytes 196616 | tf_op jit(solution)/shard_map/ppermute | solution.py:174
  184.4 1.4 collective-permute-start.18
  185.9 2.4 %collective-permute-start.19 = (bf16[16,2048]{1,0:T(8,128)(2,1)S(1)}, bf16[16,2048]{1,0:T(8,128)(2,1)S(1)}, u32[]{:S(2)}, u32[]{:S(2)}) collective-permute-start(bf16[16,2048]{1,0:T(8,128)(2,1)S(1)} %get-tuple-element.72), channel_id=1, source_target_pairs={{0,19},{1,18},{2,17},{3,16},{4,23},{5,22},{6,21},{7,20},{8,27},{9,... | collective-permute-start | bytes 196616 | tf_op jit(solution)/shard_map/ppermute | solution.py:174
  188.2 1.3 collective-permute-start.20
  189.5 3.9 %collective-permute-done.16.refs_2_ = bf16[16,2048]{1,0:T(8,128)(2,1)S(1)} collective-permute-done((bf16[16,2048]{1,0:T(8,128)(2,1)S(1)}, bf16[16,2048]{1,0:T(8,128)(2,1)S(1)}, u32[]{:S(2)}, u32[]{:S(2)}) %collective-permute-start.16) | collective-permute-done | bytes 65568 | tf_op jit(solution)/shard_map/ppermute | solution.py:174
  193.4 4.2 %collective-permute-start.22 = (bf16[16,2048]{1,0:T(8,128)(2,1)S(1)}, bf16[16,2048]{1,0:T(8,128)(2,1)S(1)}, u32[]{:S(2)}, u32[]{:S(2)}) collective-permute-start(bf16[16,2048]{1,0:T(8,128)(2,1)S(1)} %get-tuple-element.75), channel_id=1, source_target_pairs={{0,22},{1,23},{2,20},{3,21},{4,18},{5,19},{6,16},{7,17},{8,30},{9,... | collective-permute-start | bytes 196616 | tf_op jit(solution)/shard_map/ppermute | solution.py:174
  197.6 2.3 %collective-permute-done.18.refs_4_ = bf16[16,2048]{1,0:T(8,128)(2,1)S(1)} collective-permute-done((bf16[16,2048]{1,0:T(8,128)(2,1)S(1)}, bf16[16,2048]{1,0:T(8,128)(2,1)S(1)}, u32[]{:S(2)}, u32[]{:S(2)}) %collective-permute-start.18) | collective-permute-done | bytes 65568 | tf_op jit(solution)/shard_map/ppermute | solution.py:174
  200.4 0.9 collective-permute-start.27
  201.3 2.8 %collective-permute-done.20.refs_6_ = bf16[16,2048]{1,0:T(8,128)(2,1)S(1)} collective-permute-done((bf16[16,2048]{1,0:T(8,128)(2,1)S(1)}, bf16[16,2048]{1,0:T(8,128)(2,1)S(1)}, u32[]{:S(2)}, u32[]{:S(2)}) %collective-permute-start.20) | collective-permute-done | bytes 65568 | tf_op jit(solution)/shard_map/ppermute | solution.py:174
  204.1 2.0 collective-permute-start.28
  206.2 0.7 collective-permute-start.29
  206.9 3.2 %collective-permute-done.22.refs_8_ = bf16[16,2048]{1,0:T(8,128)(2,1)S(1)} collective-permute-done((bf16[16,2048]{1,0:T(8,128)(2,1)S(1)}, bf16[16,2048]{1,0:T(8,128)(2,1)S(1)}, u32[]{:S(2)}, u32[]{:S(2)}) %collective-permute-start.22) | collective-permute-done | bytes 65568 | tf_op jit(solution)/shard_map/ppermute | solution.py:174
  210.1 1.1 collective-permute-start.30
  211.1 2.8 %collective-permute-start.31 = (bf16[16,2048]{1,0:T(8,128)(2,1)}, bf16[16,2048]{1,0:T(8,128)(2,1)S(1)}, u32[]{:S(2)}, u32[]{:S(2)}) collective-permute-start(bf16[16,2048]{1,0:T(8,128)(2,1)} %get-tuple-element.84), channel_id=1, source_target_pairs={{0,31},{1,30},{2,29},{3,28},{4,27},{5,26},{6,25},{7,24},{8,23},{9,... | collective-permute-start | bytes 196616 | tf_op jit(solution)/shard_map/ppermute | solution.py:174
  215.2 3.4 %collective-permute-done.30.refs_8_ = bf16[16,2048]{1,0:T(8,128)(2,1)S(1)} collective-permute-done((bf16[16,2048]{1,0:T(8,128)(2,1)}, bf16[16,2048]{1,0:T(8,128)(2,1)S(1)}, u32[]{:S(2)}, u32[]{:S(2)}) %collective-permute-start.30) | collective-permute-done | bytes 65568 | tf_op jit(solution)/shard_map/ppermute | solution.py:174
  218.5 0.6 collective-permute-done.31.refs_9_
  219.2 1.4 unpack_blocks.5
  (62 shorter events, 3.3 us)
Async XLA Ops:
  2.0 1.2 copy-start
  3.2 1.2 copy-start.2
  6.5 74.0 %all-to-all-start = ((bf16[16,16,4096]{2,1,0:T(8,128)(2,1)}), bf16[16,16,4096]{2,1,0:T(8,128)(2,1)S(1)}, u32[]{:S(2)}, u32[]{:S(2)}) async-start(bf16[16,16,4096]{2,1,0:T(8,128)(2,1)} %bitcast.11), calls=%async_computation | async-start | bytes 4194304 | tf_op jit(solution)/shard_map/all_to_all | solution.py:177
  12.8 1.2 copy-start.1
  14.0 1.2 copy-start.3
  16.7 0.7 copy-start.8
  17.4 49.6 %copy-start.4 = (bf16[16,4096]{1,0:T(8,128)(2,1)}, bf16[16,4096]{1,0:T(8,128)(2,1)S(1)}, u32[]{:S(2)}) copy-start(bf16[16,4096]{1,0:T(8,128)(2,1)S(1)} %get-tuple-element.52) | copy-start | bytes 393220
  17.4 49.6 %copy-start.5 = (bf16[16,4096]{1,0:T(8,128)(2,1)}, bf16[16,4096]{1,0:T(8,128)(2,1)S(1)}, u32[]{:S(2)}) copy-start(bf16[16,4096]{1,0:T(8,128)(2,1)S(1)} %get-tuple-element.51) | copy-start | bytes 393220
  17.4 49.6 %copy-start.6 = (bf16[16,4096]{1,0:T(8,128)(2,1)}, bf16[16,4096]{1,0:T(8,128)(2,1)S(1)}, u32[]{:S(2)}) copy-start(bf16[16,4096]{1,0:T(8,128)(2,1)S(1)} %get-tuple-element.50) | copy-start | bytes 393220
  17.4 49.6 %copy-start.7 = (bf16[16,4096]{1,0:T(8,128)(2,1)}, bf16[16,4096]{1,0:T(8,128)(2,1)S(1)}, u32[]{:S(2)}) copy-start(bf16[16,4096]{1,0:T(8,128)(2,1)S(1)} %get-tuple-element.49) | copy-start | bytes 393220
  17.4 34.1 %collective-permute-start.10 = (bf16[16,4096]{1,0:T(8,128)(2,1)S(1)}, bf16[16,4096]{1,0:T(8,128)(2,1)S(1)}, u32[]{:S(2)}, u32[]{:S(2)}) collective-permute-start(bf16[16,4096]{1,0:T(8,128)(2,1)S(1)} %get-tuple-element.63), channel_id=1, source_target_pairs={{0,26},{1,27},{2,24},{3,25},{4,30},{5,31},{6,28},{7,29},{8,18},{9,... | collective-permute-start | bytes 393224 | tf_op jit(solution)/shard_map/ppermute | solution.py:174
  22.3 31.1 %collective-permute-start.11 = (bf16[16,4096]{1,0:T(8,128)(2,1)S(1)}, bf16[16,4096]{1,0:T(8,128)(2,1)S(1)}, u32[]{:S(2)}, u32[]{:S(2)}) collective-permute-start(bf16[16,4096]{1,0:T(8,128)(2,1)S(1)} %get-tuple-element.64), channel_id=1, source_target_pairs={{0,27},{1,26},{2,25},{3,24},{4,31},{5,30},{6,29},{7,28},{8,19},{9,... | collective-permute-start | bytes 393224 | tf_op jit(solution)/shard_map/ppermute | solution.py:174
  22.3 37.2 %collective-permute-start.12 = (bf16[16,4096]{1,0:T(8,128)(2,1)S(1)}, bf16[16,4096]{1,0:T(8,128)(2,1)S(1)}, u32[]{:S(2)}, u32[]{:S(2)}) collective-permute-start(bf16[16,4096]{1,0:T(8,128)(2,1)S(1)} %get-tuple-element.65), channel_id=1, source_target_pairs={{0,28},{1,29},{2,30},{3,31},{4,24},{5,25},{6,26},{7,27},{8,20},{9,... | collective-permute-start | bytes 393224 | tf_op jit(solution)/shard_map/ppermute | solution.py:174
  26.5 35.1 %collective-permute-start.13 = (bf16[16,4096]{1,0:T(8,128)(2,1)S(1)}, bf16[16,4096]{1,0:T(8,128)(2,1)S(1)}, u32[]{:S(2)}, u32[]{:S(2)}) collective-permute-start(bf16[16,4096]{1,0:T(8,128)(2,1)S(1)} %get-tuple-element.66), channel_id=1, source_target_pairs={{0,29},{1,28},{2,31},{3,30},{4,25},{5,24},{6,27},{7,26},{8,21},{9,... | collective-permute-start | bytes 393224 | tf_op jit(solution)/shard_map/ppermute | solution.py:174
  26.8 38.3 %collective-permute-start.14 = (bf16[16,4096]{1,0:T(8,128)(2,1)S(1)}, bf16[16,4096]{1,0:T(8,128)(2,1)S(1)}, u32[]{:S(2)}, u32[]{:S(2)}) collective-permute-start(bf16[16,4096]{1,0:T(8,128)(2,1)S(1)} %get-tuple-element.67), channel_id=1, source_target_pairs={{0,30},{1,31},{2,28},{3,29},{4,26},{5,27},{6,24},{7,25},{8,22},{9,... | collective-permute-start | bytes 393224 | tf_op jit(solution)/shard_map/ppermute | solution.py:174
  51.6 15.4 %collective-permute-start.15 = (bf16[16,4096]{1,0:T(8,128)(2,1)S(1)}, bf16[16,4096]{1,0:T(8,128)(2,1)S(1)}, u32[]{:S(2)}, u32[]{:S(2)}) collective-permute-start(bf16[16,4096]{1,0:T(8,128)(2,1)S(1)} %get-tuple-element.68), channel_id=1, source_target_pairs={{0,31},{1,30},{2,29},{3,28},{4,27},{5,26},{6,25},{7,24},{8,23},{9,... | collective-permute-start | bytes 393224 | tf_op jit(solution)/shard_map/ppermute | solution.py:174
  53.4 59.7 %collective-permute-start.8 = (bf16[16,4096]{1,0:T(8,128)(2,1)}, bf16[16,4096]{1,0:T(8,128)(2,1)S(1)}, u32[]{:S(2)}, u32[]{:S(2)}) collective-permute-start(bf16[16,4096]{1,0:T(8,128)(2,1)} %get-tuple-element.61), channel_id=1, source_target_pairs={{0,24},{1,25},{2,26},{3,27},{4,28},{5,29},{6,30},{7,31},{8,16},{9,... | collective-permute-start | bytes 393224 | tf_op jit(solution)/shard_map/ppermute | solution.py:174
  59.5 55.0 %collective-permute-start.9 = (bf16[16,4096]{1,0:T(8,128)(2,1)}, bf16[16,4096]{1,0:T(8,128)(2,1)S(1)}, u32[]{:S(2)}, u32[]{:S(2)}) collective-permute-start(bf16[16,4096]{1,0:T(8,128)(2,1)} %get-tuple-element.62), channel_id=1, source_target_pairs={{0,25},{1,24},{2,27},{3,26},{4,29},{5,28},{6,31},{7,30},{8,17},{9,... | collective-permute-start | bytes 393224 | tf_op jit(solution)/shard_map/ppermute | solution.py:174
  61.6 56.3 %collective-permute-start = (bf16[16,4096]{1,0:T(8,128)(2,1)}, bf16[16,4096]{1,0:T(8,128)(2,1)S(1)}, u32[]{:S(2)}, u32[]{:S(2)}) collective-permute-start(bf16[16,4096]{1,0:T(8,128)(2,1)} %get-tuple-element.45), channel_id=1, source_target_pairs={{0,16},{1,17},{2,18},{3,19},{4,20},{5,21},{6,22},{7,23},{8,24},{9,... | collective-permute-start | bytes 393224 | tf_op jit(solution)/shard_map/ppermute | solution.py:174
  65.1 52.9 %collective-permute-start.1 = (bf16[16,4096]{1,0:T(8,128)(2,1)}, bf16[16,4096]{1,0:T(8,128)(2,1)S(1)}, u32[]{:S(2)}, u32[]{:S(2)}) collective-permute-start(bf16[16,4096]{1,0:T(8,128)(2,1)} %get-tuple-element.46), channel_id=1, source_target_pairs={{0,17},{1,16},{2,19},{3,18},{4,21},{5,20},{6,23},{7,22},{8,25},{9,... | collective-permute-start | bytes 393224 | tf_op jit(solution)/shard_map/ppermute | solution.py:174
  67.0 54.4 %collective-permute-start.2 = (bf16[16,4096]{1,0:T(8,128)(2,1)}, bf16[16,4096]{1,0:T(8,128)(2,1)S(1)}, u32[]{:S(2)}, u32[]{:S(2)}) collective-permute-start(bf16[16,4096]{1,0:T(8,128)(2,1)} %get-tuple-element.47), channel_id=1, source_target_pairs={{0,18},{1,19},{2,16},{3,17},{4,22},{5,23},{6,20},{7,21},{8,26},{9,... | collective-permute-start | bytes 393224 | tf_op jit(solution)/shard_map/ppermute | solution.py:174
  109.3 104.8 %all-to-all-start.1 = ((bf16[16,16,2048]{2,1,0:T(8,128)(2,1)}), bf16[16,16,2048]{2,1,0:T(8,128)(2,1)S(1)}, u32[]{:S(2)}, u32[]{:S(2)}) async-start(bf16[16,16,2048]{2,1,0:T(8,128)(2,1)} %bitcast.13), calls=%async_computation.1 | async-start | bytes 2097152 | tf_op jit(solution)/shard_map/all_to_all | solution.py:177
  113.1 36.0 %collective-permute-start.3 = (bf16[16,4096]{1,0:T(8,128)(2,1)}, bf16[16,4096]{1,0:T(8,128)(2,1)S(1)}, u32[]{:S(2)}, u32[]{:S(2)}) collective-permute-start(bf16[16,4096]{1,0:T(8,128)(2,1)} %copy-done.8), channel_id=1, source_target_pairs={{0,19},{1,18},{2,17},{3,16},{4,23},{5,22},{6,21},{7,20},{8,27},{9,... | collective-permute-start | bytes 393224 | tf_op jit(solution)/shard_map/ppermute | solution.py:174
  114.5 38.1 %collective-permute-start.4 = (bf16[16,4096]{1,0:T(8,128)(2,1)}, bf16[16,4096]{1,0:T(8,128)(2,1)S(1)}, u32[]{:S(2)}, u32[]{:S(2)}) collective-permute-start(bf16[16,4096]{1,0:T(8,128)(2,1)} %copy-done.7), channel_id=1, source_target_pairs={{0,20},{1,21},{2,22},{3,23},{4,16},{5,17},{6,18},{7,19},{8,28},{9,... | collective-permute-start | bytes 393224 | tf_op jit(solution)/shard_map/ppermute | solution.py:174
  117.9 34.8 %collective-permute-start.5 = (bf16[16,4096]{1,0:T(8,128)(2,1)}, bf16[16,4096]{1,0:T(8,128)(2,1)S(1)}, u32[]{:S(2)}, u32[]{:S(2)}) collective-permute-start(bf16[16,4096]{1,0:T(8,128)(2,1)} %copy-done.6), channel_id=1, source_target_pairs={{0,21},{1,20},{2,23},{3,22},{4,17},{5,16},{6,19},{7,18},{8,29},{9,... | collective-permute-start | bytes 393224 | tf_op jit(solution)/shard_map/ppermute | solution.py:174
  118.0 38.1 %collective-permute-start.6 = (bf16[16,4096]{1,0:T(8,128)(2,1)}, bf16[16,4096]{1,0:T(8,128)(2,1)S(1)}, u32[]{:S(2)}, u32[]{:S(2)}) collective-permute-start(bf16[16,4096]{1,0:T(8,128)(2,1)} %copy-done.5), channel_id=1, source_target_pairs={{0,22},{1,23},{2,20},{3,21},{4,18},{5,19},{6,16},{7,17},{8,30},{9,... | collective-permute-start | bytes 393224 | tf_op jit(solution)/shard_map/ppermute | solution.py:174
  121.4 34.7 %collective-permute-start.7 = (bf16[16,4096]{1,0:T(8,128)(2,1)}, bf16[16,4096]{1,0:T(8,128)(2,1)S(1)}, u32[]{:S(2)}, u32[]{:S(2)}) collective-permute-start(bf16[16,4096]{1,0:T(8,128)(2,1)} %copy-done.4), channel_id=1, source_target_pairs={{0,23},{1,22},{2,21},{3,20},{4,19},{5,18},{6,17},{7,16},{8,31},{9,... | collective-permute-start | bytes 393224 | tf_op jit(solution)/shard_map/ppermute | solution.py:174
  149.1 35.3 %collective-permute-start.24 = (bf16[16,2048]{1,0:T(8,128)(2,1)S(1)}, bf16[16,2048]{1,0:T(8,128)(2,1)S(1)}, u32[]{:S(2)}, u32[]{:S(2)}) collective-permute-start(bf16[16,2048]{1,0:T(8,128)(2,1)S(1)} %get-tuple-element.77), channel_id=1, source_target_pairs={{0,24},{1,25},{2,26},{3,27},{4,28},{5,29},{6,30},{7,31},{8,16},{9,... | collective-permute-start | bytes 196616 | tf_op jit(solution)/shard_map/ppermute | solution.py:174
  152.6 33.2 %collective-permute-start.25 = (bf16[16,2048]{1,0:T(8,128)(2,1)S(1)}, bf16[16,2048]{1,0:T(8,128)(2,1)S(1)}, u32[]{:S(2)}, u32[]{:S(2)}) collective-permute-start(bf16[16,2048]{1,0:T(8,128)(2,1)S(1)} %get-tuple-element.78), channel_id=1, source_target_pairs={{0,25},{1,24},{2,27},{3,26},{4,29},{5,28},{6,31},{7,30},{8,17},{9,... | collective-permute-start | bytes 196616 | tf_op jit(solution)/shard_map/ppermute | solution.py:174
  152.7 35.5 %collective-permute-start.26 = (bf16[16,2048]{1,0:T(8,128)(2,1)S(1)}, bf16[16,2048]{1,0:T(8,128)(2,1)S(1)}, u32[]{:S(2)}, u32[]{:S(2)}) collective-permute-start(bf16[16,2048]{1,0:T(8,128)(2,1)S(1)} %get-tuple-element.79), channel_id=1, source_target_pairs={{0,26},{1,27},{2,24},{3,25},{4,30},{5,31},{6,28},{7,29},{8,18},{9,... | collective-permute-start | bytes 196616 | tf_op jit(solution)/shard_map/ppermute | solution.py:174
  182.0 11.4 %collective-permute-start.16 = (bf16[16,2048]{1,0:T(8,128)(2,1)S(1)}, bf16[16,2048]{1,0:T(8,128)(2,1)S(1)}, u32[]{:S(2)}, u32[]{:S(2)}) collective-permute-start(bf16[16,2048]{1,0:T(8,128)(2,1)S(1)} %get-tuple-element.69), channel_id=1, source_target_pairs={{0,16},{1,17},{2,18},{3,19},{4,20},{5,21},{6,22},{7,23},{8,24},{9,... | collective-permute-start | bytes 196616 | tf_op jit(solution)/shard_map/ppermute | solution.py:174
  182.0 11.4 %collective-permute-start.17 = (bf16[16,2048]{1,0:T(8,128)(2,1)S(1)}, bf16[16,2048]{1,0:T(8,128)(2,1)S(1)}, u32[]{:S(2)}, u32[]{:S(2)}) collective-permute-start(bf16[16,2048]{1,0:T(8,128)(2,1)S(1)} %get-tuple-element.70), channel_id=1, source_target_pairs={{0,17},{1,16},{2,19},{3,18},{4,21},{5,20},{6,23},{7,22},{8,25},{9,... | collective-permute-start | bytes 196616 | tf_op jit(solution)/shard_map/ppermute | solution.py:174
  184.4 15.5 %collective-permute-start.18 = (bf16[16,2048]{1,0:T(8,128)(2,1)S(1)}, bf16[16,2048]{1,0:T(8,128)(2,1)S(1)}, u32[]{:S(2)}, u32[]{:S(2)}) collective-permute-start(bf16[16,2048]{1,0:T(8,128)(2,1)S(1)} %get-tuple-element.71), channel_id=1, source_target_pairs={{0,18},{1,19},{2,16},{3,17},{4,22},{5,23},{6,20},{7,21},{8,26},{9,... | collective-permute-start | bytes 196616 | tf_op jit(solution)/shard_map/ppermute | solution.py:174
  185.9 14.5 %collective-permute-start.19 = (bf16[16,2048]{1,0:T(8,128)(2,1)S(1)}, bf16[16,2048]{1,0:T(8,128)(2,1)S(1)}, u32[]{:S(2)}, u32[]{:S(2)}) collective-permute-start(bf16[16,2048]{1,0:T(8,128)(2,1)S(1)} %get-tuple-element.72), channel_id=1, source_target_pairs={{0,19},{1,18},{2,17},{3,16},{4,23},{5,22},{6,21},{7,20},{8,27},{9,... | collective-permute-start | bytes 196616 | tf_op jit(solution)/shard_map/ppermute | solution.py:174
  188.2 15.9 %collective-permute-start.20 = (bf16[16,2048]{1,0:T(8,128)(2,1)S(1)}, bf16[16,2048]{1,0:T(8,128)(2,1)S(1)}, u32[]{:S(2)}, u32[]{:S(2)}) collective-permute-start(bf16[16,2048]{1,0:T(8,128)(2,1)S(1)} %get-tuple-element.73), channel_id=1, source_target_pairs={{0,20},{1,21},{2,22},{3,23},{4,16},{5,17},{6,18},{7,19},{8,28},{9,... | collective-permute-start | bytes 196616 | tf_op jit(solution)/shard_map/ppermute | solution.py:174
  193.4 12.8 %collective-permute-start.21 = (bf16[16,2048]{1,0:T(8,128)(2,1)S(1)}, bf16[16,2048]{1,0:T(8,128)(2,1)S(1)}, u32[]{:S(2)}, u32[]{:S(2)}) collective-permute-start(bf16[16,2048]{1,0:T(8,128)(2,1)S(1)} %get-tuple-element.74), channel_id=1, source_target_pairs={{0,21},{1,20},{2,23},{3,22},{4,17},{5,16},{6,19},{7,18},{8,29},{9,... | collective-permute-start | bytes 196616 | tf_op jit(solution)/shard_map/ppermute | solution.py:174
  193.4 16.7 %collective-permute-start.22 = (bf16[16,2048]{1,0:T(8,128)(2,1)S(1)}, bf16[16,2048]{1,0:T(8,128)(2,1)S(1)}, u32[]{:S(2)}, u32[]{:S(2)}) collective-permute-start(bf16[16,2048]{1,0:T(8,128)(2,1)S(1)} %get-tuple-element.75), channel_id=1, source_target_pairs={{0,22},{1,23},{2,20},{3,21},{4,18},{5,19},{6,16},{7,17},{8,30},{9,... | collective-permute-start | bytes 196616 | tf_op jit(solution)/shard_map/ppermute | solution.py:174
  199.9 11.2 %collective-permute-start.23 = (bf16[16,2048]{1,0:T(8,128)(2,1)S(1)}, bf16[16,2048]{1,0:T(8,128)(2,1)S(1)}, u32[]{:S(2)}, u32[]{:S(2)}) collective-permute-start(bf16[16,2048]{1,0:T(8,128)(2,1)S(1)} %get-tuple-element.76), channel_id=1, source_target_pairs={{0,23},{1,22},{2,21},{3,20},{4,19},{5,18},{6,17},{7,16},{8,31},{9,... | collective-permute-start | bytes 196616 | tf_op jit(solution)/shard_map/ppermute | solution.py:174
  200.4 14.8 %collective-permute-start.27 = (bf16[16,2048]{1,0:T(8,128)(2,1)}, bf16[16,2048]{1,0:T(8,128)(2,1)S(1)}, u32[]{:S(2)}, u32[]{:S(2)}) collective-permute-start(bf16[16,2048]{1,0:T(8,128)(2,1)} %get-tuple-element.80), channel_id=1, source_target_pairs={{0,27},{1,26},{2,25},{3,24},{4,31},{5,30},{6,29},{7,28},{8,19},{9,... | collective-permute-start | bytes 196616 | tf_op jit(solution)/shard_map/ppermute | solution.py:174
  204.1 11.0 %collective-permute-start.28 = (bf16[16,2048]{1,0:T(8,128)(2,1)}, bf16[16,2048]{1,0:T(8,128)(2,1)S(1)}, u32[]{:S(2)}, u32[]{:S(2)}) collective-permute-start(bf16[16,2048]{1,0:T(8,128)(2,1)} %get-tuple-element.81), channel_id=1, source_target_pairs={{0,28},{1,29},{2,30},{3,31},{4,24},{5,25},{6,26},{7,27},{8,20},{9,... | collective-permute-start | bytes 196616 | tf_op jit(solution)/shard_map/ppermute | solution.py:174
  206.2 9.0 %collective-permute-start.29 = (bf16[16,2048]{1,0:T(8,128)(2,1)}, bf16[16,2048]{1,0:T(8,128)(2,1)S(1)}, u32[]{:S(2)}, u32[]{:S(2)}) collective-permute-start(bf16[16,2048]{1,0:T(8,128)(2,1)} %get-tuple-element.82), channel_id=1, source_target_pairs={{0,29},{1,28},{2,31},{3,30},{4,25},{5,24},{6,27},{7,26},{8,21},{9,... | collective-permute-start | bytes 196616 | tf_op jit(solution)/shard_map/ppermute | solution.py:174
  210.1 8.5 %collective-permute-start.30 = (bf16[16,2048]{1,0:T(8,128)(2,1)}, bf16[16,2048]{1,0:T(8,128)(2,1)S(1)}, u32[]{:S(2)}, u32[]{:S(2)}) collective-permute-start(bf16[16,2048]{1,0:T(8,128)(2,1)} %get-tuple-element.83), channel_id=1, source_target_pairs={{0,30},{1,31},{2,28},{3,29},{4,26},{5,27},{6,24},{7,25},{8,22},{9,... | collective-permute-start | bytes 196616 | tf_op jit(solution)/shard_map/ppermute | solution.py:174
  211.1 8.0 %collective-permute-start.31 = (bf16[16,2048]{1,0:T(8,128)(2,1)}, bf16[16,2048]{1,0:T(8,128)(2,1)S(1)}, u32[]{:S(2)}, u32[]{:S(2)}) collective-permute-start(bf16[16,2048]{1,0:T(8,128)(2,1)} %get-tuple-element.84), channel_id=1, source_target_pairs={{0,31},{1,30},{2,29},{3,28},{4,27},{5,26},{6,25},{7,24},{8,23},{9,... | collective-permute-start | bytes 196616 | tf_op jit(solution)/shard_map/ppermute | solution.py:174

commit v4 on v2

--- a/solution.py
+++ b/solution.py
@@ -32,24 +32,26 @@
     return partial_sum.astype(jnp.bfloat16)
 
 
-def expert_kernel(pair_ref, gate_ref, up_ref, down_ref, out_ref, total):
+def expert_kernel(pair_ref, gate_ref, up_ref, down_ref, out_ref, grads_t, total_t):
     width = out_ref.shape[1]
     step = pl.program_id(0)
 
     @pl.when(step == 0)
     def _():
-        total[...] = jnp.zeros_like(total)
+        grads_t[...] = pair_ref[:, width:].T
+        total_t[...] = jnp.zeros_like(total_t)
 
     gate, up = gate_ref[0], up_ref[0]
     rows = pair_ref[:, :width]
-    gate_pre, up_pre = dot(rows, gate, ((1,), (0,))), dot(rows, up, ((1,), (0,)))
-    hidden_grad = dot(pair_ref[:, width:], down_ref[0], ((1,), (1,)))
+    gate_pre = dot(rows, gate, ((1,), (0,))).T
+    up_pre = dot(rows, up, ((1,), (0,))).T
+    hidden_grad = dot(down_ref[0], grads_t[...], ((1,), (0,)))
     gate_grad, up_grad = hidden_grads(gate_pre, up_pre, hidden_grad)
-    total[...] += dot(gate_grad, gate, ((1,), (1,))) + dot(up_grad, up, ((1,), (1,)))
+    total_t[...] += dot(gate, gate_grad, ((1,), (0,))) + dot(up, up_grad, ((1,), (0,)))
 
     @pl.when(step == pl.num_programs(0) - 1)
     def _():
-        out_ref[...] = total[...].astype(out_ref.dtype)
+        out_ref[...] = total_t[...].T.astype(out_ref.dtype)
 
 
 def expert_piece(pair, gate_weight, up_weight, down_weight):
@@ -67,34 +69,112 @@
         ],
         out_specs=pl.BlockSpec((rows, width), lambda i: (0, 0)),
         out_shape=jax.ShapeDtypeStruct((rows, width), jnp.bfloat16),
-        scratch_shapes=[pltpu.VMEM((rows, width), jnp.float32)],
+        scratch_shapes=[
+            pltpu.VMEM((width, rows), jnp.bfloat16),
+            pltpu.VMEM((width, rows), jnp.float32),
+        ],
         compiler_params=pltpu.CompilerParams(vmem_limit_bytes=40 * MIB),
         cost_estimate=pl.CostEstimate(
             flops=10 * rows * width * hidden,
             bytes_accessed=6 * width * hidden + 6 * rows * width,
             transcendentals=rows * hidden,
         ),
+        name="expert_piece",
     )(pair, gate_weight, up_weight, down_weight)
 
 
-def pack_kernel(place_ref, rows_ref, grads_ref, out_ref):
+def place_rows(species, table, depth, pieces):
+    experts, rows = table.shape[1], species.shape[1]
+    ids = lax.broadcasted_iota(jnp.int32, (experts, rows), 0)
+    named = (ids == species).astype(jnp.bfloat16)
+    expert_ids = lax.broadcasted_iota(jnp.int32, (experts, experts), 0)
+    moved = (expert_ids == table).astype(jnp.bfloat16)
+    hits = dot(moved, named, ((1,), (0,)))
+    row_ids = lax.broadcasted_iota(jnp.int32, (rows, rows), 0)
+    column_ids = lax.broadcasted_iota(jnp.int32, (rows, rows), 1)
+    before = (row_ids < column_ids).astype(jnp.bfloat16)
+    earlier = dot(hits.astype(jnp.bfloat16), before, ((1,), (0,)))
+    slot = jnp.sum(earlier * hits, axis=0, keepdims=True).astype(jnp.int32)
+    expert = jnp.sum(ids.astype(jnp.float32) * hits, axis=0, keepdims=True).astype(jnp.int32)
+    found = []
+    for piece in range(pieces):
+        own = slot - piece * depth
+        found.append(jnp.where((own >= 0) & (own < depth), expert * depth + own, -1))
+    return found
+
+
+def select_rows(place, count):
+    ids = lax.broadcasted_iota(jnp.int32, (count, place.shape[1]), 0)
+    return (ids == place).astype(jnp.bfloat16)
+
+
+def first_kernel(
+    depth, species_ref, table_ref, rows_ref, grads_ref, place_ref, out_ref, held, packed, sems
+):
+    width, part = rows_ref.shape[1], held.shape[2]
+    parts = width // part
+    sources = [ref.at[:, c * part : (c + 1) * part] for ref in (rows_ref, grads_ref) for c in range(parts)]
+    arriving = [
+        pltpu.make_async_copy(source, held.at[i], sems.at[0, i]) for i, source in enumerate(sources)
+    ]
+    leaving = [
+        pltpu.make_async_copy(packed.at[i], out_ref.at[:, i * part : (i + 1) * part], sems.at[1, i])
+        for i in range(2 * parts)
+    ]
+    for copy in arriving:
+        copy.start()
+    place = place_rows(species_ref[...], table_ref[...], depth, place_ref.shape[0])
+    for piece, found in enumerate(place):
+        place_ref[piece : piece + 1, :] = found
+    select = select_rows(place[0], packed.shape[1])
+    for i in range(2 * parts):
+        arriving[i].wait()
+        packed[i] = dot(select, held[i], ((1,), (0,))).astype(packed.dtype)
+        leaving[i].start()
+    for copy in leaving:
+        copy.wait()
+
+
+def pack_first(species, expert_table, tokens, out_grads, depth, pieces):
+    (rows, width), experts = tokens.shape, expert_table.shape[0]
+    count, part = experts * depth, min(512, width)
+    copies = 2 * width // part
+    return pl.pallas_call(
+        functools.partial(first_kernel, depth),
+        in_specs=[pl.BlockSpec(memory_space=pltpu.VMEM)] * 2 + [pl.BlockSpec(memory_space=pl.ANY)] * 2,
+        out_specs=[pl.BlockSpec(memory_space=pltpu.VMEM), pl.BlockSpec(memory_space=pl.ANY)],
+        out_shape=[
+            jax.ShapeDtypeStruct((pieces, rows), jnp.int32),
+            jax.ShapeDtypeStruct((count, 2 * width), jnp.bfloat16),
+        ],
+        scratch_shapes=[
+            pltpu.VMEM((copies, rows, part), jnp.bfloat16),
+            pltpu.VMEM((copies, count, part), jnp.bfloat16),
+            pltpu.SemaphoreType.DMA((2, copies)),
+        ],
+        compiler_params=pltpu.CompilerParams(vmem_limit_bytes=60 * MIB),
+        name="pack_first",
+    )(species.reshape(1, rows), expert_table.reshape(1, experts), tokens, out_grads)
+
+
+def pack_kernel(piece, place_ref, rows_ref, grads_ref, out_ref):
     count, width = out_ref.shape[0], rows_ref.shape[1]
-    ids = lax.broadcasted_iota(jnp.int32, (count, place_ref.shape[1]), 0)
-    select = (ids == place_ref[...]).astype(jnp.bfloat16)
+    select = select_rows(place_ref[piece : piece + 1, :], count)
     out_ref[:, :width] = dot(select, rows_ref[...], ((1,), (0,))).astype(out_ref.dtype)
     out_ref[:, width:] = dot(select, grads_ref[...], ((1,), (0,))).astype(out_ref.dtype)
 
 
-def pack_pair(place, tokens, out_grads, count):
+def pack_pair(place, piece, tokens, out_grads, count):
     rows, width = tokens.shape
     return pl.pallas_call(
-        pack_kernel,
+        functools.partial(pack_kernel, piece),
         out_shape=jax.ShapeDtypeStruct((count, 2 * width), jnp.bfloat16),
         compiler_params=pltpu.CompilerParams(vmem_limit_bytes=24 * MIB),
         cost_estimate=pl.CostEstimate(
             flops=4 * count * rows * width, bytes_accessed=4 * (rows + count) * width, transcendentals=0
         ),
-    )(place[None, :], tokens, out_grads)
+        name="pack_pair",
+    )(place, tokens, out_grads)
 
 
 def places(species, expert_table, tensor_size):
@@ -116,15 +196,13 @@
     experts = expert_table.shape[0]
     depth = 2 * rows_dev // experts // PIECES
     count = experts * depth
-    expert_of, slot_of = places(species, expert_table, 1)
-    slot = slot_of[0][None, :] - depth * jnp.arange(PIECES, dtype=jnp.int32)[:, None]
-    place_of = jnp.where((slot >= 0) & (slot < depth), expert_of * depth + slot, -1)
+    place_of, packed = pack_first(species, expert_table, tokens, out_grads, depth, PIECES)
     exchange = functools.partial(
         lax.all_to_all, axis_name="expert", split_axis=0, concat_axis=0, tiled=True
     )
-    arrived = []
-    for piece in range(PIECES):
-        packed = pack_pair(place_of[piece], tokens, out_grads, count)
+    arrived = [exchange(packed.reshape(experts, depth, 2 * width))]
+    for piece in range(1, PIECES):
+        packed = pack_pair(place_of, piece, tokens, out_grads, count)
         arrived.append(exchange(packed.reshape(experts, depth, 2 * width)))
     own = None
     for piece in range(PIECES):

time: 183 us -> 190 us (1.038)
  Pallas kernels: 62.6 us -> 84.3 us
  waiting for transfers between devices: 90.3 us -> 81 us
  local copies, waits for them, and re-layouts: 2.87 us -> 0.03 us
    all_to_all x2 -> x1, waiting for transfers between devices: 65.8 us -> 9.74 us  [in_pieces(): arrived.append(exchange(packed.reshape(experts, depth, 2 * width)))]
    all_to_all x0 -> x1, waiting for transfers between devices: none -> 46.8 us  [in_pieces(): arrived = [exchange(packed.reshape(experts, depth, 2 * width))]]
    pallas_call x2, Pallas kernels: 58.5 us -> 77.2 us  [expert_piece(): pl.pallas_call(expert_kernel, grid=(hidden // tile,), in_specs=[pl.BlockS...]
    all_to_all x2 -> x1, starting transfers between devices: 11.4 us -> 4.01 us  [in_pieces(): arrived.append(exchange(packed.reshape(experts, depth, 2 * width)))]
    all_to_all x0 -> x1, starting transfers between devices: none -> 7.42 us  [in_pieces(): arrived = [exchange(packed.reshape(experts, depth, 2 * width))]]
    pallas_call x2, Pallas kernels: 4.05 us -> 7.01 us  [the longest x1 4.96 us: pack_first(): pl.pallas_call(functools.partial(first_kernel, depth), in_specs=[pl.Block...]
    unnamed x10 -> x8, local copies, waits for them, and re-layouts: 2.46 us -> 0.02 us
  transfers between devices with their start and end apart: 4 -> 4, of which waited for: 3 -> 3; matrix products, arithmetic and copies ran while one was open for 1% -> 1% of each run, Pallas kernels for 33% -> 42%
where the time goes in v4:
time: 190 us
  Pallas kernels  84.3 us (44%)
  waiting for transfers between devices  81 us (43%)
  starting transfers between devices  21.3 us (11%)
  matrix products  3.18 us (2%)
    pallas_call x2, Pallas kernels, expert_piece(): pl.pallas_call(expert_kernel, grid=(hidden // tile,), in_specs=[pl.BlockS...  77.2 us
    all_to_all x1, waiting for transfers between devices, in_pieces(): arrived = [exchange(packed.reshape(experts, depth, 2 * width))]  46.8 us
    all_to_all x2, waiting for transfers between devices, in_pieces(): exchange(partial_sum.reshape(experts, depth, width)).reshape(count, width)  24.5 us
    all_to_all x2, starting transfers between devices, in_pieces(): exchange(partial_sum.reshape(experts, depth, width)).reshape(count, width)  9.84 us
    all_to_all x1, waiting for transfers between devices, in_pieces(): arrived.append(exchange(packed.reshape(experts, depth, 2 * width)))  9.74 us
    all_to_all x1, starting transfers between devices, in_pieces(): arrived = [exchange(packed.reshape(experts, depth, 2 * width))]  7.42 us
    pallas_call x1, Pallas kernels, pack_first(): pl.pallas_call(functools.partial(first_kernel, depth), in_specs=[pl.Block...  4.96 us
    all_to_all x1, starting transfers between devices, in_pieces(): arrived.append(exchange(packed.reshape(experts, depth, 2 * width)))  4.01 us
  transfers between devices with their start and end apart: 4, of which 3 were waited for; matrix products, arithmetic and copies ran while one was open for 1% of the time, Pallas kernels for 42%

profile of v4, /device:TPU:0, one launch (start us, length us, event | category | flops | bytes accessed | tf_op | source)
XLA Modules:
  0.0 189.9 jit_solution(14160818191488546652)
XLA Ops:
  0.0 5.0 %pack_first.1 = (s32[2,256]{1,0:T(2,128)}, bf16[256,4096]{1,0:T(8,128)(2,1)}) custom-call(s32[1,256]{1,0:T(1,128)} %bitcast.20, s32[1,32]{1,0:T(1,128)} %bitcast.21, bf16[256,2048]{1,0:T(8,128)(2,1)} %rows_ref.3, bf16[256,2048]{1,0:T(8,128)(2,1)} %grads_ref.3), custom_call_target="tpu_custom_call" | custom-call | tf_op jit(solution)/shard_map/pack_first/pallas_call | solution.py:142
  5.0 0.0 copy-start
  5.0 0.0 copy-start.1
  5.0 0.0 copy-start.2
  5.0 7.4 %all-to-all-start = ((bf16[32,8,4096]{2,1,0:T(8,128)(2,1)}), bf16[32,8,4096]{2,1,0:T(8,128)(2,1)}, u32[]{:S(2)}, u32[]{:S(2)}) async-start(bf16[32,8,4096]{2,1,0:T(8,128)(2,1)} %bitcast.17), calls=%async_computation | async-start | bytes 4194304 | tf_op jit(solution)/shard_map/all_to_all | solution.py:203
  12.4 0.0 copy-done
  12.4 0.0 copy-done.1
  12.5 0.0 copy-done.2
  12.5 2.0 %pack_pair.1 = bf16[256,4096]{1,0:T(8,128)(2,1)} custom-call(s32[2,256]{1,0:T(2,128)S(1)} %copy-done.2, bf16[256,2048]{1,0:T(8,128)(2,1)S(1)} %copy-done, bf16[256,2048]{1,0:T(8,128)(2,1)S(1)} %copy-done.1), custom_call_target="tpu_custom_call" | custom-call | flops 536870912 | bytes 4194304 | tf_op jit(solution)/shard_map/pack_pair/pallas_call | solution.py:169
  14.5 46.8 %all-to-all-done = bf16[32,8,4096]{2,1,0:T(8,128)(2,1)} async-done(((bf16[32,8,4096]{2,1,0:T(8,128)(2,1)}), bf16[32,8,4096]{2,1,0:T(8,128)(2,1)}, u32[]{:S(2)}, u32[]{:S(2)}) %all-to-all-start) | async-done | bytes 2097184 | tf_op jit(solution)/shard_map/all_to_all | solution.py:203
  61.3 4.0 %all-to-all-start.2 = ((bf16[32,8,4096]{2,1,0:T(8,128)(2,1)}), bf16[32,8,4096]{2,1,0:T(8,128)(2,1)S(1)}, u32[]{:S(2)}, u32[]{:S(2)}) async-start(bf16[32,8,4096]{2,1,0:T(8,128)(2,1)} %bitcast.8), calls=%async_computation.2 | async-start | bytes 4194304 | tf_op jit(solution)/shard_map/all_to_all | solution.py:206
  65.3 39.2 %expert_piece.2 = bf16[256,2048]{1,0:T(8,128)(2,1)} custom-call(bf16[256,4096]{1,0:T(8,128)(2,1)} %bitcast.4.pair_ref, bf16[1,2048,4096]{2,1,0:T(8,128)(2,1)} %gate_ref.3, bf16[1,2048,4096]{2,1,0:T(8,128)(2,1)} %up_ref.3, bf16[1,4096,2048]{2,1,0:T(8,128)(2,1)} %down_ref.3), custom_call_target="tpu_custom_call" | custom-call | flops 21474836480 | bytes 53477376 | tf_op jit(solution)/shard_map/expert_piece/pallas_call | solution.py:61
  104.5 9.7 %all-to-all-done.2 = bf16[32,8,4096]{2,1,0:T(8,128)(2,1)S(1)} async-done(((bf16[32,8,4096]{2,1,0:T(8,128)(2,1)}), bf16[32,8,4096]{2,1,0:T(8,128)(2,1)S(1)}, u32[]{:S(2)}, u32[]{:S(2)}) %all-to-all-start.2) | async-done | bytes 2097184 | tf_op jit(solution)/shard_map/all_to_all | solution.py:206
  114.2 4.0 %all-to-all-start.1 = ((bf16[32,8,2048]{2,1,0:T(8,128)(2,1)}), bf16[32,8,2048]{2,1,0:T(8,128)(2,1)S(1)}, u32[]{:S(2)}, u32[]{:S(2)}) async-start(bf16[32,8,2048]{2,1,0:T(8,128)(2,1)} %bitcast.5), calls=%async_computation.1 | async-start | bytes 2097152 | tf_op jit(solution)/shard_map/all_to_all | solution.py:211
  118.2 38.1 %expert_piece.3 = bf16[256,2048]{1,0:T(8,128)(2,1)} custom-call(bf16[256,4096]{1,0:T(8,128)(2,1)S(1)} %bitcast.16, bf16[1,2048,4096]{2,1,0:T(8,128)(2,1)} %gate_ref.3, bf16[1,2048,4096]{2,1,0:T(8,128)(2,1)} %up_ref.3, bf16[1,4096,2048]{2,1,0:T(8,128)(2,1)} %down_ref.3), custom_call_target="tpu_custom_call" | custom-call | flops 21474836480 | bytes 53477376 | tf_op jit(solution)/shard_map/expert_piece/pallas_call | solution.py:61
  156.3 0.0 all-to-all-done.1
  156.3 0.0 copy-start.3
  156.3 5.8 %all-to-all-start.3 = ((bf16[32,8,2048]{2,1,0:T(8,128)(2,1)}), bf16[32,8,2048]{2,1,0:T(8,128)(2,1)S(1)}, u32[]{:S(2)}, u32[]{:S(2)}) async-start(bf16[32,8,2048]{2,1,0:T(8,128)(2,1)} %bitcast.10), calls=%async_computation.3 | async-start | bytes 2097152 | tf_op jit(solution)/shard_map/all_to_all | solution.py:211
  162.2 0.0 copy-done.3
  162.2 1.7 fusion.2
  163.9 24.5 %all-to-all-done.3 = bf16[32,8,2048]{2,1,0:T(8,128)(2,1)S(1)} async-done(((bf16[32,8,2048]{2,1,0:T(8,128)(2,1)}), bf16[32,8,2048]{2,1,0:T(8,128)(2,1)S(1)}, u32[]{:S(2)}, u32[]{:S(2)}) %all-to-all-start.3) | async-done | bytes 1048608 | tf_op jit(solution)/shard_map/all_to_all | solution.py:211
  188.4 1.5 fusion
  (1 shorter events, 0.0 us)
Async XLA Ops:
  5.0 7.5 %copy-start = (bf16[256,2048]{1,0:T(8,128)(2,1)S(1)}, bf16[256,2048]{1,0:T(8,128)(2,1)}, u32[]{:S(2)}) copy-start(bf16[256,2048]{1,0:T(8,128)(2,1)} %rows_ref.3) | copy-start | bytes 3145732
  5.0 7.5 %copy-start.1 = (bf16[256,2048]{1,0:T(8,128)(2,1)S(1)}, bf16[256,2048]{1,0:T(8,128)(2,1)}, u32[]{:S(2)}) copy-start(bf16[256,2048]{1,0:T(8,128)(2,1)} %grads_ref.3) | copy-start | bytes 3145732
  5.0 7.5 %copy-start.2 = (s32[2,256]{1,0:T(2,128)S(1)}, s32[2,256]{1,0:T(2,128)}, u32[]{:S(2)}) copy-start(s32[2,256]{1,0:T(2,128)} %get-tuple-element.7.place_ref) | copy-start | bytes 6148
  5.0 56.3 %all-to-all-start = ((bf16[32,8,4096]{2,1,0:T(8,128)(2,1)}), bf16[32,8,4096]{2,1,0:T(8,128)(2,1)}, u32[]{:S(2)}, u32[]{:S(2)}) async-start(bf16[32,8,4096]{2,1,0:T(8,128)(2,1)} %bitcast.17), calls=%async_computation | async-start | bytes 4194304 | tf_op jit(solution)/shard_map/all_to_all | solution.py:203
  61.3 52.9 %all-to-all-start.2 = ((bf16[32,8,4096]{2,1,0:T(8,128)(2,1)}), bf16[32,8,4096]{2,1,0:T(8,128)(2,1)S(1)}, u32[]{:S(2)}, u32[]{:S(2)}) async-start(bf16[32,8,4096]{2,1,0:T(8,128)(2,1)} %bitcast.8), calls=%async_computation.2 | async-start | bytes 4194304 | tf_op jit(solution)/shard_map/all_to_all | solution.py:206
  114.2 42.1 %all-to-all-start.1 = ((bf16[32,8,2048]{2,1,0:T(8,128)(2,1)}), bf16[32,8,2048]{2,1,0:T(8,128)(2,1)S(1)}, u32[]{:S(2)}, u32[]{:S(2)}) async-start(bf16[32,8,2048]{2,1,0:T(8,128)(2,1)} %bitcast.5), calls=%async_computation.1 | async-start | bytes 2097152 | tf_op jit(solution)/shard_map/all_to_all | solution.py:211
  156.3 5.9 %copy-start.3 = (bf16[32,8,2048]{2,1,0:T(8,128)(2,1)}, bf16[32,8,2048]{2,1,0:T(8,128)(2,1)S(1)}, u32[]{:S(2)}) copy-start(bf16[32,8,2048]{2,1,0:T(8,128)(2,1)S(1)} %all-to-all-done.1) | copy-start | bytes 3145732
  156.3 32.1 %all-to-all-start.3 = ((bf16[32,8,2048]{2,1,0:T(8,128)(2,1)}), bf16[32,8,2048]{2,1,0:T(8,128)(2,1)S(1)}, u32[]{:S(2)}, u32[]{:S(2)}) async-start(bf16[32,8,2048]{2,1,0:T(8,128)(2,1)} %bitcast.10), calls=%async_computation.3 | async-start | bytes 2097152 | tf_op jit(solution)/shard_map/all_to_all | solution.py:211

commit v5 on v4

--- a/solution.py
+++ b/solution.py
@@ -32,26 +32,56 @@
     return partial_sum.astype(jnp.bfloat16)
 
 
-def expert_kernel(pair_ref, gate_ref, up_ref, down_ref, out_ref, grads_t, total_t):
-    width = out_ref.shape[1]
-    step = pl.program_id(0)
-
-    @pl.when(step == 0)
-    def _():
-        grads_t[...] = pair_ref[:, width:].T
-        total_t[...] = jnp.zeros_like(total_t)
-
-    gate, up = gate_ref[0], up_ref[0]
-    rows = pair_ref[:, :width]
-    gate_pre = dot(rows, gate, ((1,), (0,))).T
-    up_pre = dot(rows, up, ((1,), (0,))).T
-    hidden_grad = dot(down_ref[0], grads_t[...], ((1,), (0,)))
-    gate_grad, up_grad = hidden_grads(gate_pre, up_pre, hidden_grad)
-    total_t[...] += dot(gate, gate_grad, ((1,), (0,))) + dot(up, up_grad, ((1,), (0,)))
-
-    @pl.when(step == pl.num_programs(0) - 1)
-    def _():
-        out_ref[...] = total_t[...].T.astype(out_ref.dtype)
+def expert_kernel(
+    pair_ref, gate_ref, up_ref, down_ref, out_ref, wide, tall, both, total, sems
+):
+    width, tile = out_ref.shape[1], tall.shape[1]
+    steps = gate_ref.shape[2] // tile
+    half, strip = min(256, tile), min(512, width)
+
+    def copies(step, slot):
+        part = pl.ds(pl.multiple_of(step * tile, tile), tile)
+        return [
+            pltpu.make_async_copy(source, target, sems.at[slot, i])
+            for i, (source, target) in enumerate(
+                (
+                    (gate_ref.at[0, :, part], wide.at[slot, :, :tile]),
+                    (up_ref.at[0, :, part], wide.at[slot, :, tile:]),
+                    (down_ref.at[0, part, :], tall.at[slot]),
+                )
+            )
+        ]
+
+    for copy in copies(0, 0):
+        copy.start()
+    total[...] = jnp.zeros_like(total)
+
+    def body(step, carry):
+        slot = lax.rem(step, 2)
+
+        @pl.when(step + 1 < steps)
+        def _():
+            for copy in copies(step + 1, 1 - slot):
+                copy.start()
+
+        for copy in copies(step, slot):
+            copy.wait()
+        rows, grads = pair_ref[:, :width], pair_ref[:, width:]
+        for low in range(0, tile, half):
+            high = low + half
+            gate_pre = dot(rows, wide[slot, :, low:high], ((1,), (0,)))
+            up_pre = dot(rows, wide[slot, :, tile + low : tile + high], ((1,), (0,)))
+            hidden_grad = dot(grads, tall[slot, low:high, :], ((1,), (1,)))
+            gate_grad, up_grad = hidden_grads(gate_pre, up_pre, hidden_grad)
+            both[:, low:high] = gate_grad
+            both[:, tile + low : tile + high] = up_grad
+        for low in range(0, width, strip):
+            high = low + strip
+            total[:, low:high] += dot(both[...], wide[slot, low:high, :], ((1,), (1,)))
+        return carry
+
+    lax.fori_loop(0, steps, body, 0)
+    out_ref[...] = total[...].astype(out_ref.dtype)
 
 
 def expert_piece(pair, gate_weight, up_weight, down_weight):
@@ -60,18 +90,15 @@
     tile = min(512, hidden)
     return pl.pallas_call(
         expert_kernel,
-        grid=(hidden // tile,),
-        in_specs=[
-            pl.BlockSpec((rows, 2 * width), lambda i: (0, 0)),
-            pl.BlockSpec((1, width, tile), lambda i: (0, 0, i)),
-            pl.BlockSpec((1, width, tile), lambda i: (0, 0, i)),
-            pl.BlockSpec((1, tile, width), lambda i: (0, i, 0)),
-        ],
-        out_specs=pl.BlockSpec((rows, width), lambda i: (0, 0)),
+        in_specs=[pl.BlockSpec(memory_space=pltpu.VMEM)] + [pl.BlockSpec(memory_space=pl.ANY)] * 3,
+        out_specs=pl.BlockSpec(memory_space=pltpu.VMEM),
         out_shape=jax.ShapeDtypeStruct((rows, width), jnp.bfloat16),
         scratch_shapes=[
-            pltpu.VMEM((width, rows), jnp.bfloat16),
-            pltpu.VMEM((width, rows), jnp.float32),
+            pltpu.VMEM((2, width, 2 * tile), jnp.bfloat16),
+            pltpu.VMEM((2, tile, width), jnp.bfloat16),
+            pltpu.VMEM((rows, 2 * tile), jnp.bfloat16),
+            pltpu.VMEM((rows, width), jnp.float32),
+            pltpu.SemaphoreType.DMA((2, 3)),
         ],
         compiler_params=pltpu.CompilerParams(vmem_limit_bytes=40 * MIB),
         cost_estimate=pl.CostEstimate(

time: 190 us -> 181 us (0.953)
  Pallas kernels: 84.3 us -> 65.9 us
  waiting for transfers between devices: 81 us -> 89.9 us
    pallas_call x2, Pallas kernels: 77.2 us -> 58.9 us  [expert_piece(): pl.pallas_call(expert_kernel, in_specs=[pl.BlockSpec(memory_space=pltpu.V...]
    all_to_all x1, waiting for transfers between devices: 9.74 us -> 18.6 us  [in_pieces(): arrived.append(exchange(packed.reshape(experts, depth, 2 * width)))]
  transfers between devices with their start and end apart: 4 -> 4, of which waited for: 3 -> 3; matrix products, arithmetic and copies ran while one was open for 1% -> 1% of each run, Pallas kernels for 42% -> 34%
where the time goes in v5:
time: 181 us; the launch traced here: 180 us
  waiting for transfers between devices  89.9 us (50%)
  Pallas kernels  65.9 us (36%)
  starting transfers between devices  21.3 us (12%)
  matrix products  3.18 us (2%)
    pallas_call x2, Pallas kernels, expert_piece(): pl.pallas_call(expert_kernel, in_specs=[pl.BlockSpec(memory_space=pltpu.V...  58.9 us
    all_to_all x1, waiting for transfers between devices, in_pieces(): arrived = [exchange(packed.reshape(experts, depth, 2 * width))]  46.8 us
    all_to_all x2, waiting for transfers between devices, in_pieces(): exchange(partial_sum.reshape(experts, depth, width)).reshape(count, width)  24.5 us
    all_to_all x1, waiting for transfers between devices, in_pieces(): arrived.append(exchange(packed.reshape(experts, depth, 2 * width)))  18.6 us
    all_to_all x2, starting transfers between devices, in_pieces(): exchange(partial_sum.reshape(experts, depth, width)).reshape(count, width)  9.85 us
    all_to_all x1, starting transfers between devices, in_pieces(): arrived = [exchange(packed.reshape(experts, depth, 2 * width))]  7.42 us
    pallas_call x1, Pallas kernels, pack_first(): pl.pallas_call(functools.partial(first_kernel, depth), in_specs=[pl.Block...  4.96 us
    all_to_all x1, starting transfers between devices, in_pieces(): arrived.append(exchange(packed.reshape(experts, depth, 2 * width)))  4.01 us
  transfers between devices with their start and end apart: 4, of which 3 were waited for; matrix products, arithmetic and copies ran while one was open for 1% of the time, Pallas kernels for 34%

profile of v5, /device:TPU:0, one launch (start us, length us, event | category | flops | bytes accessed | tf_op | source)
XLA Modules:
  0.0 180.4 jit_solution(16664821873605283015)
XLA Ops:
  0.0 5.0 %pack_first.1 = (s32[2,256]{1,0:T(2,128)}, bf16[256,4096]{1,0:T(8,128)(2,1)}) custom-call(s32[1,256]{1,0:T(1,128)} %bitcast.20, s32[1,32]{1,0:T(1,128)} %bitcast.21, bf16[256,2048]{1,0:T(8,128)(2,1)} %rows_ref.3, bf16[256,2048]{1,0:T(8,128)(2,1)} %grads_ref.3), custom_call_target="tpu_custom_call" | custom-call | tf_op jit(solution)/shard_map/pack_first/pallas_call | solution.py:169
  5.0 0.0 copy-start
  5.0 0.0 copy-start.1
  5.0 0.0 copy-start.2
  5.0 7.4 %all-to-all-start = ((bf16[32,8,4096]{2,1,0:T(8,128)(2,1)}), bf16[32,8,4096]{2,1,0:T(8,128)(2,1)}, u32[]{:S(2)}, u32[]{:S(2)}) async-start(bf16[32,8,4096]{2,1,0:T(8,128)(2,1)} %bitcast.17), calls=%async_computation | async-start | bytes 4194304 | tf_op jit(solution)/shard_map/all_to_all | solution.py:230
  12.4 0.0 copy-done
  12.4 0.0 copy-done.1
  12.5 0.0 copy-done.2
  12.5 2.0 %pack_pair.1 = bf16[256,4096]{1,0:T(8,128)(2,1)} custom-call(s32[2,256]{1,0:T(2,128)S(1)} %copy-done.2, bf16[256,2048]{1,0:T(8,128)(2,1)S(1)} %copy-done, bf16[256,2048]{1,0:T(8,128)(2,1)S(1)} %copy-done.1), custom_call_target="tpu_custom_call" | custom-call | flops 536870912 | bytes 4194304 | tf_op jit(solution)/shard_map/pack_pair/pallas_call | solution.py:196
  14.5 46.8 %all-to-all-done = bf16[32,8,4096]{2,1,0:T(8,128)(2,1)} async-done(((bf16[32,8,4096]{2,1,0:T(8,128)(2,1)}), bf16[32,8,4096]{2,1,0:T(8,128)(2,1)}, u32[]{:S(2)}, u32[]{:S(2)}) %all-to-all-start) | async-done | bytes 2097184 | tf_op jit(solution)/shard_map/all_to_all | solution.py:230
  61.3 4.0 %all-to-all-start.2 = ((bf16[32,8,4096]{2,1,0:T(8,128)(2,1)}), bf16[32,8,4096]{2,1,0:T(8,128)(2,1)S(1)}, u32[]{:S(2)}, u32[]{:S(2)}) async-start(bf16[32,8,4096]{2,1,0:T(8,128)(2,1)} %bitcast.8), calls=%async_computation.2 | async-start | bytes 4194304 | tf_op jit(solution)/shard_map/all_to_all | solution.py:233
  65.3 30.3 %expert_piece.2 = bf16[256,2048]{1,0:T(8,128)(2,1)} custom-call(bf16[256,4096]{1,0:T(8,128)(2,1)} %bitcast.4.pair_ref, bf16[1,2048,4096]{2,1,0:T(8,128)(2,1)} %gate_ref.3, bf16[1,2048,4096]{2,1,0:T(8,128)(2,1)} %up_ref.3, bf16[1,4096,2048]{2,1,0:T(8,128)(2,1)} %down_ref.3), custom_call_target="tpu_custom_call" | custom-call | flops 21474836480 | bytes 53477376 | tf_op jit(solution)/shard_map/expert_piece/pallas_call | solution.py:91
  95.6 18.6 %all-to-all-done.2 = bf16[32,8,4096]{2,1,0:T(8,128)(2,1)S(1)} async-done(((bf16[32,8,4096]{2,1,0:T(8,128)(2,1)}), bf16[32,8,4096]{2,1,0:T(8,128)(2,1)S(1)}, u32[]{:S(2)}, u32[]{:S(2)}) %all-to-all-start.2) | async-done | bytes 2097184 | tf_op jit(solution)/shard_map/all_to_all | solution.py:233
  114.2 4.0 %all-to-all-start.1 = ((bf16[32,8,2048]{2,1,0:T(8,128)(2,1)}), bf16[32,8,2048]{2,1,0:T(8,128)(2,1)S(1)}, u32[]{:S(2)}, u32[]{:S(2)}) async-start(bf16[32,8,2048]{2,1,0:T(8,128)(2,1)} %bitcast.5), calls=%async_computation.1 | async-start | bytes 2097152 | tf_op jit(solution)/shard_map/all_to_all | solution.py:238
  118.2 28.6 %expert_piece.3 = bf16[256,2048]{1,0:T(8,128)(2,1)} custom-call(bf16[256,4096]{1,0:T(8,128)(2,1)S(1)} %bitcast.16, bf16[1,2048,4096]{2,1,0:T(8,128)(2,1)} %gate_ref.3, bf16[1,2048,4096]{2,1,0:T(8,128)(2,1)} %up_ref.3, bf16[1,4096,2048]{2,1,0:T(8,128)(2,1)} %down_ref.3), custom_call_target="tpu_custom_call" | custom-call | flops 21474836480 | bytes 53477376 | tf_op jit(solution)/shard_map/expert_piece/pallas_call | solution.py:91
  146.9 0.0 all-to-all-done.1
  146.9 0.0 copy-start.3
  146.9 5.8 %all-to-all-start.3 = ((bf16[32,8,2048]{2,1,0:T(8,128)(2,1)}), bf16[32,8,2048]{2,1,0:T(8,128)(2,1)S(1)}, u32[]{:S(2)}, u32[]{:S(2)}) async-start(bf16[32,8,2048]{2,1,0:T(8,128)(2,1)} %bitcast.10), calls=%async_computation.3 | async-start | bytes 2097152 | tf_op jit(solution)/shard_map/all_to_all | solution.py:238
  152.7 0.0 copy-done.3
  152.8 1.7 fusion.2
  154.5 24.5 %all-to-all-done.3 = bf16[32,8,2048]{2,1,0:T(8,128)(2,1)S(1)} async-done(((bf16[32,8,2048]{2,1,0:T(8,128)(2,1)}), bf16[32,8,2048]{2,1,0:T(8,128)(2,1)S(1)}, u32[]{:S(2)}, u32[]{:S(2)}) %all-to-all-start.3) | async-done | bytes 1048608 | tf_op jit(solution)/shard_map/all_to_all | solution.py:238
  179.0 1.5 fusion
  (1 shorter events, 0.0 us)
Async XLA Ops:
  5.0 7.5 %copy-start = (bf16[256,2048]{1,0:T(8,128)(2,1)S(1)}, bf16[256,2048]{1,0:T(8,128)(2,1)}, u32[]{:S(2)}) copy-start(bf16[256,2048]{1,0:T(8,128)(2,1)} %rows_ref.3) | copy-start | bytes 3145732
  5.0 7.5 %copy-start.1 = (bf16[256,2048]{1,0:T(8,128)(2,1)S(1)}, bf16[256,2048]{1,0:T(8,128)(2,1)}, u32[]{:S(2)}) copy-start(bf16[256,2048]{1,0:T(8,128)(2,1)} %grads_ref.3) | copy-start | bytes 3145732
  5.0 7.5 %copy-start.2 = (s32[2,256]{1,0:T(2,128)S(1)}, s32[2,256]{1,0:T(2,128)}, u32[]{:S(2)}) copy-start(s32[2,256]{1,0:T(2,128)} %get-tuple-element.7.place_ref) | copy-start | bytes 6148
  5.0 56.3 %all-to-all-start = ((bf16[32,8,4096]{2,1,0:T(8,128)(2,1)}), bf16[32,8,4096]{2,1,0:T(8,128)(2,1)}, u32[]{:S(2)}, u32[]{:S(2)}) async-start(bf16[32,8,4096]{2,1,0:T(8,128)(2,1)} %bitcast.17), calls=%async_computation | async-start | bytes 4194304 | tf_op jit(solution)/shard_map/all_to_all | solution.py:230
  61.3 52.9 %all-to-all-start.2 = ((bf16[32,8,4096]{2,1,0:T(8,128)(2,1)}), bf16[32,8,4096]{2,1,0:T(8,128)(2,1)S(1)}, u32[]{:S(2)}, u32[]{:S(2)}) async-start(bf16[32,8,4096]{2,1,0:T(8,128)(2,1)} %bitcast.8), calls=%async_computation.2 | async-start | bytes 4194304 | tf_op jit(solution)/shard_map/all_to_all | solution.py:233
  114.2 32.6 %all-to-all-start.1 = ((bf16[32,8,2048]{2,1,0:T(8,128)(2,1)}), bf16[32,8,2048]{2,1,0:T(8,128)(2,1)S(1)}, u32[]{:S(2)}, u32[]{:S(2)}) async-start(bf16[32,8,2048]{2,1,0:T(8,128)(2,1)} %bitcast.5), calls=%async_computation.1 | async-start | bytes 2097152 | tf_op jit(solution)/shard_map/all_to_all | solution.py:238
  146.9 5.9 %copy-start.3 = (bf16[32,8,2048]{2,1,0:T(8,128)(2,1)}, bf16[32,8,2048]{2,1,0:T(8,128)(2,1)S(1)}, u32[]{:S(2)}) copy-start(bf16[32,8,2048]{2,1,0:T(8,128)(2,1)S(1)} %all-to-all-done.1) | copy-start | bytes 3145732
  146.9 32.1 %all-to-all-start.3 = ((bf16[32,8,2048]{2,1,0:T(8,128)(2,1)}), bf16[32,8,2048]{2,1,0:T(8,128)(2,1)S(1)}, u32[]{:S(2)}, u32[]{:S(2)}) async-start(bf16[32,8,2048]{2,1,0:T(8,128)(2,1)} %bitcast.10), calls=%async_computation.3 | async-start | bytes 2097152 | tf_op jit(solution)/shard_map/all_to_all | solution.py:238

commit v6 on v5

--- a/solution.py
+++ b/solution.py
@@ -32,41 +32,59 @@
     return partial_sum.astype(jnp.bfloat16)
 
 
+def parts_of(source, target, parts):
+    rows = source.shape[0] // parts
+    for i in range(parts):
+        part = slice(i * rows, (i + 1) * rows)
+        yield source.at[part], target.at[part]
+
+
 def expert_kernel(
-    pair_ref, gate_ref, up_ref, down_ref, out_ref, wide, tall, both, total, sems
+    pair_ref, gate_ref, up_ref, down_ref, out_ref, pair, wide, tall, both, total, leaving, pair_sems, sems, out_sems
 ):
     width, tile = out_ref.shape[1], tall.shape[1]
     steps = gate_ref.shape[2] // tile
-    half, strip = min(256, tile), min(512, width)
+    half, strip = min(256, tile), leaving.shape[2]
+    slots, cuts = wide.shape[0], sems.shape[2]
 
     def copies(step, slot):
         part = pl.ds(pl.multiple_of(step * tile, tile), tile)
+        pairs = (
+            (gate_ref.at[0, :, part], wide.at[slot, :, :tile]),
+            (up_ref.at[0, :, part], wide.at[slot, :, tile:]),
+            (down_ref.at[0, part, :], tall.at[slot]),
+        )
         return [
-            pltpu.make_async_copy(source, target, sems.at[slot, i])
-            for i, (source, target) in enumerate(
-                (
-                    (gate_ref.at[0, :, part], wide.at[slot, :, :tile]),
-                    (up_ref.at[0, :, part], wide.at[slot, :, tile:]),
-                    (down_ref.at[0, part, :], tall.at[slot]),
-                )
-            )
+            pltpu.make_async_copy(source, target, sems.at[slot, i, k])
+            for i, (whole, held) in enumerate(pairs)
+            for k, (source, target) in enumerate(parts_of(whole, held, cuts))
         ]
 
-    for copy in copies(0, 0):
+    arriving = [
+        pltpu.make_async_copy(source, target, pair_sems.at[k])
+        for k, (source, target) in enumerate(parts_of(pair_ref, pair, pair_sems.shape[0]))
+    ]
+    for copy in arriving + copies(0, 0):
         copy.start()
+    for step in range(1, min(slots - 1, steps)):
+        for copy in copies(step, step):
+            copy.start()
     total[...] = jnp.zeros_like(total)
+    for copy in arriving:
+        copy.wait()
 
     def body(step, carry):
-        slot = lax.rem(step, 2)
-
-        @pl.when(step + 1 < steps)
+        slot = lax.rem(step, slots)
+        ahead = step + slots - 1
+
+        @pl.when(ahead < steps)
         def _():
-            for copy in copies(step + 1, 1 - slot):
+            for copy in copies(ahead, lax.rem(ahead, slots)):
                 copy.start()
 
         for copy in copies(step, slot):
             copy.wait()
-        rows, grads = pair_ref[:, :width], pair_ref[:, width:]
+        rows, grads = pair[:, :width], pair[:, width:]
         for low in range(0, tile, half):
             high = low + half
             gate_pre = dot(rows, wide[slot, :, low:high], ((1,), (0,)))
@@ -81,26 +99,38 @@
         return carry
 
     lax.fori_loop(0, steps, body, 0)
-    out_ref[...] = total[...].astype(out_ref.dtype)
+    results = []
+    for i in range(width // strip):
+        columns = slice(i * strip, (i + 1) * strip)
+        leaving[i] = total[:, columns].astype(leaving.dtype)
+        results.append(pltpu.make_async_copy(leaving.at[i], out_ref.at[:, columns], out_sems.at[i]))
+        results[-1].start()
+    for copy in results:
+        copy.wait()
 
 
 def expert_piece(pair, gate_weight, up_weight, down_weight):
     rows, width = pair.shape[0], pair.shape[1] // 2
     hidden = gate_weight.shape[2]
-    tile = min(512, hidden)
+    tile, strip = min(512, hidden), min(512, width)
+    slots, cuts = 3, 4
     return pl.pallas_call(
         expert_kernel,
-        in_specs=[pl.BlockSpec(memory_space=pltpu.VMEM)] + [pl.BlockSpec(memory_space=pl.ANY)] * 3,
-        out_specs=pl.BlockSpec(memory_space=pltpu.VMEM),
+        in_specs=[pl.BlockSpec(memory_space=pl.ANY)] * 4,
+        out_specs=pl.BlockSpec(memory_space=pl.ANY),
         out_shape=jax.ShapeDtypeStruct((rows, width), jnp.bfloat16),
         scratch_shapes=[
-            pltpu.VMEM((2, width, 2 * tile), jnp.bfloat16),
-            pltpu.VMEM((2, tile, width), jnp.bfloat16),
+            pltpu.VMEM((rows, 2 * width), jnp.bfloat16),
+            pltpu.VMEM((slots, width, 2 * tile), jnp.bfloat16),
+            pltpu.VMEM((slots, tile, width), jnp.bfloat16),
             pltpu.VMEM((rows, 2 * tile), jnp.bfloat16),
             pltpu.VMEM((rows, width), jnp.float32),
-            pltpu.SemaphoreType.DMA((2, 3)),
+            pltpu.VMEM((width // strip, rows, strip), jnp.bfloat16),
+            pltpu.SemaphoreType.DMA((4,)),
+            pltpu.SemaphoreType.DMA((slots, 3, cuts)),
+            pltpu.SemaphoreType.DMA((width // strip,)),
         ],
-        compiler_params=pltpu.CompilerParams(vmem_limit_bytes=40 * MIB),
+        compiler_params=pltpu.CompilerParams(vmem_limit_bytes=56 * MIB),
         cost_estimate=pl.CostEstimate(
             flops=10 * rows * width * hidden,
             bytes_accessed=6 * width * hidden + 6 * rows * width,

time: 181 us -> 185 us (1.022)
  Pallas kernels: 65.9 us -> 69.8 us
    pallas_call x2, Pallas kernels: 58.9 us -> 62.8 us  [expert_piece(): pl.pallas_call(expert_kernel, in_specs=[pl.BlockSpec(memory_space=pl.ANY)...]
  transfers between devices with their start and end apart: 4 -> 4, of which waited for: 3 -> 3; matrix products, arithmetic and copies ran while one was open for 1% -> 1% of each run, Pallas kernels for 34% -> 35%
where the time goes in v6:
time: 185 us; the launch traced here: 184 us
  waiting for transfers between devices  88.8 us (48%)
  Pallas kernels  69.8 us (38%)
  starting transfers between devices  21.3 us (12%)
  matrix products  3.18 us (2%)
    pallas_call x2, Pallas kernels, expert_piece(): pl.pallas_call(expert_kernel, in_specs=[pl.BlockSpec(memory_space=pl.ANY)...  62.8 us
    all_to_all x1, waiting for transfers between devices, in_pieces(): arrived = [exchange(packed.reshape(experts, depth, 2 * width))]  46.8 us
    all_to_all x2, waiting for transfers between devices, in_pieces(): exchange(partial_sum.reshape(experts, depth, width)).reshape(count, width)  24.5 us
    all_to_all x1, waiting for transfers between devices, in_pieces(): arrived.append(exchange(packed.reshape(experts, depth, 2 * width)))  17.5 us
    all_to_all x2, starting transfers between devices, in_pieces(): exchange(partial_sum.reshape(experts, depth, width)).reshape(count, width)  9.84 us
    all_to_all x1, starting transfers between devices, in_pieces(): arrived = [exchange(packed.reshape(experts, depth, 2 * width))]  7.42 us
    pallas_call x1, Pallas kernels, pack_first(): pl.pallas_call(functools.partial(first_kernel, depth), in_specs=[pl.Block...  4.94 us
    all_to_all x1, starting transfers between devices, in_pieces(): arrived.append(exchange(packed.reshape(experts, depth, 2 * width)))  4.01 us
  transfers between devices with their start and end apart: 4, of which 3 were waited for; matrix products, arithmetic and copies ran while one was open for 1% of the time, Pallas kernels for 35%

profile of v6, /device:TPU:0, one launch (start us, length us, event | category | flops | bytes accessed | tf_op | source)
XLA Modules:
  0.0 184.2 jit_solution(5059181825319898137)
XLA Ops:
  0.0 4.9 %pack_first.1 = (s32[2,256]{1,0:T(2,128)}, bf16[256,4096]{1,0:T(8,128)(2,1)}) custom-call(s32[1,256]{1,0:T(1,128)} %bitcast.22, s32[1,32]{1,0:T(1,128)} %bitcast.23, bf16[256,2048]{1,0:T(8,128)(2,1)} %rows_ref.3, bf16[256,2048]{1,0:T(8,128)(2,1)} %grads_ref.3), custom_call_target="tpu_custom_call" | custom-call | tf_op jit(solution)/shard_map/pack_first/pallas_call | solution.py:199
  5.0 0.0 copy-start
  5.0 0.0 copy-start.1
  5.0 0.0 copy-start.2
  5.0 7.4 %all-to-all-start = ((bf16[32,8,4096]{2,1,0:T(8,128)(2,1)}), bf16[32,8,4096]{2,1,0:T(8,128)(2,1)}, u32[]{:S(2)}, u32[]{:S(2)}) async-start(bf16[32,8,4096]{2,1,0:T(8,128)(2,1)} %bitcast.17), calls=%async_computation | async-start | bytes 4194304 | tf_op jit(solution)/shard_map/all_to_all | solution.py:260
  12.4 0.0 copy-done
  12.4 0.0 copy-done.1
  12.4 0.0 copy-done.2
  12.4 2.1 %pack_pair.1 = bf16[256,4096]{1,0:T(8,128)(2,1)} custom-call(s32[2,256]{1,0:T(2,128)S(1)} %copy-done.2, bf16[256,2048]{1,0:T(8,128)(2,1)S(1)} %copy-done, bf16[256,2048]{1,0:T(8,128)(2,1)S(1)} %copy-done.1), custom_call_target="tpu_custom_call" | custom-call | flops 536870912 | bytes 4194304 | tf_op jit(solution)/shard_map/pack_pair/pallas_call | solution.py:226
  14.5 46.8 %all-to-all-done = bf16[32,8,4096]{2,1,0:T(8,128)(2,1)} async-done(((bf16[32,8,4096]{2,1,0:T(8,128)(2,1)}), bf16[32,8,4096]{2,1,0:T(8,128)(2,1)}, u32[]{:S(2)}, u32[]{:S(2)}) %all-to-all-start) | async-done | bytes 2097184 | tf_op jit(solution)/shard_map/all_to_all | solution.py:260
  61.3 4.0 %all-to-all-start.2 = ((bf16[32,8,4096]{2,1,0:T(8,128)(2,1)}), bf16[32,8,4096]{2,1,0:T(8,128)(2,1)S(1)}, u32[]{:S(2)}, u32[]{:S(2)}) async-start(bf16[32,8,4096]{2,1,0:T(8,128)(2,1)} %bitcast.8), calls=%async_computation.2 | async-start | bytes 4194304 | tf_op jit(solution)/shard_map/all_to_all | solution.py:263
  65.3 31.4 %expert_piece.2 = bf16[256,2048]{1,0:T(8,128)(2,1)} custom-call(bf16[256,4096]{1,0:T(8,128)(2,1)} %bitcast.4.pair_ref, bf16[1,2048,4096]{2,1,0:T(8,128)(2,1)} %gate_ref.3, bf16[1,2048,4096]{2,1,0:T(8,128)(2,1)} %up_ref.3, bf16[1,4096,2048]{2,1,0:T(8,128)(2,1)} %down_ref.3), custom_call_target="tpu_custom_call" | custom-call | flops 21474836480 | bytes 53477376 | tf_op jit(solution)/shard_map/expert_piece/pallas_call | solution.py:117
  96.7 17.5 %all-to-all-done.2 = bf16[32,8,4096]{2,1,0:T(8,128)(2,1)S(1)} async-done(((bf16[32,8,4096]{2,1,0:T(8,128)(2,1)}), bf16[32,8,4096]{2,1,0:T(8,128)(2,1)S(1)}, u32[]{:S(2)}, u32[]{:S(2)}) %all-to-all-start.2) | async-done | bytes 2097184 | tf_op jit(solution)/shard_map/all_to_all | solution.py:263
  114.2 0.0 copy-start.4
  114.2 4.0 %all-to-all-start.1 = ((bf16[32,8,2048]{2,1,0:T(8,128)(2,1)}), bf16[32,8,2048]{2,1,0:T(8,128)(2,1)S(1)}, u32[]{:S(2)}, u32[]{:S(2)}) async-start(bf16[32,8,2048]{2,1,0:T(8,128)(2,1)} %bitcast.19), calls=%async_computation.1 | async-start | bytes 2097152 | tf_op jit(solution)/shard_map/all_to_all | solution.py:268
  118.2 0.0 copy-done.4
  118.2 31.4 %expert_piece.3 = bf16[256,2048]{1,0:T(8,128)(2,1)} custom-call(bf16[256,4096]{1,0:T(8,128)(2,1)} %bitcast.16, bf16[1,2048,4096]{2,1,0:T(8,128)(2,1)} %gate_ref.3, bf16[1,2048,4096]{2,1,0:T(8,128)(2,1)} %up_ref.3, bf16[1,4096,2048]{2,1,0:T(8,128)(2,1)} %down_ref.3), custom_call_target="tpu_custom_call" | custom-call | flops 21474836480 | bytes 53477376 | tf_op jit(solution)/shard_map/expert_piece/pallas_call | solution.py:117
  149.7 0.0 all-to-all-done.1
  149.7 0.0 copy-start.3
  149.7 1.0 copy-done.3
  150.7 5.8 %all-to-all-start.3 = ((bf16[32,8,2048]{2,1,0:T(8,128)(2,1)}), bf16[32,8,2048]{2,1,0:T(8,128)(2,1)S(1)}, u32[]{:S(2)}, u32[]{:S(2)}) async-start(bf16[32,8,2048]{2,1,0:T(8,128)(2,1)} %bitcast.18), calls=%async_computation.3 | async-start | bytes 2097152 | tf_op jit(solution)/shard_map/all_to_all | solution.py:268
  156.5 1.7 fusion.2
  158.2 24.5 %all-to-all-done.3 = bf16[32,8,2048]{2,1,0:T(8,128)(2,1)S(1)} async-done(((bf16[32,8,2048]{2,1,0:T(8,128)(2,1)}), bf16[32,8,2048]{2,1,0:T(8,128)(2,1)S(1)}, u32[]{:S(2)}, u32[]{:S(2)}) %all-to-all-start.3) | async-done | bytes 1048608 | tf_op jit(solution)/shard_map/all_to_all | solution.py:268
  182.7 1.5 fusion
  (1 shorter events, 0.0 us)
Async XLA Ops:
  5.0 7.5 %copy-start = (bf16[256,2048]{1,0:T(8,128)(2,1)S(1)}, bf16[256,2048]{1,0:T(8,128)(2,1)}, u32[]{:S(2)}) copy-start(bf16[256,2048]{1,0:T(8,128)(2,1)} %rows_ref.3) | copy-start | bytes 3145732
  5.0 7.5 %copy-start.1 = (bf16[256,2048]{1,0:T(8,128)(2,1)S(1)}, bf16[256,2048]{1,0:T(8,128)(2,1)}, u32[]{:S(2)}) copy-start(bf16[256,2048]{1,0:T(8,128)(2,1)} %grads_ref.3) | copy-start | bytes 3145732
  5.0 7.5 %copy-start.2 = (s32[2,256]{1,0:T(2,128)S(1)}, s32[2,256]{1,0:T(2,128)}, u32[]{:S(2)}) copy-start(s32[2,256]{1,0:T(2,128)} %get-tuple-element.7.place_ref) | copy-start | bytes 6148
  5.0 56.3 %all-to-all-start = ((bf16[32,8,4096]{2,1,0:T(8,128)(2,1)}), bf16[32,8,4096]{2,1,0:T(8,128)(2,1)}, u32[]{:S(2)}, u32[]{:S(2)}) async-start(bf16[32,8,4096]{2,1,0:T(8,128)(2,1)} %bitcast.17), calls=%async_computation | async-start | bytes 4194304 | tf_op jit(solution)/shard_map/all_to_all | solution.py:260
  61.3 52.9 %all-to-all-start.2 = ((bf16[32,8,4096]{2,1,0:T(8,128)(2,1)}), bf16[32,8,4096]{2,1,0:T(8,128)(2,1)S(1)}, u32[]{:S(2)}, u32[]{:S(2)}) async-start(bf16[32,8,4096]{2,1,0:T(8,128)(2,1)} %bitcast.8), calls=%async_computation.2 | async-start | bytes 4194304 | tf_op jit(solution)/shard_map/all_to_all | solution.py:263
  114.2 4.0 %copy-start.4 = (bf16[32,8,4096]{2,1,0:T(8,128)(2,1)}, bf16[32,8,4096]{2,1,0:T(8,128)(2,1)S(1)}, u32[]{:S(2)}) copy-start(bf16[32,8,4096]{2,1,0:T(8,128)(2,1)S(1)} %all-to-all-done.2) | copy-start | bytes 6291460
  114.2 35.5 %all-to-all-start.1 = ((bf16[32,8,2048]{2,1,0:T(8,128)(2,1)}), bf16[32,8,2048]{2,1,0:T(8,128)(2,1)S(1)}, u32[]{:S(2)}, u32[]{:S(2)}) async-start(bf16[32,8,2048]{2,1,0:T(8,128)(2,1)} %bitcast.19), calls=%async_computation.1 | async-start | bytes 2097152 | tf_op jit(solution)/shard_map/all_to_all | solution.py:268
  149.7 1.0 copy-start.3
  150.7 32.1 %all-to-all-start.3 = ((bf16[32,8,2048]{2,1,0:T(8,128)(2,1)}), bf16[32,8,2048]{2,1,0:T(8,128)(2,1)S(1)}, u32[]{:S(2)}, u32[]{:S(2)}) async-start(bf16[32,8,2048]{2,1,0:T(8,128)(2,1)} %bitcast.18), calls=%async_computation.3 | async-start | bytes 2097152 | tf_op jit(solution)/shard_map/all_to_all | solution.py:268

commit v7 on v5

--- a/solution.py
+++ b/solution.py
@@ -110,6 +110,11 @@
     )(pair, gate_weight, up_weight, down_weight)
 
 
+def turn_of(device, count):
+    quarter = device // (count // 4)
+    return device % (count // 4) * 4 + quarter % 2 * 2 + quarter // 2
+
+
 def place_rows(species, table, depth, pieces):
     experts, rows = table.shape[1], species.shape[1]
     ids = lax.broadcasted_iota(jnp.int32, (experts, rows), 0)
@@ -122,7 +127,8 @@
     before = (row_ids < column_ids).astype(jnp.bfloat16)
     earlier = dot(hits.astype(jnp.bfloat16), before, ((1,), (0,)))
     slot = jnp.sum(earlier * hits, axis=0, keepdims=True).astype(jnp.int32)
-    expert = jnp.sum(ids.astype(jnp.float32) * hits, axis=0, keepdims=True).astype(jnp.int32)
+    turn = turn_of(ids, experts).astype(jnp.float32)
+    expert = jnp.sum(turn * hits, axis=0, keepdims=True).astype(jnp.int32)
     found = []
     for piece in range(pieces):
         own = slot - piece * depth
@@ -225,7 +231,12 @@
     count = experts * depth
     place_of, packed = pack_first(species, expert_table, tokens, out_grads, depth, PIECES)
     exchange = functools.partial(
-        lax.all_to_all, axis_name="expert", split_axis=0, concat_axis=0, tiled=True
+        lax.all_to_all,
+        axis_name="expert",
+        split_axis=0,
+        concat_axis=0,
+        axis_index_groups=[sorted(range(experts), key=lambda i: turn_of(i, experts))],
+        tiled=True,
     )
     arrived = [exchange(packed.reshape(experts, depth, 2 * width))]
     for piece in range(1, PIECES):
@@ -290,6 +301,7 @@
 def per_device(tokens, out_grads, species, expert_table, *weights):
     whole = lax.axis_size("tensor") == 1
     capacity = 2 * tokens.shape[0] // expert_table.shape[0]
+    whole = whole and expert_table.shape[0] % 4 == 0
     form = in_pieces if whole and capacity % (8 * PIECES) == 0 else in_groups
     return form(tokens, out_grads, species, expert_table, *weights)
 

time: 181 us -> 182 us (level)
  waiting for transfers between devices: 89.9 us -> 93.7 us
  starting transfers between devices: 21.3 us -> 18.6 us
where the time goes in v7:
time: 182 us
  waiting for transfers between devices  93.7 us (51%)
  Pallas kernels  65.9 us (36%)
  starting transfers between devices  18.6 us (10%)
  matrix products  3.18 us (2%)
    pallas_call x2, Pallas kernels, expert_piece(): pl.pallas_call(expert_kernel, in_specs=[pl.BlockSpec(memory_space=pltpu.V...  58.9 us
    all_to_all x1, waiting for transfers between devices, in_pieces(): arrived = [exchange(packed.reshape(experts, depth, 2 * width))]  48 us
    all_to_all x2, waiting for transfers between devices, in_pieces(): exchange(partial_sum.reshape(experts, depth, width)).reshape(count, width)  25.8 us
    all_to_all x1, waiting for transfers between devices, in_pieces(): arrived.append(exchange(packed.reshape(experts, depth, 2 * width)))  19.8 us
    all_to_all x2, starting transfers between devices, in_pieces(): exchange(partial_sum.reshape(experts, depth, width)).reshape(count, width)  8.49 us
    all_to_all x1, starting transfers between devices, in_pieces(): arrived = [exchange(packed.reshape(experts, depth, 2 * width))]  7.42 us
    pallas_call x1, Pallas kernels, pack_first(): pl.pallas_call(functools.partial(first_kernel, depth), in_specs=[pl.Block...  4.96 us
  transfers between devices with their start and end apart: 4, of which 3 were waited for; matrix products, arithmetic and copies ran while one was open for 1% of the time, Pallas kernels for 34%

profile of v7, /device:TPU:0, one launch (start us, length us, event | category | flops | bytes accessed | tf_op | source)
XLA Modules:
  0.0 181.6 jit_solution(3550183627493417566)
XLA Ops:
  0.0 5.0 %pack_first.1 = (s32[2,256]{1,0:T(2,128)}, bf16[256,4096]{1,0:T(8,128)(2,1)}) custom-call(s32[1,256]{1,0:T(1,128)} %bitcast.20, s32[1,32]{1,0:T(1,128)} %bitcast.21, bf16[256,2048]{1,0:T(8,128)(2,1)} %rows_ref.3, bf16[256,2048]{1,0:T(8,128)(2,1)} %grads_ref.3), custom_call_target="tpu_custom_call" | custom-call | tf_op jit(solution)/shard_map/pack_first/pallas_call | solution.py:175
  5.0 0.0 copy-start
  5.0 0.0 copy-start.1
  5.0 0.0 copy-start.2
  5.0 7.4 %all-to-all-start = ((bf16[32,8,4096]{2,1,0:T(8,128)(2,1)}), bf16[32,8,4096]{2,1,0:T(8,128)(2,1)}, u32[]{:S(2)}, u32[]{:S(2)}) async-start(bf16[32,8,4096]{2,1,0:T(8,128)(2,1)} %bitcast.17), calls=%async_computation | async-start | bytes 4194304 | tf_op jit(solution)/shard_map/all_to_all | solution.py:241
  12.4 0.0 copy-done
  12.4 0.0 copy-done.1
  12.5 0.0 copy-done.2
  12.5 2.0 %pack_pair.1 = bf16[256,4096]{1,0:T(8,128)(2,1)} custom-call(s32[2,256]{1,0:T(2,128)S(1)} %copy-done.2, bf16[256,2048]{1,0:T(8,128)(2,1)S(1)} %copy-done, bf16[256,2048]{1,0:T(8,128)(2,1)S(1)} %copy-done.1), custom_call_target="tpu_custom_call" | custom-call | flops 536870912 | bytes 4194304 | tf_op jit(solution)/shard_map/pack_pair/pallas_call | solution.py:202
  14.5 48.0 %all-to-all-done = bf16[32,8,4096]{2,1,0:T(8,128)(2,1)} async-done(((bf16[32,8,4096]{2,1,0:T(8,128)(2,1)}), bf16[32,8,4096]{2,1,0:T(8,128)(2,1)}, u32[]{:S(2)}, u32[]{:S(2)}) %all-to-all-start) | async-done | bytes 2097184 | tf_op jit(solution)/shard_map/all_to_all | solution.py:241
  62.5 2.7 %all-to-all-start.2 = ((bf16[32,8,4096]{2,1,0:T(8,128)(2,1)}), bf16[32,8,4096]{2,1,0:T(8,128)(2,1)S(1)}, u32[]{:S(2)}, u32[]{:S(2)}) async-start(bf16[32,8,4096]{2,1,0:T(8,128)(2,1)} %bitcast.8), calls=%async_computation.2 | async-start | bytes 4194304 | tf_op jit(solution)/shard_map/all_to_all | solution.py:244
  65.2 30.3 %expert_piece.2 = bf16[256,2048]{1,0:T(8,128)(2,1)} custom-call(bf16[256,4096]{1,0:T(8,128)(2,1)} %bitcast.4.pair_ref, bf16[1,2048,4096]{2,1,0:T(8,128)(2,1)} %gate_ref.3, bf16[1,2048,4096]{2,1,0:T(8,128)(2,1)} %up_ref.3, bf16[1,4096,2048]{2,1,0:T(8,128)(2,1)} %down_ref.3), custom_call_target="tpu_custom_call" | custom-call | flops 21474836480 | bytes 53477376 | tf_op jit(solution)/shard_map/expert_piece/pallas_call | solution.py:91
  95.5 19.8 %all-to-all-done.2 = bf16[32,8,4096]{2,1,0:T(8,128)(2,1)S(1)} async-done(((bf16[32,8,4096]{2,1,0:T(8,128)(2,1)}), bf16[32,8,4096]{2,1,0:T(8,128)(2,1)S(1)}, u32[]{:S(2)}, u32[]{:S(2)}) %all-to-all-start.2) | async-done | bytes 2097184 | tf_op jit(solution)/shard_map/all_to_all | solution.py:244
  115.4 2.6 %all-to-all-start.1 = ((bf16[32,8,2048]{2,1,0:T(8,128)(2,1)}), bf16[32,8,2048]{2,1,0:T(8,128)(2,1)S(1)}, u32[]{:S(2)}, u32[]{:S(2)}) async-start(bf16[32,8,2048]{2,1,0:T(8,128)(2,1)} %bitcast.5), calls=%async_computation.1 | async-start | bytes 2097152 | tf_op jit(solution)/shard_map/all_to_all | solution.py:249
  118.0 28.6 %expert_piece.3 = bf16[256,2048]{1,0:T(8,128)(2,1)} custom-call(bf16[256,4096]{1,0:T(8,128)(2,1)S(1)} %bitcast.16, bf16[1,2048,4096]{2,1,0:T(8,128)(2,1)} %gate_ref.3, bf16[1,2048,4096]{2,1,0:T(8,128)(2,1)} %up_ref.3, bf16[1,4096,2048]{2,1,0:T(8,128)(2,1)} %down_ref.3), custom_call_target="tpu_custom_call" | custom-call | flops 21474836480 | bytes 53477376 | tf_op jit(solution)/shard_map/expert_piece/pallas_call | solution.py:91
  146.6 0.0 all-to-all-done.1
  146.6 0.0 copy-start.3
  146.7 5.8 %all-to-all-start.3 = ((bf16[32,8,2048]{2,1,0:T(8,128)(2,1)}), bf16[32,8,2048]{2,1,0:T(8,128)(2,1)S(1)}, u32[]{:S(2)}, u32[]{:S(2)}) async-start(bf16[32,8,2048]{2,1,0:T(8,128)(2,1)} %bitcast.10), calls=%async_computation.3 | async-start | bytes 2097152 | tf_op jit(solution)/shard_map/all_to_all | solution.py:249
  152.5 0.0 copy-done.3
  152.5 1.7 fusion.2
  154.2 25.8 %all-to-all-done.3 = bf16[32,8,2048]{2,1,0:T(8,128)(2,1)S(1)} async-done(((bf16[32,8,2048]{2,1,0:T(8,128)(2,1)}), bf16[32,8,2048]{2,1,0:T(8,128)(2,1)S(1)}, u32[]{:S(2)}, u32[]{:S(2)}) %all-to-all-start.3) | async-done | bytes 1048608 | tf_op jit(solution)/shard_map/all_to_all | solution.py:249
  180.1 1.5 fusion
  (1 shorter events, 0.0 us)
Async XLA Ops:
  5.0 7.5 %copy-start = (bf16[256,2048]{1,0:T(8,128)(2,1)S(1)}, bf16[256,2048]{1,0:T(8,128)(2,1)}, u32[]{:S(2)}) copy-start(bf16[256,2048]{1,0:T(8,128)(2,1)} %rows_ref.3) | copy-start | bytes 3145732
  5.0 7.5 %copy-start.1 = (bf16[256,2048]{1,0:T(8,128)(2,1)S(1)}, bf16[256,2048]{1,0:T(8,128)(2,1)}, u32[]{:S(2)}) copy-start(bf16[256,2048]{1,0:T(8,128)(2,1)} %grads_ref.3) | copy-start | bytes 3145732
  5.0 7.5 %copy-start.2 = (s32[2,256]{1,0:T(2,128)S(1)}, s32[2,256]{1,0:T(2,128)}, u32[]{:S(2)}) copy-start(s32[2,256]{1,0:T(2,128)} %get-tuple-element.7.place_ref) | copy-start | bytes 6148
  5.0 57.5 %all-to-all-start = ((bf16[32,8,4096]{2,1,0:T(8,128)(2,1)}), bf16[32,8,4096]{2,1,0:T(8,128)(2,1)}, u32[]{:S(2)}, u32[]{:S(2)}) async-start(bf16[32,8,4096]{2,1,0:T(8,128)(2,1)} %bitcast.17), calls=%async_computation | async-start | bytes 4194304 | tf_op jit(solution)/shard_map/all_to_all | solution.py:241
  62.5 52.8 %all-to-all-start.2 = ((bf16[32,8,4096]{2,1,0:T(8,128)(2,1)}), bf16[32,8,4096]{2,1,0:T(8,128)(2,1)S(1)}, u32[]{:S(2)}, u32[]{:S(2)}) async-start(bf16[32,8,4096]{2,1,0:T(8,128)(2,1)} %bitcast.8), calls=%async_computation.2 | async-start | bytes 4194304 | tf_op jit(solution)/shard_map/all_to_all | solution.py:244
  115.4 31.3 %all-to-all-start.1 = ((bf16[32,8,2048]{2,1,0:T(8,128)(2,1)}), bf16[32,8,2048]{2,1,0:T(8,128)(2,1)S(1)}, u32[]{:S(2)}, u32[]{:S(2)}) async-start(bf16[32,8,2048]{2,1,0:T(8,128)(2,1)} %bitcast.5), calls=%async_computation.1 | async-start | bytes 2097152 | tf_op jit(solution)/shard_map/all_to_all | solution.py:249
  146.6 5.9 %copy-start.3 = (bf16[32,8,2048]{2,1,0:T(8,128)(2,1)}, bf16[32,8,2048]{2,1,0:T(8,128)(2,1)S(1)}, u32[]{:S(2)}) copy-start(bf16[32,8,2048]{2,1,0:T(8,128)(2,1)S(1)} %all-to-all-done.1) | copy-start | bytes 3145732
  146.7 33.4 %all-to-all-start.3 = ((bf16[32,8,2048]{2,1,0:T(8,128)(2,1)}), bf16[32,8,2048]{2,1,0:T(8,128)(2,1)S(1)}, u32[]{:S(2)}, u32[]{:S(2)}) async-start(bf16[32,8,2048]{2,1,0:T(8,128)(2,1)} %bitcast.10), calls=%async_computation.3 | async-start | bytes 2097152 | tf_op jit(solution)/shard_map/all_to_all | solution.py:249

commit v8 on v5

--- a/solution.py
+++ b/solution.py
@@ -33,55 +33,81 @@
 
 
 def expert_kernel(
-    pair_ref, gate_ref, up_ref, down_ref, out_ref, wide, tall, both, total, sems
+    pair_ref, gate_ref, up_ref, down_ref, out_ref, wide, tall, even, odd, total, wide_sems, tall_sems
 ):
     width, tile = out_ref.shape[1], tall.shape[1]
     steps = gate_ref.shape[2] // tile
     half, strip = min(256, tile), min(512, width)
-
-    def copies(step, slot):
+    slots = wide.shape[0]
+
+    def copies(step):
         part = pl.ds(pl.multiple_of(step * tile, tile), tile)
-        return [
-            pltpu.make_async_copy(source, target, sems.at[slot, i])
-            for i, (source, target) in enumerate(
-                (
-                    (gate_ref.at[0, :, part], wide.at[slot, :, :tile]),
-                    (up_ref.at[0, :, part], wide.at[slot, :, tile:]),
-                    (down_ref.at[0, part, :], tall.at[slot]),
-                )
-            )
-        ]
-
-    for copy in copies(0, 0):
-        copy.start()
-    total[...] = jnp.zeros_like(total)
-
-    def body(step, carry):
-        slot = lax.rem(step, 2)
-
-        @pl.when(step + 1 < steps)
-        def _():
-            for copy in copies(step + 1, 1 - slot):
-                copy.start()
-
-        for copy in copies(step, slot):
-            copy.wait()
+        slot, other = lax.rem(step, slots), lax.rem(step, 2)
+        return (
+            pltpu.make_async_copy(
+                gate_ref.at[0, :, part], wide.at[slot, :, :tile], wide_sems.at[slot, 0]
+            ),
+            pltpu.make_async_copy(
+                up_ref.at[0, :, part], wide.at[slot, :, tile:], wide_sems.at[slot, 1]
+            ),
+            pltpu.make_async_copy(down_ref.at[0, part, :], tall.at[other], tall_sems.at[other]),
+        )
+
+    def first_stage(step, both):
+        slot, other = lax.rem(step, slots), lax.rem(step, 2)
         rows, grads = pair_ref[:, :width], pair_ref[:, width:]
         for low in range(0, tile, half):
             high = low + half
             gate_pre = dot(rows, wide[slot, :, low:high], ((1,), (0,)))
             up_pre = dot(rows, wide[slot, :, tile + low : tile + high], ((1,), (0,)))
-            hidden_grad = dot(grads, tall[slot, low:high, :], ((1,), (1,)))
+            hidden_grad = dot(grads, tall[other, low:high, :], ((1,), (1,)))
             gate_grad, up_grad = hidden_grads(gate_pre, up_pre, hidden_grad)
             both[:, low:high] = gate_grad
             both[:, tile + low : tile + high] = up_grad
+
+    def partial_sum(step, both, low):
+        slot = lax.rem(step, slots)
+        return dot(both[...], wide[slot, low : low + strip, :], ((1,), (1,)))
+
+    def start(step):
+        for copy in copies(step):
+            copy.start()
+
+    def wait(step):
+        for copy in copies(step):
+            copy.wait()
+
+    start(0)
+    total[...] = jnp.zeros_like(total)
+    wait(0)
+    if steps > 1:
+        start(1)
+    first_stage(0, even)
+
+    def skewed(step, now, before):
+        wait(step)
+
+        @pl.when(step + 1 < steps)
+        def _():
+            start(step + 1)
+
+        first_stage(step, now)
         for low in range(0, width, strip):
-            high = low + strip
-            total[:, low:high] += dot(both[...], wide[slot, low:high, :], ((1,), (1,)))
+            total[:, low : low + strip] += partial_sum(step - 1, before, low)
+
+    def body(turn, carry):
+        skewed(2 * turn + 1, odd, even)
+        skewed(2 * turn + 2, even, odd)
         return carry
 
-    lax.fori_loop(0, steps, body, 0)
-    out_ref[...] = total[...].astype(out_ref.dtype)
+    lax.fori_loop(0, (steps - 1) // 2, body, 0)
+    if steps % 2 == 0:
+        skewed(steps - 1, odd, even)
+    last = odd if steps % 2 == 0 else even
+    for low in range(0, width, strip):
+        high = low + strip
+        found = total[:, low:high] + partial_sum(steps - 1, last, low)
+        out_ref[:, low:high] = found.astype(out_ref.dtype)
 
 
 def expert_piece(pair, gate_weight, up_weight, down_weight):
@@ -94,11 +120,13 @@
         out_specs=pl.BlockSpec(memory_space=pltpu.VMEM),
         out_shape=jax.ShapeDtypeStruct((rows, width), jnp.bfloat16),
         scratch_shapes=[
-            pltpu.VMEM((2, width, 2 * tile), jnp.bfloat16),
+            pltpu.VMEM((3, width, 2 * tile), jnp.bfloat16),
             pltpu.VMEM((2, tile, width), jnp.bfloat16),
             pltpu.VMEM((rows, 2 * tile), jnp.bfloat16),
+            pltpu.VMEM((rows, 2 * tile), jnp.bfloat16),
             pltpu.VMEM((rows, width), jnp.float32),
-            pltpu.SemaphoreType.DMA((2, 3)),
+            pltpu.SemaphoreType.DMA((3, 2)),
+            pltpu.SemaphoreType.DMA((2,)),
         ],
         compiler_params=pltpu.CompilerParams(vmem_limit_bytes=40 * MIB),
         cost_estimate=pl.CostEstimate(

time: 181 us -> 181 us (level)
  no operation moved by 1% of the time
where the time goes in v8:
time: 181 us
  waiting for transfers between devices  89.4 us (49%)
  Pallas kernels  66.9 us (37%)
  starting transfers between devices  21.3 us (12%)
  matrix products  3.18 us (2%)
    pallas_call x2, Pallas kernels, expert_piece(): pl.pallas_call(expert_kernel, in_specs=[pl.BlockSpec(memory_space=pltpu.V...  59.9 us
    all_to_all x1, waiting for transfers between devices, in_pieces(): arrived = [exchange(packed.reshape(experts, depth, 2 * width))]  46.8 us
    all_to_all x2, waiting for transfers between devices, in_pieces(): exchange(partial_sum.reshape(experts, depth, width)).reshape(count, width)  24.5 us
    all_to_all x1, waiting for transfers between devices, in_pieces(): arrived.append(exchange(packed.reshape(experts, depth, 2 * width)))  18.1 us
    all_to_all x2, starting transfers between devices, in_pieces(): exchange(partial_sum.reshape(experts, depth, width)).reshape(count, width)  9.86 us
    all_to_all x1, starting transfers between devices, in_pieces(): arrived = [exchange(packed.reshape(experts, depth, 2 * width))]  7.41 us
    pallas_call x1, Pallas kernels, pack_first(): pl.pallas_call(functools.partial(first_kernel, depth), in_specs=[pl.Block...  4.96 us
    all_to_all x1, starting transfers between devices, in_pieces(): arrived.append(exchange(packed.reshape(experts, depth, 2 * width)))  4.01 us
  transfers between devices with their start and end apart: 4, of which 3 were waited for; matrix products, arithmetic and copies ran while one was open for 1% of the time, Pallas kernels for 34%

profile of v8, /device:TPU:0, one launch (start us, length us, event | category | flops | bytes accessed | tf_op | source)
XLA Modules:
  0.0 180.9 jit_solution(5129807951139270285)
XLA Ops:
  0.0 5.0 %pack_first.1 = (s32[2,256]{1,0:T(2,128)}, bf16[256,4096]{1,0:T(8,128)(2,1)}) custom-call(s32[1,256]{1,0:T(1,128)} %bitcast.20, s32[1,32]{1,0:T(1,128)} %bitcast.21, bf16[256,2048]{1,0:T(8,128)(2,1)} %rows_ref.3, bf16[256,2048]{1,0:T(8,128)(2,1)} %grads_ref.3), custom_call_target="tpu_custom_call" | custom-call | tf_op jit(solution)/shard_map/pack_first/pallas_call | solution.py:197
  5.0 0.0 copy-start
  5.0 0.0 copy-start.1
  5.0 0.0 copy-start.2
  5.0 7.4 %all-to-all-start = ((bf16[32,8,4096]{2,1,0:T(8,128)(2,1)}), bf16[32,8,4096]{2,1,0:T(8,128)(2,1)}, u32[]{:S(2)}, u32[]{:S(2)}) async-start(bf16[32,8,4096]{2,1,0:T(8,128)(2,1)} %bitcast.17), calls=%async_computation | async-start | bytes 4194304 | tf_op jit(solution)/shard_map/all_to_all | solution.py:258
  12.4 0.0 copy-done
  12.4 0.0 copy-done.1
  12.4 0.0 copy-done.2
  12.5 2.0 %pack_pair.1 = bf16[256,4096]{1,0:T(8,128)(2,1)} custom-call(s32[2,256]{1,0:T(2,128)S(1)} %copy-done.2, bf16[256,2048]{1,0:T(8,128)(2,1)S(1)} %copy-done, bf16[256,2048]{1,0:T(8,128)(2,1)S(1)} %copy-done.1), custom_call_target="tpu_custom_call" | custom-call | flops 536870912 | bytes 4194304 | tf_op jit(solution)/shard_map/pack_pair/pallas_call | solution.py:224
  14.5 46.8 %all-to-all-done = bf16[32,8,4096]{2,1,0:T(8,128)(2,1)} async-done(((bf16[32,8,4096]{2,1,0:T(8,128)(2,1)}), bf16[32,8,4096]{2,1,0:T(8,128)(2,1)}, u32[]{:S(2)}, u32[]{:S(2)}) %all-to-all-start) | async-done | bytes 2097184 | tf_op jit(solution)/shard_map/all_to_all | solution.py:258
  61.3 4.0 %all-to-all-start.2 = ((bf16[32,8,4096]{2,1,0:T(8,128)(2,1)}), bf16[32,8,4096]{2,1,0:T(8,128)(2,1)S(1)}, u32[]{:S(2)}, u32[]{:S(2)}) async-start(bf16[32,8,4096]{2,1,0:T(8,128)(2,1)} %bitcast.8), calls=%async_computation.2 | async-start | bytes 4194304 | tf_op jit(solution)/shard_map/all_to_all | solution.py:261
  65.3 30.8 %expert_piece.2 = bf16[256,2048]{1,0:T(8,128)(2,1)} custom-call(bf16[256,4096]{1,0:T(8,128)(2,1)} %bitcast.4.pair_ref, bf16[1,2048,4096]{2,1,0:T(8,128)(2,1)} %gate_ref.3, bf16[1,2048,4096]{2,1,0:T(8,128)(2,1)} %up_ref.3, bf16[1,4096,2048]{2,1,0:T(8,128)(2,1)} %down_ref.3), custom_call_target="tpu_custom_call" | custom-call | flops 21474836480 | bytes 53477376 | tf_op jit(solution)/shard_map/expert_piece/pallas_call | solution.py:117
  96.1 18.1 %all-to-all-done.2 = bf16[32,8,4096]{2,1,0:T(8,128)(2,1)S(1)} async-done(((bf16[32,8,4096]{2,1,0:T(8,128)(2,1)}), bf16[32,8,4096]{2,1,0:T(8,128)(2,1)S(1)}, u32[]{:S(2)}, u32[]{:S(2)}) %all-to-all-start.2) | async-done | bytes 2097184 | tf_op jit(solution)/shard_map/all_to_all | solution.py:261
  114.2 4.2 %all-to-all-start.1 = ((bf16[32,8,2048]{2,1,0:T(8,128)(2,1)}), bf16[32,8,2048]{2,1,0:T(8,128)(2,1)S(1)}, u32[]{:S(2)}, u32[]{:S(2)}) async-start(bf16[32,8,2048]{2,1,0:T(8,128)(2,1)} %bitcast.5), calls=%async_computation.1 | async-start | bytes 2097152 | tf_op jit(solution)/shard_map/all_to_all | solution.py:266
  118.4 29.1 %expert_piece.3 = bf16[256,2048]{1,0:T(8,128)(2,1)} custom-call(bf16[256,4096]{1,0:T(8,128)(2,1)S(1)} %bitcast.16, bf16[1,2048,4096]{2,1,0:T(8,128)(2,1)} %gate_ref.3, bf16[1,2048,4096]{2,1,0:T(8,128)(2,1)} %up_ref.3, bf16[1,4096,2048]{2,1,0:T(8,128)(2,1)} %down_ref.3), custom_call_target="tpu_custom_call" | custom-call | flops 21474836480 | bytes 53477376 | tf_op jit(solution)/shard_map/expert_piece/pallas_call | solution.py:117
  147.5 0.0 all-to-all-done.1
  147.5 0.0 copy-start.3
  147.6 5.7 %all-to-all-start.3 = ((bf16[32,8,2048]{2,1,0:T(8,128)(2,1)}), bf16[32,8,2048]{2,1,0:T(8,128)(2,1)S(1)}, u32[]{:S(2)}, u32[]{:S(2)}) async-start(bf16[32,8,2048]{2,1,0:T(8,128)(2,1)} %bitcast.10), calls=%async_computation.3 | async-start | bytes 2097152 | tf_op jit(solution)/shard_map/all_to_all | solution.py:266
  153.2 0.0 copy-done.3
  153.3 1.7 fusion.2
  155.0 24.5 %all-to-all-done.3 = bf16[32,8,2048]{2,1,0:T(8,128)(2,1)S(1)} async-done(((bf16[32,8,2048]{2,1,0:T(8,128)(2,1)}), bf16[32,8,2048]{2,1,0:T(8,128)(2,1)S(1)}, u32[]{:S(2)}, u32[]{:S(2)}) %all-to-all-start.3) | async-done | bytes 1048608 | tf_op jit(solution)/shard_map/all_to_all | solution.py:266
  179.5 1.5 fusion
  (1 shorter events, 0.0 us)
Async XLA Ops:
  5.0 7.5 %copy-start = (bf16[256,2048]{1,0:T(8,128)(2,1)S(1)}, bf16[256,2048]{1,0:T(8,128)(2,1)}, u32[]{:S(2)}) copy-start(bf16[256,2048]{1,0:T(8,128)(2,1)} %rows_ref.3) | copy-start | bytes 3145732
  5.0 7.5 %copy-start.1 = (bf16[256,2048]{1,0:T(8,128)(2,1)S(1)}, bf16[256,2048]{1,0:T(8,128)(2,1)}, u32[]{:S(2)}) copy-start(bf16[256,2048]{1,0:T(8,128)(2,1)} %grads_ref.3) | copy-start | bytes 3145732
  5.0 7.5 %copy-start.2 = (s32[2,256]{1,0:T(2,128)S(1)}, s32[2,256]{1,0:T(2,128)}, u32[]{:S(2)}) copy-start(s32[2,256]{1,0:T(2,128)} %get-tuple-element.7.place_ref) | copy-start | bytes 6148
  5.0 56.3 %all-to-all-start = ((bf16[32,8,4096]{2,1,0:T(8,128)(2,1)}), bf16[32,8,4096]{2,1,0:T(8,128)(2,1)}, u32[]{:S(2)}, u32[]{:S(2)}) async-start(bf16[32,8,4096]{2,1,0:T(8,128)(2,1)} %bitcast.17), calls=%async_computation | async-start | bytes 4194304 | tf_op jit(solution)/shard_map/all_to_all | solution.py:258
  61.3 52.9 %all-to-all-start.2 = ((bf16[32,8,4096]{2,1,0:T(8,128)(2,1)}), bf16[32,8,4096]{2,1,0:T(8,128)(2,1)S(1)}, u32[]{:S(2)}, u32[]{:S(2)}) async-start(bf16[32,8,4096]{2,1,0:T(8,128)(2,1)} %bitcast.8), calls=%async_computation.2 | async-start | bytes 4194304 | tf_op jit(solution)/shard_map/all_to_all | solution.py:261
  114.2 33.3 %all-to-all-start.1 = ((bf16[32,8,2048]{2,1,0:T(8,128)(2,1)}), bf16[32,8,2048]{2,1,0:T(8,128)(2,1)S(1)}, u32[]{:S(2)}, u32[]{:S(2)}) async-start(bf16[32,8,2048]{2,1,0:T(8,128)(2,1)} %bitcast.5), calls=%async_computation.1 | async-start | bytes 2097152 | tf_op jit(solution)/shard_map/all_to_all | solution.py:266
  147.5 5.7 %copy-start.3 = (bf16[32,8,2048]{2,1,0:T(8,128)(2,1)}, bf16[32,8,2048]{2,1,0:T(8,128)(2,1)S(1)}, u32[]{:S(2)}) copy-start(bf16[32,8,2048]{2,1,0:T(8,128)(2,1)S(1)} %all-to-all-done.1) | copy-start | bytes 3145732
  147.6 31.9 %all-to-all-start.3 = ((bf16[32,8,2048]{2,1,0:T(8,128)(2,1)}), bf16[32,8,2048]{2,1,0:T(8,128)(2,1)S(1)}, u32[]{:S(2)}, u32[]{:S(2)}) async-start(bf16[32,8,2048]{2,1,0:T(8,128)(2,1)} %bitcast.10), calls=%async_computation.3 | async-start | bytes 2097152 | tf_op jit(solution)/shard_map/all_to_all | solution.py:266

commit v9 on v5

--- a/solution.py
+++ b/solution.py
@@ -136,8 +136,9 @@
 
 
 def first_kernel(
-    depth, species_ref, table_ref, rows_ref, grads_ref, place_ref, out_ref, held, packed, sems
+    depth, species_ref, table_ref, rows_ref, grads_ref, place_ref, out_ref, *scratch
 ):
+    species, table, places_held, held, packed, sems, small_sems = scratch
     width, part = rows_ref.shape[1], held.shape[2]
     parts = width // part
     sources = [ref.at[:, c * part : (c + 1) * part] for ref in (rows_ref, grads_ref) for c in range(parts)]
@@ -148,16 +149,25 @@
         pltpu.make_async_copy(packed.at[i], out_ref.at[:, i * part : (i + 1) * part], sems.at[1, i])
         for i in range(2 * parts)
     ]
-    for copy in arriving:
+    named = [
+        pltpu.make_async_copy(source, target, small_sems.at[i])
+        for i, (source, target) in enumerate(((species_ref, species), (table_ref, table)))
+    ]
+    for copy in named + arriving:
         copy.start()
-    place = place_rows(species_ref[...], table_ref[...], depth, place_ref.shape[0])
+    for copy in named:
+        copy.wait()
+    place = place_rows(species[...], table[...], depth, place_ref.shape[0])
     for piece, found in enumerate(place):
-        place_ref[piece : piece + 1, :] = found
+        places_held[piece : piece + 1, :] = found
+    placed = pltpu.make_async_copy(places_held, place_ref, small_sems.at[2])
+    placed.start()
     select = select_rows(place[0], packed.shape[1])
     for i in range(2 * parts):
         arriving[i].wait()
         packed[i] = dot(select, held[i], ((1,), (0,))).astype(packed.dtype)
         leaving[i].start()
+    placed.wait()
     for copy in leaving:
         copy.wait()
 
@@ -168,16 +178,20 @@
     copies = 2 * width // part
     return pl.pallas_call(
         functools.partial(first_kernel, depth),
-        in_specs=[pl.BlockSpec(memory_space=pltpu.VMEM)] * 2 + [pl.BlockSpec(memory_space=pl.ANY)] * 2,
-        out_specs=[pl.BlockSpec(memory_space=pltpu.VMEM), pl.BlockSpec(memory_space=pl.ANY)],
+        in_specs=[pl.BlockSpec(memory_space=pl.ANY)] * 4,
+        out_specs=[pl.BlockSpec(memory_space=pl.ANY)] * 2,
         out_shape=[
             jax.ShapeDtypeStruct((pieces, rows), jnp.int32),
             jax.ShapeDtypeStruct((count, 2 * width), jnp.bfloat16),
         ],
         scratch_shapes=[
+            pltpu.VMEM((1, rows), jnp.int32),
+            pltpu.VMEM((1, experts), jnp.int32),
+            pltpu.VMEM((pieces, rows), jnp.int32),
             pltpu.VMEM((copies, rows, part), jnp.bfloat16),
             pltpu.VMEM((copies, count, part), jnp.bfloat16),
             pltpu.SemaphoreType.DMA((2, copies)),
+            pltpu.SemaphoreType.DMA((3,)),
         ],
         compiler_params=pltpu.CompilerParams(vmem_limit_bytes=60 * MIB),
         name="pack_first",

time: 181 us -> 180 us (level)
  no operation moved by 1% of the time
where the time goes in v9:
time: 180 us
  waiting for transfers between devices  89.9 us (50%)
  Pallas kernels  65.3 us (36%)
  starting transfers between devices  21.3 us (12%)
  matrix products  3.18 us (2%)
    pallas_call x2, Pallas kernels, expert_piece(): pl.pallas_call(expert_kernel, in_specs=[pl.BlockSpec(memory_space=pltpu.V...  58.9 us
    all_to_all x1, waiting for transfers between devices, in_pieces(): arrived = [exchange(packed.reshape(experts, depth, 2 * width))]  46.8 us
    all_to_all x2, waiting for transfers between devices, in_pieces(): exchange(partial_sum.reshape(experts, depth, width)).reshape(count, width)  24.5 us
    all_to_all x1, waiting for transfers between devices, in_pieces(): arrived.append(exchange(packed.reshape(experts, depth, 2 * width)))  18.6 us
    all_to_all x2, starting transfers between devices, in_pieces(): exchange(partial_sum.reshape(experts, depth, width)).reshape(count, width)  9.85 us
    all_to_all x1, starting transfers between devices, in_pieces(): arrived = [exchange(packed.reshape(experts, depth, 2 * width))]  7.43 us
    pallas_call x1, Pallas kernels, pack_first(): pl.pallas_call(functools.partial(first_kernel, depth), in_specs=[pl.Block...  4.31 us
    all_to_all x1, starting transfers between devices, in_pieces(): arrived.append(exchange(packed.reshape(experts, depth, 2 * width)))  4.01 us
  transfers between devices with their start and end apart: 4, of which 3 were waited for; matrix products, arithmetic and copies ran while one was open for 1% of the time, Pallas kernels for 34%

profile of v9, /device:TPU:0, one launch (start us, length us, event | category | flops | bytes accessed | tf_op | source)
XLA Modules:
  0.0 179.8 jit_solution(5455304852804142114)
XLA Ops:
  0.0 4.3 %pack_first.1 = (s32[2,256]{1,0:T(2,128)}, bf16[256,4096]{1,0:T(8,128)(2,1)}) custom-call(s32[1,256]{1,0:T(1,128)} %bitcast.20, s32[1,32]{1,0:T(1,128)} %bitcast.21, bf16[256,2048]{1,0:T(8,128)(2,1)} %rows_ref.3, bf16[256,2048]{1,0:T(8,128)(2,1)} %grads_ref.3), custom_call_target="tpu_custom_call" | custom-call | tf_op jit(solution)/shard_map/pack_first/pallas_call | solution.py:179
  4.3 0.0 copy-start
  4.3 0.0 copy-start.1
  4.3 0.0 copy-start.2
  4.4 7.4 %all-to-all-start = ((bf16[32,8,4096]{2,1,0:T(8,128)(2,1)}), bf16[32,8,4096]{2,1,0:T(8,128)(2,1)}, u32[]{:S(2)}, u32[]{:S(2)}) async-start(bf16[32,8,4096]{2,1,0:T(8,128)(2,1)} %bitcast.17), calls=%async_computation | async-start | bytes 4194304 | tf_op jit(solution)/shard_map/all_to_all | solution.py:244
  11.8 0.0 copy-done
  11.8 0.0 copy-done.1
  11.8 0.0 copy-done.2
  11.8 2.0 %pack_pair.1 = bf16[256,4096]{1,0:T(8,128)(2,1)} custom-call(s32[2,256]{1,0:T(2,128)S(1)} %copy-done.2, bf16[256,2048]{1,0:T(8,128)(2,1)S(1)} %copy-done, bf16[256,2048]{1,0:T(8,128)(2,1)S(1)} %copy-done.1), custom_call_target="tpu_custom_call" | custom-call | flops 536870912 | bytes 4194304 | tf_op jit(solution)/shard_map/pack_pair/pallas_call | solution.py:210
  13.9 46.8 %all-to-all-done = bf16[32,8,4096]{2,1,0:T(8,128)(2,1)} async-done(((bf16[32,8,4096]{2,1,0:T(8,128)(2,1)}), bf16[32,8,4096]{2,1,0:T(8,128)(2,1)}, u32[]{:S(2)}, u32[]{:S(2)}) %all-to-all-start) | async-done | bytes 2097184 | tf_op jit(solution)/shard_map/all_to_all | solution.py:244
  60.7 4.0 %all-to-all-start.2 = ((bf16[32,8,4096]{2,1,0:T(8,128)(2,1)}), bf16[32,8,4096]{2,1,0:T(8,128)(2,1)S(1)}, u32[]{:S(2)}, u32[]{:S(2)}) async-start(bf16[32,8,4096]{2,1,0:T(8,128)(2,1)} %bitcast.8), calls=%async_computation.2 | async-start | bytes 4194304 | tf_op jit(solution)/shard_map/all_to_all | solution.py:247
  64.7 30.3 %expert_piece.2 = bf16[256,2048]{1,0:T(8,128)(2,1)} custom-call(bf16[256,4096]{1,0:T(8,128)(2,1)} %bitcast.4.pair_ref, bf16[1,2048,4096]{2,1,0:T(8,128)(2,1)} %gate_ref.3, bf16[1,2048,4096]{2,1,0:T(8,128)(2,1)} %up_ref.3, bf16[1,4096,2048]{2,1,0:T(8,128)(2,1)} %down_ref.3), custom_call_target="tpu_custom_call" | custom-call | flops 21474836480 | bytes 53477376 | tf_op jit(solution)/shard_map/expert_piece/pallas_call | solution.py:91
  95.0 18.6 %all-to-all-done.2 = bf16[32,8,4096]{2,1,0:T(8,128)(2,1)S(1)} async-done(((bf16[32,8,4096]{2,1,0:T(8,128)(2,1)}), bf16[32,8,4096]{2,1,0:T(8,128)(2,1)S(1)}, u32[]{:S(2)}, u32[]{:S(2)}) %all-to-all-start.2) | async-done | bytes 2097184 | tf_op jit(solution)/shard_map/all_to_all | solution.py:247
  113.6 4.0 %all-to-all-start.1 = ((bf16[32,8,2048]{2,1,0:T(8,128)(2,1)}), bf16[32,8,2048]{2,1,0:T(8,128)(2,1)S(1)}, u32[]{:S(2)}, u32[]{:S(2)}) async-start(bf16[32,8,2048]{2,1,0:T(8,128)(2,1)} %bitcast.5), calls=%async_computation.1 | async-start | bytes 2097152 | tf_op jit(solution)/shard_map/all_to_all | solution.py:252
  117.6 28.6 %expert_piece.3 = bf16[256,2048]{1,0:T(8,128)(2,1)} custom-call(bf16[256,4096]{1,0:T(8,128)(2,1)S(1)} %bitcast.16, bf16[1,2048,4096]{2,1,0:T(8,128)(2,1)} %gate_ref.3, bf16[1,2048,4096]{2,1,0:T(8,128)(2,1)} %up_ref.3, bf16[1,4096,2048]{2,1,0:T(8,128)(2,1)} %down_ref.3), custom_call_target="tpu_custom_call" | custom-call | flops 21474836480 | bytes 53477376 | tf_op jit(solution)/shard_map/expert_piece/pallas_call | solution.py:91
  146.2 0.0 all-to-all-done.1
  146.2 0.0 copy-start.3
  146.2 5.8 %all-to-all-start.3 = ((bf16[32,8,2048]{2,1,0:T(8,128)(2,1)}), bf16[32,8,2048]{2,1,0:T(8,128)(2,1)S(1)}, u32[]{:S(2)}, u32[]{:S(2)}) async-start(bf16[32,8,2048]{2,1,0:T(8,128)(2,1)} %bitcast.10), calls=%async_computation.3 | async-start | bytes 2097152 | tf_op jit(solution)/shard_map/all_to_all | solution.py:252
  152.1 0.0 copy-done.3
  152.1 1.7 fusion.2
  153.8 24.5 %all-to-all-done.3 = bf16[32,8,2048]{2,1,0:T(8,128)(2,1)S(1)} async-done(((bf16[32,8,2048]{2,1,0:T(8,128)(2,1)}), bf16[32,8,2048]{2,1,0:T(8,128)(2,1)S(1)}, u32[]{:S(2)}, u32[]{:S(2)}) %all-to-all-start.3) | async-done | bytes 1048608 | tf_op jit(solution)/shard_map/all_to_all | solution.py:252
  178.3 1.5 fusion
  (1 shorter events, 0.0 us)
Async XLA Ops:
  4.3 7.5 %copy-start = (bf16[256,2048]{1,0:T(8,128)(2,1)S(1)}, bf16[256,2048]{1,0:T(8,128)(2,1)}, u32[]{:S(2)}) copy-start(bf16[256,2048]{1,0:T(8,128)(2,1)} %rows_ref.3) | copy-start | bytes 3145732
  4.3 7.5 %copy-start.1 = (bf16[256,2048]{1,0:T(8,128)(2,1)S(1)}, bf16[256,2048]{1,0:T(8,128)(2,1)}, u32[]{:S(2)}) copy-start(bf16[256,2048]{1,0:T(8,128)(2,1)} %grads_ref.3) | copy-start | bytes 3145732
  4.3 7.5 %copy-start.2 = (s32[2,256]{1,0:T(2,128)S(1)}, s32[2,256]{1,0:T(2,128)}, u32[]{:S(2)}) copy-start(s32[2,256]{1,0:T(2,128)} %get-tuple-element.7.place_ref) | copy-start | bytes 6148
  4.4 56.3 %all-to-all-start = ((bf16[32,8,4096]{2,1,0:T(8,128)(2,1)}), bf16[32,8,4096]{2,1,0:T(8,128)(2,1)}, u32[]{:S(2)}, u32[]{:S(2)}) async-start(bf16[32,8,4096]{2,1,0:T(8,128)(2,1)} %bitcast.17), calls=%async_computation | async-start | bytes 4194304 | tf_op jit(solution)/shard_map/all_to_all | solution.py:244
  60.7 52.9 %all-to-all-start.2 = ((bf16[32,8,4096]{2,1,0:T(8,128)(2,1)}), bf16[32,8,4096]{2,1,0:T(8,128)(2,1)S(1)}, u32[]{:S(2)}, u32[]{:S(2)}) async-start(bf16[32,8,4096]{2,1,0:T(8,128)(2,1)} %bitcast.8), calls=%async_computation.2 | async-start | bytes 4194304 | tf_op jit(solution)/shard_map/all_to_all | solution.py:247
  113.6 32.6 %all-to-all-start.1 = ((bf16[32,8,2048]{2,1,0:T(8,128)(2,1)}), bf16[32,8,2048]{2,1,0:T(8,128)(2,1)S(1)}, u32[]{:S(2)}, u32[]{:S(2)}) async-start(bf16[32,8,2048]{2,1,0:T(8,128)(2,1)} %bitcast.5), calls=%async_computation.1 | async-start | bytes 2097152 | tf_op jit(solution)/shard_map/all_to_all | solution.py:252
  146.2 5.9 %copy-start.3 = (bf16[32,8,2048]{2,1,0:T(8,128)(2,1)}, bf16[32,8,2048]{2,1,0:T(8,128)(2,1)S(1)}, u32[]{:S(2)}) copy-start(bf16[32,8,2048]{2,1,0:T(8,128)(2,1)S(1)} %all-to-all-done.1) | copy-start | bytes 3145732
  146.2 32.1 %all-to-all-start.3 = ((bf16[32,8,2048]{2,1,0:T(8,128)(2,1)}), bf16[32,8,2048]{2,1,0:T(8,128)(2,1)S(1)}, u32[]{:S(2)}, u32[]{:S(2)}) async-start(bf16[32,8,2048]{2,1,0:T(8,128)(2,1)} %bitcast.10), calls=%async_computation.3 | async-start | bytes 2097152 | tf_op jit(solution)/shard_map/all_to_all | solution.py:252

commit v10 on v9

--- a/solution.py
+++ b/solution.py
@@ -64,13 +64,17 @@
             for copy in copies(step + 1, 1 - slot):
                 copy.start()
 
-        for copy in copies(step, slot):
-            copy.wait()
+        gate_copy, up_copy, down_copy = copies(step, slot)
+        gate_copy.wait()
         rows, grads = pair_ref[:, :width], pair_ref[:, width:]
         for low in range(0, tile, half):
             high = low + half
             gate_pre = dot(rows, wide[slot, :, low:high], ((1,), (0,)))
+            if low == 0:
+                up_copy.wait()
             up_pre = dot(rows, wide[slot, :, tile + low : tile + high], ((1,), (0,)))
+            if low == 0:
+                down_copy.wait()
             hidden_grad = dot(grads, tall[slot, low:high, :], ((1,), (1,)))
             gate_grad, up_grad = hidden_grads(gate_pre, up_pre, hidden_grad)
             both[:, low:high] = gate_grad

time: 180 us -> 186 us (1.033)
  Pallas kernels: 65.3 us -> 76.8 us
  waiting for transfers between devices: 89.9 us -> 84.2 us
    pallas_call x2, Pallas kernels: 58.9 us -> 70.4 us  [expert_piece(): pl.pallas_call(expert_kernel, in_specs=[pl.BlockSpec(memory_space=pltpu.V...]
    all_to_all x1, waiting for transfers between devices: 18.6 us -> 12.9 us  [in_pieces(): arrived.append(exchange(packed.reshape(experts, depth, 2 * width)))]
  transfers between devices with their start and end apart: 4 -> 4, of which waited for: 3 -> 3; matrix products, arithmetic and copies ran while one was open for 1% -> 1% of each run, Pallas kernels for 34% -> 39%
where the time goes in v10:
time: 186 us
  waiting for transfers between devices  84.2 us (45%)
  Pallas kernels  76.8 us (41%)
  starting transfers between devices  21.3 us (11%)
  matrix products  3.18 us (2%)
    pallas_call x2, Pallas kernels, expert_piece(): pl.pallas_call(expert_kernel, in_specs=[pl.BlockSpec(memory_space=pltpu.V...  70.4 us
    all_to_all x1, waiting for transfers between devices, in_pieces(): arrived = [exchange(packed.reshape(experts, depth, 2 * width))]  46.8 us
    all_to_all x2, waiting for transfers between devices, in_pieces(): exchange(partial_sum.reshape(experts, depth, width)).reshape(count, width)  24.5 us
    all_to_all x1, waiting for transfers between devices, in_pieces(): arrived.append(exchange(packed.reshape(experts, depth, 2 * width)))  12.9 us
    all_to_all x2, starting transfers between devices, in_pieces(): exchange(partial_sum.reshape(experts, depth, width)).reshape(count, width)  9.85 us
    all_to_all x1, starting transfers between devices, in_pieces(): arrived = [exchange(packed.reshape(experts, depth, 2 * width))]  7.43 us
    pallas_call x1, Pallas kernels, pack_first(): pl.pallas_call(functools.partial(first_kernel, depth), in_specs=[pl.Block...  4.31 us
    all_to_all x1, starting transfers between devices, in_pieces(): arrived.append(exchange(packed.reshape(experts, depth, 2 * width)))  4.01 us
  transfers between devices with their start and end apart: 4, of which 3 were waited for; matrix products, arithmetic and copies ran while one was open for 1% of the time, Pallas kernels for 39%

profile of v10, /device:TPU:0, one launch (start us, length us, event | category | flops | bytes accessed | tf_op | source)
XLA Modules:
  0.0 185.6 jit_solution(221421184986940074)
XLA Ops:
  0.0 4.3 %pack_first.1 = (s32[2,256]{1,0:T(2,128)}, bf16[256,4096]{1,0:T(8,128)(2,1)}) custom-call(s32[1,256]{1,0:T(1,128)} %bitcast.20, s32[1,32]{1,0:T(1,128)} %bitcast.21, bf16[256,2048]{1,0:T(8,128)(2,1)} %rows_ref.3, bf16[256,2048]{1,0:T(8,128)(2,1)} %grads_ref.3), custom_call_target="tpu_custom_call" | custom-call | tf_op jit(solution)/shard_map/pack_first/pallas_call | solution.py:183
  4.3 0.0 copy-start
  4.3 0.0 copy-start.1
  4.3 0.0 copy-start.2
  4.4 7.4 %all-to-all-start = ((bf16[32,8,4096]{2,1,0:T(8,128)(2,1)}), bf16[32,8,4096]{2,1,0:T(8,128)(2,1)}, u32[]{:S(2)}, u32[]{:S(2)}) async-start(bf16[32,8,4096]{2,1,0:T(8,128)(2,1)} %bitcast.17), calls=%async_computation | async-start | bytes 4194304 | tf_op jit(solution)/shard_map/all_to_all | solution.py:248
  11.8 0.0 copy-done
  11.8 0.0 copy-done.1
  11.8 0.0 copy-done.2
  11.8 2.0 %pack_pair.1 = bf16[256,4096]{1,0:T(8,128)(2,1)} custom-call(s32[2,256]{1,0:T(2,128)S(1)} %copy-done.2, bf16[256,2048]{1,0:T(8,128)(2,1)S(1)} %copy-done, bf16[256,2048]{1,0:T(8,128)(2,1)S(1)} %copy-done.1), custom_call_target="tpu_custom_call" | custom-call | flops 536870912 | bytes 4194304 | tf_op jit(solution)/shard_map/pack_pair/pallas_call | solution.py:214
  13.9 46.8 %all-to-all-done = bf16[32,8,4096]{2,1,0:T(8,128)(2,1)} async-done(((bf16[32,8,4096]{2,1,0:T(8,128)(2,1)}), bf16[32,8,4096]{2,1,0:T(8,128)(2,1)}, u32[]{:S(2)}, u32[]{:S(2)}) %all-to-all-start) | async-done | bytes 2097184 | tf_op jit(solution)/shard_map/all_to_all | solution.py:248
  60.7 4.0 %all-to-all-start.2 = ((bf16[32,8,4096]{2,1,0:T(8,128)(2,1)}), bf16[32,8,4096]{2,1,0:T(8,128)(2,1)S(1)}, u32[]{:S(2)}, u32[]{:S(2)}) async-start(bf16[32,8,4096]{2,1,0:T(8,128)(2,1)} %bitcast.8), calls=%async_computation.2 | async-start | bytes 4194304 | tf_op jit(solution)/shard_map/all_to_all | solution.py:251
  64.7 36.0 %expert_piece.2 = bf16[256,2048]{1,0:T(8,128)(2,1)} custom-call(bf16[256,4096]{1,0:T(8,128)(2,1)} %bitcast.4.pair_ref, bf16[1,2048,4096]{2,1,0:T(8,128)(2,1)} %gate_ref.3, bf16[1,2048,4096]{2,1,0:T(8,128)(2,1)} %up_ref.3, bf16[1,4096,2048]{2,1,0:T(8,128)(2,1)} %down_ref.3), custom_call_target="tpu_custom_call" | custom-call | flops 21474836480 | bytes 53477376 | tf_op jit(solution)/shard_map/expert_piece/pallas_call | solution.py:95
  100.7 12.9 %all-to-all-done.2 = bf16[32,8,4096]{2,1,0:T(8,128)(2,1)S(1)} async-done(((bf16[32,8,4096]{2,1,0:T(8,128)(2,1)}), bf16[32,8,4096]{2,1,0:T(8,128)(2,1)S(1)}, u32[]{:S(2)}, u32[]{:S(2)}) %all-to-all-start.2) | async-done | bytes 2097184 | tf_op jit(solution)/shard_map/all_to_all | solution.py:251
  113.6 4.0 %all-to-all-start.1 = ((bf16[32,8,2048]{2,1,0:T(8,128)(2,1)}), bf16[32,8,2048]{2,1,0:T(8,128)(2,1)S(1)}, u32[]{:S(2)}, u32[]{:S(2)}) async-start(bf16[32,8,2048]{2,1,0:T(8,128)(2,1)} %bitcast.5), calls=%async_computation.1 | async-start | bytes 2097152 | tf_op jit(solution)/shard_map/all_to_all | solution.py:256
  117.6 34.4 %expert_piece.3 = bf16[256,2048]{1,0:T(8,128)(2,1)} custom-call(bf16[256,4096]{1,0:T(8,128)(2,1)S(1)} %bitcast.16, bf16[1,2048,4096]{2,1,0:T(8,128)(2,1)} %gate_ref.3, bf16[1,2048,4096]{2,1,0:T(8,128)(2,1)} %up_ref.3, bf16[1,4096,2048]{2,1,0:T(8,128)(2,1)} %down_ref.3), custom_call_target="tpu_custom_call" | custom-call | flops 21474836480 | bytes 53477376 | tf_op jit(solution)/shard_map/expert_piece/pallas_call | solution.py:95
  152.0 0.0 all-to-all-done.1
  152.0 0.0 copy-start.3
  152.1 5.8 %all-to-all-start.3 = ((bf16[32,8,2048]{2,1,0:T(8,128)(2,1)}), bf16[32,8,2048]{2,1,0:T(8,128)(2,1)S(1)}, u32[]{:S(2)}, u32[]{:S(2)}) async-start(bf16[32,8,2048]{2,1,0:T(8,128)(2,1)} %bitcast.10), calls=%async_computation.3 | async-start | bytes 2097152 | tf_op jit(solution)/shard_map/all_to_all | solution.py:256
  157.9 0.0 copy-done.3
  157.9 1.7 fusion.2
  159.6 24.5 %all-to-all-done.3 = bf16[32,8,2048]{2,1,0:T(8,128)(2,1)S(1)} async-done(((bf16[32,8,2048]{2,1,0:T(8,128)(2,1)}), bf16[32,8,2048]{2,1,0:T(8,128)(2,1)S(1)}, u32[]{:S(2)}, u32[]{:S(2)}) %all-to-all-start.3) | async-done | bytes 1048608 | tf_op jit(solution)/shard_map/all_to_all | solution.py:256
  184.1 1.5 fusion
  (1 shorter events, 0.0 us)
Async XLA Ops:
  4.3 7.5 %copy-start = (bf16[256,2048]{1,0:T(8,128)(2,1)S(1)}, bf16[256,2048]{1,0:T(8,128)(2,1)}, u32[]{:S(2)}) copy-start(bf16[256,2048]{1,0:T(8,128)(2,1)} %rows_ref.3) | copy-start | bytes 3145732
  4.3 7.5 %copy-start.1 = (bf16[256,2048]{1,0:T(8,128)(2,1)S(1)}, bf16[256,2048]{1,0:T(8,128)(2,1)}, u32[]{:S(2)}) copy-start(bf16[256,2048]{1,0:T(8,128)(2,1)} %grads_ref.3) | copy-start | bytes 3145732
  4.3 7.5 %copy-start.2 = (s32[2,256]{1,0:T(2,128)S(1)}, s32[2,256]{1,0:T(2,128)}, u32[]{:S(2)}) copy-start(s32[2,256]{1,0:T(2,128)} %get-tuple-element.7.place_ref) | copy-start | bytes 6148
  4.4 56.3 %all-to-all-start = ((bf16[32,8,4096]{2,1,0:T(8,128)(2,1)}), bf16[32,8,4096]{2,1,0:T(8,128)(2,1)}, u32[]{:S(2)}, u32[]{:S(2)}) async-start(bf16[32,8,4096]{2,1,0:T(8,128)(2,1)} %bitcast.17), calls=%async_computation | async-start | bytes 4194304 | tf_op jit(solution)/shard_map/all_to_all | solution.py:248
  60.7 52.9 %all-to-all-start.2 = ((bf16[32,8,4096]{2,1,0:T(8,128)(2,1)}), bf16[32,8,4096]{2,1,0:T(8,128)(2,1)S(1)}, u32[]{:S(2)}, u32[]{:S(2)}) async-start(bf16[32,8,4096]{2,1,0:T(8,128)(2,1)} %bitcast.8), calls=%async_computation.2 | async-start | bytes 4194304 | tf_op jit(solution)/shard_map/all_to_all | solution.py:251
  113.6 38.5 %all-to-all-start.1 = ((bf16[32,8,2048]{2,1,0:T(8,128)(2,1)}), bf16[32,8,2048]{2,1,0:T(8,128)(2,1)S(1)}, u32[]{:S(2)}, u32[]{:S(2)}) async-start(bf16[32,8,2048]{2,1,0:T(8,128)(2,1)} %bitcast.5), calls=%async_computation.1 | async-start | bytes 2097152 | tf_op jit(solution)/shard_map/all_to_all | solution.py:256
  152.0 5.9 %copy-start.3 = (bf16[32,8,2048]{2,1,0:T(8,128)(2,1)}, bf16[32,8,2048]{2,1,0:T(8,128)(2,1)S(1)}, u32[]{:S(2)}) copy-start(bf16[32,8,2048]{2,1,0:T(8,128)(2,1)S(1)} %all-to-all-done.1) | copy-start | bytes 3145732
  152.1 32.1 %all-to-all-start.3 = ((bf16[32,8,2048]{2,1,0:T(8,128)(2,1)}), bf16[32,8,2048]{2,1,0:T(8,128)(2,1)S(1)}, u32[]{:S(2)}, u32[]{:S(2)}) async-start(bf16[32,8,2048]{2,1,0:T(8,128)(2,1)} %bitcast.10), calls=%async_computation.3 | async-start | bytes 2097152 | tf_op jit(solution)/shard_map/all_to_all | solution.py:256
